TPU v7x, 1024 devices: a whole 4x8x16 slice. The times are simulated.
1024 devices in a mesh: rep: 32 (over y_hi, z), exp: 32 (over x, y_lo, core).
Axes of the slice: x: 4, y: 8 (y_hi: 2, y_lo: 4; y = y_hi * 4 + y_lo), z: 16, core: 2. Of those that a mesh axis runs over, the one named last changes fastest.
Arguments:
- tokens: bfloat16 [131072, 2048], P(('rep', 'exp')), may hold values from -6 to 6
- expert_ids: int32 [131072, 8], P(('rep', 'exp')), may hold values from 0 to 127, all different within a row
- route_weights: float32 [131072, 8], P(('rep', 'exp')), may hold values from 0.05 to 1
- w_gate: bfloat16 [32, 2048, 384], P('exp'), may hold values from -0.125 to 0.125
- w_up: bfloat16 [32, 2048, 384], P('exp'), may hold values from -0.125 to 0.125
- w_down: bfloat16 [32, 384, 2048], P('exp'), may hold values from -0.21875 to 0.21875
- pseudo_values: bfloat16 [32, 2048, 2048], P('rep', 'exp'), may hold values from -4 to 4
- block_scales: float32 [32, 2048, 16], P('rep', 'exp'), may hold values from 0.1 to 1.5
- outer_params: float32 [3, 2048, 2048], P(None, 'exp'), may hold values from -6 to 6
- momentum: float32 [2048, 2048], P('exp'), may hold values from -4 to 4
- fragment: int32 [1], replicated, may hold values from 0 to 2
Outputs:
- moe_out: bfloat16 [131072, 2048], P(('rep', 'exp'))
- new_params: float32 [2048, 2048], P('exp')
- new_momentum: float32 [2048, 2048], P('exp')
Inputs may be any that keep to these rules, and one draw needn't show every extreme that they name: `expert_ids`: each row names 8 different experts.
All inputs are finite; a program needn't handle non-finite values.
Results may differ from a plain program's by a relative error of at most 0.0085.
Values may be sent and summed in bfloat16 or wider, within the bound.
No kernel may reach another device: no remote copies, remote signals or barrier semaphores. Data moves between devices by JAX's collectives and lax.ppermute only.
A program may use at most 64 MiB of HBM per device.

v0:
```python
import jax
import jax.numpy as jnp
from jax import lax
from jax.sharding import PartitionSpec as P

TOPK = 8
CAP = 16


momentum_rate = 0.9
outer_rate = 0.7


def route_slots(expert_ids, experts, capacity):
    rows_count = expert_ids.shape[0]
    columns = jnp.arange(experts, dtype=jnp.int32)
    onehot = (expert_ids[:, :, None] == columns[None, None, :]).astype(jnp.float32)
    per_token = jnp.sum(onehot, axis=1)
    row_pos = jnp.arange(rows_count, dtype=jnp.int32)
    lower = (row_pos[:, None] > row_pos[None, :]).astype(jnp.float32)
    prefix = jnp.dot(
        lower, per_token, precision=lax.Precision.HIGHEST, preferred_element_type=jnp.float32
    )
    rank_float = jnp.sum(onehot * prefix[:, None, :], axis=2)
    rank_in = (rank_float + 0.5).astype(jnp.int32).reshape(-1)
    flat_ids = expert_ids.reshape(-1)
    kept_mask = (flat_ids < experts) & (rank_in < capacity)
    slot_index = jnp.where(kept_mask, flat_ids * capacity + rank_in, experts * capacity)
    return slot_index


def build_buffer(tokens, slot_index, experts, capacity, topk):
    count = tokens.shape[0] * topk
    source = jnp.arange(count, dtype=jnp.int32) // topk + 1
    owner = jnp.zeros((experts * capacity + 1,), jnp.int32).at[slot_index].set(source)
    owner = owner[: experts * capacity]
    picked = jnp.take(tokens, jnp.maximum(owner - 1, 0), axis=0)
    filled = jnp.where((owner > 0)[:, None], picked, jnp.zeros_like(picked))
    return filled.reshape(experts, capacity, tokens.shape[1])


def combine(expert_flat, slot_index, route_weights):
    topk = route_weights.shape[1]
    padded = jnp.concatenate(
        [expert_flat, jnp.zeros((1, expert_flat.shape[1]), expert_flat.dtype)], axis=0
    )
    slots = slot_index.reshape(-1, topk)
    total = jnp.zeros((slots.shape[0], expert_flat.shape[1]), expert_flat.dtype)
    for choice_idx in range(topk):
        rows_got = jnp.take(padded, slots[:, choice_idx], axis=0)
        total = total + route_weights[:, choice_idx][:, None] * rows_got
    return total.astype(jnp.bfloat16)


def outer_step(pseudo_values, block_scales, outer_params, momentum, fragment):
    frag_rows = pseudo_values.shape[1]
    width = pseudo_values.shape[2]
    blocks = block_scales.shape[2]
    dequant = (
        pseudo_values[0].astype(jnp.float32).reshape(frag_rows, blocks, width // blocks)
        * block_scales[0][:, :, None]
    ).reshape(frag_rows, width)
    base = lax.dynamic_index_in_dim(outer_params, fragment[0], 0, keepdims=False)
    replicas = lax.axis_size("rep")
    total = lax.psum(dequant.astype(jnp.bfloat16), "rep").astype(jnp.float32)
    delta = total / replicas
    new_momentum = momentum_rate * momentum + delta
    new_params = base - outer_rate * (delta + momentum_rate * new_momentum)
    return (new_params, new_momentum)


def shards(
    tokens,
    expert_ids,
    route_weights,
    w_gate,
    w_up,
    w_down,
    pseudo_values,
    block_scales,
    outer_params,
    momentum,
    fragment,
):
    experts = lax.axis_size("exp") // 2
    width = tokens.shape[1]
    slot_index = route_slots(expert_ids, experts, CAP)
    sectioned = build_buffer(tokens, slot_index, experts, CAP, TOPK)
    outgoing = jnp.broadcast_to(sectioned[:, None], (experts, 2, CAP, width)).reshape(
        2 * experts, CAP, width
    )
    received = lax.all_to_all(outgoing, "exp", split_axis=0, concat_axis=0, tiled=True)
    sources, items, _ = received.shape
    inputs = received.reshape(sources * items, width)
    gate_out = jnp.dot(inputs, w_gate[0], preferred_element_type=jnp.float32)
    up_out = jnp.dot(inputs, w_up[0], preferred_element_type=jnp.float32)
    hidden = (jax.nn.silu(gate_out) * up_out).astype(jnp.bfloat16)
    partial_value = jnp.dot(hidden, w_down[0], preferred_element_type=jnp.float32).astype(
        jnp.bfloat16
    )
    returned_rows = lax.all_to_all(
        partial_value.reshape(sources, items, width), "exp", split_axis=0, concat_axis=0, tiled=True
    )
    pairs = returned_rows.reshape(experts, 2, CAP, width)
    expert_flat = (pairs[:, 0].astype(jnp.float32) + pairs[:, 1].astype(jnp.float32)).reshape(
        experts * CAP, width
    )
    moe_out = combine(expert_flat, slot_index, route_weights)
    new_params, new_momentum = outer_step(
        pseudo_values, block_scales, outer_params, momentum, fragment
    )
    return (moe_out, new_params, new_momentum)


def solution(mesh):
    return jax.shard_map(
        shards,
        mesh=mesh,
        in_specs=(
            P(("rep", "exp"), None),
            P(("rep", "exp"), None),
            P(("rep", "exp"), None),
            P("exp", None, None),
            P("exp", None, None),
            P("exp", None, None),
            P("rep", "exp", None),
            P("rep", "exp", None),
            P(None, "exp", None),
            P("exp", None),
            P(),
        ),
        out_specs=(P(("rep", "exp"), None), P("exp", None), P("exp", None)),
        check_vma=False,
    )
```

profile of v0, /device:TPU:6, one launch (start us, length us, event | category | flops | bytes accessed | tf_op | source)
XLA Modules:
  0.0 523.8 jit_solution(3302829073036032261)
XLA Ops:
  7.2 0.8 convert_reduce_fusion
  8.1 0.8 select_reduce_fusion
  8.9 0.7 add_select_fusion.1
  9.8 4.3 scatter_custom_fusion
  14.3 3.5 gather_fusion
  18.3 64.3 %all_to_all.10 = bf16[32,16,2048]{2,1,0:T(8,128)(2,1)S(1)} all-to-all(bf16[32,16,2048]{2,1,0:T(8,128)(2,1)S(1)} %bitcast.89), channel_id=1, replica_groups=mesh['rep'=32,'exp'=32] {'exp'}, dimensions={0} | all-to-all | bytes 4194304 | tf_op jit(solution)/shard_map/all_to_all | solution.py:92
  82.6 1.3 copy-done.1
  83.9 1.2 fusion.3
  85.2 5.7 %convolution_convert_fusion = bf16[512,2048]{1,0:T(8,128)(2,1)} fusion(bf16[1,384,2048]{2,1,0:T(8,128)(2,1)S(1)} %copy-done, bf16[512,2048]{1,0:T(8,128)(2,1)} %bitcast.93, bf16[1,2048,384]{2,1,0:T(8,128)(2,1)} %param.17, f32[512,384]{1,0:T(8,128)S(1)} %fusion.3), kind=kOutput, calls=%fused_computation.10 | convolution fusion | flops 1612840960 | bytes 8126464 | tf_op jit(solution)/shard_map/dot_general | solution.py:98
  90.9 7.1 %all-to-all-start.1 = ((bf16[32,16,2048]{2,1,0:T(8,128)(2,1)}), bf16[32,16,2048]{2,1,0:T(8,128)(2,1)}, u32[]{:S(2)}, u32[]{:S(2)}) async-start(bf16[32,16,2048]{2,1,0:T(8,128)(2,1)} %bitcast.91), calls=%async_computation.1 | async-start | bytes 4194304 | tf_op jit(solution)/shard_map/all_to_all | solution.py:101
  98.5 0.9 fusion.26
  100.2 375.6 %all-reduce.3.cloned.1.call-done = bf16[64,2048]{1,0:T(8,128)(2,1)} async-done(((bf16[64,2048]{1,0:T(8,128)(2,1)}), bf16[64,2048]{1,0:T(8,128)(2,1)}) %all-reduce.3.cloned.1.call-update) | async-done | bytes 262160 | tf_op jit(solution)/shard_map/psum | solution.py:65
  475.8 2.2 bitcast_subtract_fusion
  478.0 1.9 convert_add_fusion
  479.9 1.5 concatenate.3
  481.5 3.1 gather_fusion.2
  484.5 4.0 gather_fusion.3
  488.6 4.0 gather_fusion.4
  492.6 4.0 gather_fusion.5
  496.6 4.0 gather_fusion.6
  500.6 4.0 gather_fusion.7
  504.6 4.1 gather_fusion.1
  508.7 4.0 gather_fusion.8
  512.7 4.3 fusion.12
  (36 shorter events, 1.6 us)
Async XLA Ops:
  7.2 78.0 %copy-start = (bf16[1,384,2048]{2,1,0:T(8,128)(2,1)S(1)}, bf16[1,384,2048]{2,1,0:T(8,128)(2,1)}, u32[]{:S(2)}) copy-start(bf16[1,384,2048]{2,1,0:T(8,128)(2,1)} %param.18) | copy-start | bytes 4718596
  18.3 65.6 %copy-start.6 = (bf16[1,2048,384]{2,1,0:T(8,128)(2,1)S(1)}, bf16[1,2048,384]{2,1,0:T(8,128)(2,1)}, u32[]{:S(2)}) copy-start(bf16[1,2048,384]{2,1,0:T(8,128)(2,1)} %param.16) | copy-start | bytes 4718596
  82.6 1.3 copy-start.1
  90.9 7.3 %copy-start.4 = (f32[1,64,16]{1,2,0:T(8,128)S(1)}, f32[1,64,16]{1,2,0:T(8,128)}, u32[]{:S(2)}) copy-start(f32[1,64,16]{1,2,0:T(8,128)} %param.20) | copy-start | bytes 12292
  90.9 7.6 %copy-start.3 = (bf16[1,64,2048]{2,1,0:T(8,128)(2,1)S(1)}, bf16[1,64,2048]{2,1,0:T(8,128)(2,1)}, u32[]{:S(2)}) copy-start(bf16[1,64,2048]{2,1,0:T(8,128)(2,1)} %param.19) | copy-start | bytes 786436
  90.9 9.3 %copy-start.5 = (f32[128,8]{0,1:T(8,128)S(1)}, f32[128,8]{0,1:T(8,128)}, u32[]{:S(2)}) copy-start(f32[128,8]{0,1:T(8,128)} %param.15) | copy-start | bytes 12292
  90.9 384.9 %copy-start.2 = (f32[64,2048]{1,0:T(8,128)S(1)}, f32[64,2048]{1,0:T(8,128)}, u32[]{:S(2)}) copy-start(f32[64,2048]{1,0:T(8,128)} %param.22) | copy-start | bytes 1572868
  90.9 387.1 %all-to-all-start.1 = ((bf16[32,16,2048]{2,1,0:T(8,128)(2,1)}), bf16[32,16,2048]{2,1,0:T(8,128)(2,1)}, u32[]{:S(2)}, u32[]{:S(2)}) async-start(bf16[32,16,2048]{2,1,0:T(8,128)(2,1)} %bitcast.91), calls=%async_computation.1 | async-start | bytes 4194304 | tf_op jit(solution)/shard_map/all_to_all | solution.py:101
  98.0 377.8 %all-reduce.3.cloned.1.call-start = ((), (), s32[]{:S(2)}) async-start(), calls=%async_computation.2 | async-start | bytes 524288 | tf_op jit(solution)/shard_map/psum | solution.py:65
Sparse Core Ops, SparseCore 0:
  102.9 372.8 all-reduce.2
where the time goes:
time: 525 us; the launch traced here: 524 us
  waiting for transfers between devices  376 us (72%)
  blocking collectives  64.3 us (12%)
  local copies, waits for them, and re-layouts  42.7 us (8%)
  between operations  14.9 us (3%)
  other arithmetic  11.9 us (2%)
  starting transfers between devices  7.3 us (1%)
  matrix products  7.09 us (1%)
    psum x1, waiting for transfers between devices, outer_step(): total = lax.psum(dequant.astype(jnp.bfloat16), 'rep').astype(jnp.float32)  376 us
    all_to_all x1, blocking collectives, shards(): lax.all_to_all(outgoing, 'exp', split_axis=0, concat_axis=0, tiled=True)  64.3 us
    gather x8, local copies, waits for them, and re-layouts, combine(): rows_got = jnp.take(padded, slots[:, choice_idx], axis=0)  31.2 us
  transfers between devices with their start and end apart: 2, of which 1 were waited for; matrix products, arithmetic and copies ran while one was open for 1% of the time, Pallas kernels for 0%

commit v1 on v0

v1 whole, which is shorter than its diff:
```python
import functools

import jax
import jax.numpy as jnp
from jax import lax
from jax.experimental import pallas as pl
from jax.experimental.pallas import tpu as pltpu
from jax.sharding import Mesh
from jax.sharding import PartitionSpec as P

CAP = 16

momentum_rate = 0.9
outer_rate = 0.7


def route_kernel(experts, ids_ref, weights_ref, tokens_ref, buffer_ref, combine_ref):
    topk, rows = ids_ref.shape
    ids = ids_ref[...]
    weights = weights_ref[...]
    expert = lax.broadcasted_iota(jnp.int32, (experts, rows), 0)
    named = jnp.zeros((experts, rows), jnp.float32)
    weight = jnp.zeros((experts, rows), jnp.float32)
    for k in range(topk):
        hit = ids[k : k + 1, :] == expert
        named = named + hit.astype(jnp.float32)
        weight = weight + jnp.where(hit, weights[k : k + 1, :], 0.0)
    earlier = lax.broadcasted_iota(jnp.int32, (rows, rows), 0) < lax.broadcasted_iota(
        jnp.int32, (rows, rows), 1
    )
    rank = jnp.dot(
        named.astype(jnp.bfloat16),
        earlier.astype(jnp.bfloat16),
        preferred_element_type=jnp.float32,
    ).astype(jnp.int32)
    rank = jnp.where(named > 0.5, rank, CAP)
    place = lax.broadcasted_iota(jnp.int32, (experts, CAP, rows), 1)
    chosen = rank[:, None, :] == place
    pick = jnp.where(chosen, 1.0, 0.0).reshape(experts * CAP, rows)
    combine_ref[...] = jnp.where(
        chosen, jnp.broadcast_to(weight[:, None, :], chosen.shape), 0.0
    ).reshape(experts * CAP, rows)
    buffer_ref[...] = jnp.dot(
        pick.astype(jnp.bfloat16), tokens_ref[...], preferred_element_type=jnp.float32
    ).astype(jnp.bfloat16)


def route(tokens, expert_ids, route_weights, experts):
    rows, width = tokens.shape
    return pl.pallas_call(
        functools.partial(route_kernel, experts),
        out_shape=(
            jax.ShapeDtypeStruct((experts * CAP, width), jnp.bfloat16),
            jax.ShapeDtypeStruct((experts * CAP, rows), jnp.float32),
        ),
        compiler_params=pltpu.CompilerParams(vmem_limit_bytes=32 * 1024 * 1024),
        name="route",
    )(expert_ids.T, route_weights.T, tokens)


def expert_half(rows, w_gate, w_up, w_down):
    gate_out = jnp.dot(rows, w_gate, preferred_element_type=jnp.float32)
    up_out = jnp.dot(rows, w_up, preferred_element_type=jnp.float32)
    hidden = (jax.nn.silu(gate_out) * up_out).astype(jnp.bfloat16)
    return jnp.dot(hidden, w_down, preferred_element_type=jnp.float32).astype(jnp.bfloat16)


def swap_cores(rows):
    return lax.ppermute(rows, "core", [(0, 1), (1, 0)])


def outer_step(pseudo_values, block_scales, outer_params, momentum, fragment):
    replicas = lax.axis_size("rep")
    _, frag_rows, width = pseudo_values.shape
    blocks = block_scales.shape[2]
    dequant = (
        pseudo_values[0].astype(jnp.float32).reshape(frag_rows, blocks, width // blocks)
        * block_scales[0][:, :, None]
    ).astype(jnp.bfloat16)
    pieces = dequant.reshape(replicas, frag_rows // replicas, width)
    theirs = lax.all_to_all(pieces, "rep", split_axis=0, concat_axis=0, tiled=True)
    piece = jnp.sum(theirs.astype(jnp.float32), axis=0) / replicas
    spread = jnp.broadcast_to(piece.astype(jnp.bfloat16)[None], pieces.shape)
    delta = (
        lax.all_to_all(spread, "rep", split_axis=0, concat_axis=0, tiled=True)
        .reshape(frag_rows, width)
        .astype(jnp.float32)
    )
    base = lax.dynamic_index_in_dim(outer_params, fragment[0], 0, keepdims=False)
    new_momentum = momentum_rate * momentum + delta
    new_params = base - outer_rate * (delta + momentum_rate * new_momentum)
    return (new_params, new_momentum)


def shards(
    tokens,
    expert_ids,
    route_weights,
    w_gate,
    w_up,
    w_down,
    pseudo_values,
    block_scales,
    outer_params,
    momentum,
    fragment,
):
    experts = lax.axis_size("chip")
    width = tokens.shape[1]
    buffer, combine = route(tokens, expert_ids, route_weights, experts)
    mine = lax.all_to_all(
        buffer.reshape(experts, CAP, width), "chip", split_axis=0, concat_axis=0, tiled=True
    ).reshape(experts * CAP, width)
    theirs = swap_cores(mine)
    partial_mine = expert_half(mine, w_gate[0], w_up[0], w_down[0])
    partial_theirs = expert_half(theirs, w_gate[0], w_up[0], w_down[0])
    other_half = swap_cores(partial_theirs)
    total = partial_mine.astype(jnp.float32) + other_half.astype(jnp.float32)
    returned = lax.all_to_all(
        total.astype(jnp.bfloat16).reshape(experts, CAP, width),
        "chip",
        split_axis=0,
        concat_axis=0,
        tiled=True,
    ).reshape(experts * CAP, width)
    high = combine.astype(jnp.bfloat16)
    moe_out = lax.dot_general(
        high, returned, (((0,), (0,)), ((), ())), preferred_element_type=jnp.float32
    ).astype(jnp.bfloat16)
    new_params, new_momentum = outer_step(
        pseudo_values, block_scales, outer_params, momentum, fragment
    )
    return (moe_out, new_params, new_momentum)


def solution(mesh):
    reps, exps = mesh.devices.shape
    fine = Mesh(mesh.devices.reshape(reps, exps // 2, 2), ("rep", "chip", "core"))
    exp = ("chip", "core")
    return jax.shard_map(
        shards,
        mesh=fine,
        in_specs=(
            P(("rep",) + exp, None),
            P(("rep",) + exp, None),
            P(("rep",) + exp, None),
            P(exp, None, None),
            P(exp, None, None),
            P(exp, None, None),
            P("rep", exp, None),
            P("rep", exp, None),
            P(None, exp, None),
            P(exp, None),
            P(),
        ),
        out_specs=(P(("rep",) + exp, None), P(exp, None), P(exp, None)),
        check_vma=False,
    )
```

time: 525 us -> 155 us (0.30)
  waiting for transfers between devices: 376 us -> 56 us
  local copies, waits for them, and re-layouts: 42.7 us -> 6.97 us
  blocking collectives: 64.3 us -> 33.2 us
  starting transfers between devices: 7.3 us -> 35.5 us
  between operations: 14.9 us -> 1.42 us
  other arithmetic: 11.9 us -> 4.59 us
  matrix products: 7.09 us -> 13.8 us
    psum x1 -> x0, waiting for transfers between devices: 376 us -> none  [outer_step(): total = lax.psum(dequant.astype(jnp.bfloat16), 'rep').astype(jnp.float32)]
    all_to_all x1 -> x3, waiting for transfers between devices: 0.01 us -> 56 us  [the longest x1 19.3 us: outer_step(): lax.all_to_all(spread, 'rep', split_axis=0, concat_axis=0, tiled=True)]
    gather x9 -> x0, local copies, waits for them, and re-layouts: 34.6 us -> none  [the longest x8 31.2 us: combine(): rows_got = jnp.take(padded, slots[:, choice_idx], axis=0)]
    all_to_all x1, blocking collectives: 64.3 us -> 33.2 us  [shards(): lax.all_to_all(buffer.reshape(experts, CAP, width), 'chip', split_axis=0,...]
    all_to_all x1 -> x3, starting transfers between devices: 7.08 us -> 31.5 us  [the longest x1 21.7 us: outer_step(): lax.all_to_all(pieces, 'rep', split_axis=0, concat_axis=0, tiled=True)]
    dot_general x3 -> x5, matrix products: 7.09 us -> 13.8 us  [the longest x2 8.11 us: expert_half(): jnp.dot(hidden, w_down, preferred_element_type=jnp.float32)]
  transfers between devices with their start and end apart: 2 -> 5, of which waited for: 1 -> 3; matrix products, arithmetic and copies ran while one was open for 1% -> 14% of each run, Pallas kernels for 0% -> 0%
where the time goes in v1:
time: 155 us; the launch traced here: 152 us
  waiting for transfers between devices  56 us (36%)
  starting transfers between devices  35.5 us (23%)
  blocking collectives  33.2 us (21%)
  matrix products  13.8 us (9%)
  local copies, waits for them, and re-layouts  6.97 us (4%)
  other arithmetic  4.59 us (3%)
    all_to_all x1, blocking collectives, shards(): lax.all_to_all(buffer.reshape(experts, CAP, width), 'chip', split_axis=0,...  33.2 us
    all_to_all x1, starting transfers between devices, outer_step(): lax.all_to_all(pieces, 'rep', split_axis=0, concat_axis=0, tiled=True)  21.7 us
    all_to_all x1, waiting for transfers between devices, outer_step(): lax.all_to_all(spread, 'rep', split_axis=0, concat_axis=0, tiled=True)  19.3 us
    all_to_all x1, waiting for transfers between devices, shards(): lax.all_to_all(total.astype(jnp.bfloat16).reshape(experts, CAP, width), '...  18.6 us
    all_to_all x1, waiting for transfers between devices, outer_step(): lax.all_to_all(pieces, 'rep', split_axis=0, concat_axis=0, tiled=True)  18.1 us
    dot_general x2, matrix products, expert_half(): jnp.dot(hidden, w_down, preferred_element_type=jnp.float32)  8.11 us
    all_to_all x1, starting transfers between devices, shards(): lax.all_to_all(total.astype(jnp.bfloat16).reshape(experts, CAP, width), '...  5.9 us
    ppermute x2, starting transfers between devices, swap_cores(): return lax.ppermute(rows, 'core', [(0, 1), (1, 0)])  4.02 us
  transfers between devices with their start and end apart: 5, of which 3 were waited for; matrix products, arithmetic and copies ran while one was open for 14% of the time, Pallas kernels for 0%

profile of v1, /device:TPU:6, one launch (start us, length us, event | category | flops | bytes accessed | tf_op | source)
XLA Modules:
  0.0 152.1 jit_solution(3857072152277380217)
XLA Ops:
  0.7 1.2 copy-done.1
  1.8 0.7 copy-done.2
  2.5 0.7 copy-done.3
  3.2 0.5 route.1
  3.7 33.2 %all_to_all.20 = bf16[16,16,2048]{2,1,0:T(8,128)(2,1)S(1)} all-to-all(bf16[16,16,2048]{2,1,0:T(8,128)(2,1)S(1)} %bitcast.45), channel_id=1, replica_groups=mesh['rep'=32,'chip'=16,'core'=2] {'chip'}, dimensions={0} | all-to-all | bytes 2097152 | tf_op jit(solution)/shard_map/all_to_all | solution.py:111
  37.0 1.9 %collective-permute-start = (bf16[256,2048]{1,0:T(8,128)(2,1)S(1)}, bf16[256,2048]{1,0:T(8,128)(2,1)}, u32[]{:S(2)}, u32[]{:S(2)}) collective-permute-start(bf16[256,2048]{1,0:T(8,128)(2,1)S(1)} %bitcast.48), channel_id=1, source_target_pairs={{0,1},{1,0},{2,3},{3,2},{4,5},{5,4},{6,7},{7,6},{8,9},{9,8},{10,11... | collective-permute-start | bytes 3145736 | tf_op jit(solution)/shard_map/ppermute | solution.py:69
  39.0 1.0 mul.43
  40.0 1.3 mul.44
  41.3 1.1 reshape.37
  42.4 2.0 %multiply_convert_fusion = bf16[32,2,2048]{2,1,0:T(2,128)(2,1)} fusion(f32[32,2,2048]{2,1,0:T(2,128)} %reshape.37, f32[32,2,2048]{2,1,0:T(2,128)S(1)} %mul.44), kind=kLoop, calls=%fused_computation.20 | loop fusion | flops 262144 | bytes 1310720 | tf_op jit(solution)/shard_map/convert_element_type | solution.py:79
  44.5 21.7 %all-to-all-start.2 = ((bf16[32,2,2048]{2,1,0:T(2,128)(2,1)}), bf16[32,2,2048]{2,1,0:T(2,128)(2,1)S(1)}, u32[]{:S(2)}, u32[]{:S(2)}) async-start(bf16[32,2,2048]{2,1,0:T(2,128)(2,1)} %multiply_convert_fusion), calls=%async_computation.2 | async-start | bytes 524288 | tf_op jit(solution)/shard_map/all_to_all | solution.py:81
  66.2 2.4 %fusion.5 = f32[256,384]{1,0:T(8,128)S(1)} fusion(bf16[256,2048]{1,0:T(8,128)(2,1)} %collective-permute-done, bf16[1,2048,384]{2,1,0:T(8,128)(2,1)} %param.15), kind=kOutput, calls=%fused_computation.7 | convolution fusion | flops 402653184 | bytes 3014656 | tf_op jit(solution)/shard_map/dot_general | solution.py:63
  68.7 4.1 %convolution_convert_fusion = bf16[256,2048]{1,0:T(8,128)(2,1)} fusion(bf16[1,384,2048]{2,1,0:T(8,128)(2,1)S(1)} %copy-done, f32[256,384]{1,0:T(8,128)S(1)} %fusion.5, bf16[256,2048]{1,0:T(8,128)(2,1)} %collective-permute-done, bf16[1,2048,384]{2,1,0:T(8,128)(2,1)} %param.14), kind=kOutput, calls=%fused_computation | convolution fusion | flops 806420480 | bytes 5636096 | tf_op jit(solution)/shard_map/dot_general | solution.py:65
  72.7 2.1 %collective-permute-start.1 = (bf16[256,2048]{1,0:T(8,128)(2,1)}, bf16[256,2048]{1,0:T(8,128)(2,1)}, u32[]{:S(2)}, u32[]{:S(2)}) collective-permute-start(bf16[256,2048]{1,0:T(8,128)(2,1)} %convolution_convert_fusion), channel_id=1, source_target_pairs={{0,1},{1,0},{2,3},{3,2},{4,5},{5,4},{6,7},{7,6},{8,9},{9,8},{10,11... | collective-permute-start | bytes 3145736 | tf_op jit(solution)/shard_map/ppermute | solution.py:69
  74.9 18.1 %all-to-all-done.2 = bf16[32,2,2048]{2,1,0:T(2,128)(2,1)S(1)} async-done(((bf16[32,2,2048]{2,1,0:T(2,128)(2,1)}), bf16[32,2,2048]{2,1,0:T(2,128)(2,1)S(1)}, u32[]{:S(2)}, u32[]{:S(2)}) %all-to-all-start.2) | async-done | bytes 262176 | tf_op jit(solution)/shard_map/all_to_all | solution.py:81
  93.2 0.8 broadcast_in_dim.2
  94.1 3.9 %all-to-all-start.3 = ((bf16[32,2,2048]{2,1,0:T(2,128)(2,1)}), bf16[32,2,2048]{2,1,0:T(2,128)(2,1)S(1)}, u32[]{:S(2)}, u32[]{:S(2)}) async-start(bf16[32,2,2048]{2,1,0:T(2,128)(2,1)} %broadcast_in_dim.2), calls=%async_computation.3 | async-start | bytes 524288 | tf_op jit(solution)/shard_map/all_to_all | solution.py:85
  97.9 2.1 %fusion.11 = f32[256,384]{1,0:T(8,128)S(1)} fusion(bf16[256,2048]{1,0:T(8,128)(2,1)S(1)} %bitcast.49, bf16[1,2048,384]{2,1,0:T(8,128)(2,1)} %param.14), kind=kOutput, calls=%fused_computation.13 | convolution fusion | flops 402653184 | bytes 3014656 | tf_op jit(solution)/shard_map/dot_general | solution.py:62
  100.1 4.0 %add_convert_fusion = bf16[256,2048]{1,0:T(8,128)(2,1)} fusion(bf16[256,2048]{1,0:T(8,128)(2,1)} %collective-permute-done.1, bf16[1,384,2048]{2,1,0:T(8,128)(2,1)S(1)} %copy-done, bf16[256,2048]{1,0:T(8,128)(2,1)S(1)} %bitcast.50, bf16[1,2048,384]{2,1,0:T(8,128)(2,1)} %param.15, f32[256,384]{1,0:T(8,128)S(1)} %fusion.11), kind=kOutput, calls=%fused_computation.4 | convolution fusion | flops 808517632 | bytes 6684672 | tf_op jit(solution)/shard_map/dot_general | solution.py:65
  104.1 19.3 %all-to-all-done.3 = bf16[32,2,2048]{2,1,0:T(2,128)(2,1)S(1)} async-done(((bf16[32,2,2048]{2,1,0:T(2,128)(2,1)}), bf16[32,2,2048]{2,1,0:T(2,128)(2,1)S(1)}, u32[]{:S(2)}, u32[]{:S(2)}) %all-to-all-start.3) | async-done | bytes 262176 | tf_op jit(solution)/shard_map/all_to_all | solution.py:85
  123.4 5.9 %all-to-all-start.1 = ((bf16[16,16,2048]{2,1,0:T(8,128)(2,1)}), bf16[16,16,2048]{2,1,0:T(8,128)(2,1)S(1)}, u32[]{:S(2)}, u32[]{:S(2)}) async-start(bf16[16,16,2048]{2,1,0:T(8,128)(2,1)} %bitcast.52), calls=%async_computation.1 | async-start | bytes 2097152 | tf_op jit(solution)/shard_map/all_to_all | solution.py:119
  130.0 2.3 %bitcast_subtract_fusion = (f32[64,2048]{1,0:T(8,128)}, f32[64,2048]{1,0:T(8,128)}) fusion(f32[64,2048]{1,0:T(8,128)S(1)} %reshape.38, f32[3,64,2048]{2,1,0:T(8,128)} %param.19, s32[]{:T(128)S(6)} %select_n.4, f32[64,2048]{1,0:T(8,128)} %param.20), kind=kLoop, calls=%fused_computation.17 | loop fusion | flops 786432 | bytes 2621444 | tf_op jit(solution)/shard_map/sub | solution.py:91
  132.3 18.6 %all-to-all-done.1 = bf16[16,16,2048]{2,1,0:T(8,128)(2,1)S(1)} async-done(((bf16[16,16,2048]{2,1,0:T(8,128)(2,1)}), bf16[16,16,2048]{2,1,0:T(8,128)(2,1)S(1)}, u32[]{:S(2)}, u32[]{:S(2)}) %all-to-all-start.1) | async-done | bytes 1048608 | tf_op jit(solution)/shard_map/all_to_all | solution.py:119
  150.9 1.1 convolution_convert_fusion.2
  (15 shorter events, 0.4 us)
Async XLA Ops:
  0.6 68.0 %copy-start = (bf16[1,384,2048]{2,1,0:T(8,128)(2,1)S(1)}, bf16[1,384,2048]{2,1,0:T(8,128)(2,1)}, u32[]{:S(2)}) copy-start(bf16[1,384,2048]{2,1,0:T(8,128)(2,1)} %param.16) | copy-start | bytes 4718596
  0.6 1.2 copy-start.1
  1.8 0.7 copy-start.2
  2.5 0.7 copy-start.3
  3.2 35.7 %copy-start.5 = (f32[1,64,16]{1,2,0:T(8,128)S(1)}, f32[1,64,16]{1,2,0:T(8,128)}, u32[]{:S(2)}) copy-start(f32[1,64,16]{1,2,0:T(8,128)} %param.18) | copy-start | bytes 12292
  3.7 37.5 %copy-start.4 = (bf16[1,64,2048]{2,1,0:T(8,128)(2,1)S(1)}, bf16[1,64,2048]{2,1,0:T(8,128)(2,1)}, u32[]{:S(2)}) copy-start(bf16[1,64,2048]{2,1,0:T(8,128)(2,1)} %param.17) | copy-start | bytes 786436
  37.0 29.2 %collective-permute-start = (bf16[256,2048]{1,0:T(8,128)(2,1)S(1)}, bf16[256,2048]{1,0:T(8,128)(2,1)}, u32[]{:S(2)}, u32[]{:S(2)}) collective-permute-start(bf16[256,2048]{1,0:T(8,128)(2,1)S(1)} %bitcast.48), channel_id=1, source_target_pairs={{0,1},{1,0},{2,3},{3,2},{4,5},{5,4},{6,7},{7,6},{8,9},{9,8},{10,11... | collective-permute-start | bytes 3145736 | tf_op jit(solution)/shard_map/ppermute | solution.py:69
  44.5 48.5 %all-to-all-start.2 = ((bf16[32,2,2048]{2,1,0:T(2,128)(2,1)}), bf16[32,2,2048]{2,1,0:T(2,128)(2,1)S(1)}, u32[]{:S(2)}, u32[]{:S(2)}) async-start(bf16[32,2,2048]{2,1,0:T(2,128)(2,1)} %multiply_convert_fusion), calls=%async_computation.2 | async-start | bytes 524288 | tf_op jit(solution)/shard_map/all_to_all | solution.py:81
  72.7 27.3 %collective-permute-start.1 = (bf16[256,2048]{1,0:T(8,128)(2,1)}, bf16[256,2048]{1,0:T(8,128)(2,1)}, u32[]{:S(2)}, u32[]{:S(2)}) collective-permute-start(bf16[256,2048]{1,0:T(8,128)(2,1)} %convolution_convert_fusion), channel_id=1, source_target_pairs={{0,1},{1,0},{2,3},{3,2},{4,5},{5,4},{6,7},{7,6},{8,9},{9,8},{10,11... | collective-permute-start | bytes 3145736 | tf_op jit(solution)/shard_map/ppermute | solution.py:69
  94.1 29.3 %all-to-all-start.3 = ((bf16[32,2,2048]{2,1,0:T(2,128)(2,1)}), bf16[32,2,2048]{2,1,0:T(2,128)(2,1)S(1)}, u32[]{:S(2)}, u32[]{:S(2)}) async-start(bf16[32,2,2048]{2,1,0:T(2,128)(2,1)} %broadcast_in_dim.2), calls=%async_computation.3 | async-start | bytes 524288 | tf_op jit(solution)/shard_map/all_to_all | solution.py:85
  123.4 27.6 %all-to-all-start.1 = ((bf16[16,16,2048]{2,1,0:T(8,128)(2,1)}), bf16[16,16,2048]{2,1,0:T(8,128)(2,1)S(1)}, u32[]{:S(2)}, u32[]{:S(2)}) async-start(bf16[16,16,2048]{2,1,0:T(8,128)(2,1)} %bitcast.52), calls=%async_computation.1 | async-start | bytes 2097152 | tf_op jit(solution)/shard_map/all_to_all | solution.py:119

commit v2 on v1

v2 whole, which is shorter than its diff:
```python
import functools

import jax
import jax.numpy as jnp
from jax import lax
from jax.experimental import pallas as pl
from jax.experimental.pallas import tpu as pltpu
from jax.sharding import Mesh
from jax.sharding import PartitionSpec as P

CAP = 16
RADIX = 4

momentum_rate = 0.9
outer_rate = 0.7

PARAMS = pltpu.CompilerParams(vmem_limit_bytes=20 * 1024 * 1024)
VMEM = pl.BlockSpec(memory_space=pltpu.VMEM)
SMEM = pl.BlockSpec(memory_space=pltpu.SMEM)


def route_kernel(experts, ids_ref, weights_ref, tokens_ref, buffer_ref, combine_ref):
    topk, rows = ids_ref.shape
    ids = ids_ref[...]
    weights = weights_ref[...]
    expert = lax.broadcasted_iota(jnp.int32, (experts, rows), 0)
    named = jnp.zeros((experts, rows), jnp.float32)
    weight = jnp.zeros((experts, rows), jnp.float32)
    for k in range(topk):
        hit = ids[k : k + 1, :] == expert
        named = named + hit.astype(jnp.float32)
        weight = weight + jnp.where(hit, weights[k : k + 1, :], 0.0)
    earlier = lax.broadcasted_iota(jnp.int32, (rows, rows), 0) < lax.broadcasted_iota(
        jnp.int32, (rows, rows), 1
    )
    rank = jnp.dot(
        named.astype(jnp.bfloat16),
        earlier.astype(jnp.bfloat16),
        preferred_element_type=jnp.float32,
    ).astype(jnp.int32)
    rank = jnp.where(named > 0.5, rank, CAP)
    place = lax.broadcasted_iota(jnp.int32, (experts, CAP, rows), 1)
    chosen = rank[:, None, :] == place
    pick = jnp.where(chosen, 1.0, 0.0).reshape(experts * CAP, rows)
    combine_ref[...] = (
        jnp.where(chosen, jnp.broadcast_to(weight[:, None, :], chosen.shape), 0.0)
        .reshape(experts * CAP, rows)
        .astype(jnp.bfloat16)
    )
    buffer_ref[...] = jnp.dot(
        pick.astype(jnp.bfloat16), tokens_ref[...], preferred_element_type=jnp.float32
    ).astype(jnp.bfloat16)


def route(tokens, expert_ids, route_weights, experts):
    rows, width = tokens.shape
    return pl.pallas_call(
        functools.partial(route_kernel, experts),
        out_shape=(
            jax.ShapeDtypeStruct((experts * CAP, width), jnp.bfloat16),
            jax.ShapeDtypeStruct((experts * CAP, rows), jnp.bfloat16),
        ),
        compiler_params=PARAMS,
        name="route",
    )(expert_ids.T, route_weights.T, tokens)


def expert_kernel(rows_ref, g0_ref, u0_ref, d0_ref, g1_ref, u1_ref, d1_ref, out_ref):
    rows = rows_ref[...]
    total = None
    for gate_ref, up_ref, down_ref in ((g0_ref, u0_ref, d0_ref), (g1_ref, u1_ref, d1_ref)):
        gate = jnp.dot(rows, gate_ref[0], preferred_element_type=jnp.float32)
        up = jnp.dot(rows, up_ref[0], preferred_element_type=jnp.float32)
        hidden = (gate / (1.0 + jnp.exp(-gate)) * up).astype(jnp.bfloat16)
        part = jnp.dot(hidden, down_ref[0], preferred_element_type=jnp.float32)
        total = part if total is None else total + part
    out_ref[...] = total.astype(jnp.bfloat16)


def expert_rows(rows, own, other):
    return pl.pallas_call(
        expert_kernel,
        out_shape=jax.ShapeDtypeStruct(rows.shape, jnp.bfloat16),
        compiler_params=PARAMS,
        name="expert_rows",
    )(rows, *own, *other)


def combine_kernel(combine_ref, rows_ref, out_ref):
    out_ref[...] = lax.dot_general(
        combine_ref[...],
        rows_ref[...],
        (((0,), (0,)), ((), ())),
        preferred_element_type=jnp.float32,
    ).astype(jnp.bfloat16)


def combine_rows(combine, rows):
    return pl.pallas_call(
        combine_kernel,
        out_shape=jax.ShapeDtypeStruct((combine.shape[1], rows.shape[1]), jnp.bfloat16),
        compiler_params=PARAMS,
        name="combine_rows",
    )(combine, rows)


def dequant_kernel(place_ref, values_ref, scales_ref, *out_refs):
    rows, width = out_refs[0].shape
    blocks = scales_ref.shape[0]
    column = lax.broadcasted_iota(jnp.int32, (blocks, width), 1) // (width // blocks)
    spread = (column == lax.broadcasted_iota(jnp.int32, (blocks, width), 0)).astype(jnp.bfloat16)
    scales = scales_ref[...]
    high = scales.astype(jnp.bfloat16)
    rest = scales - high.astype(jnp.float32)
    middle = rest.astype(jnp.bfloat16)
    low = (rest - middle.astype(jnp.float32)).astype(jnp.bfloat16)
    wide = sum(
        lax.dot_general(
            part, spread, (((0,), (0,)), ((), ())), preferred_element_type=jnp.float32
        )
        for part in (high, middle, low)
    )
    whole = (values_ref[0].astype(jnp.float32) * wide).astype(jnp.bfloat16)
    for place in range(RADIX):
        block = whole[place * rows : (place + 1) * rows]
        for step, out_ref in enumerate(out_refs):

            @pl.when((place_ref[0] + step) % RADIX == place)
            def _():
                out_ref[...] = block


def dequant(place, values, scales):
    _, rows, width = values.shape
    part = jax.ShapeDtypeStruct((rows // RADIX, width), jnp.bfloat16)
    return pl.pallas_call(
        dequant_kernel,
        in_specs=[SMEM, VMEM, VMEM],
        out_shape=(part,) * RADIX,
        compiler_params=PARAMS,
        name="dequant",
    )(place, values, scales[0].T)


def add_split_kernel(place_ref, *refs):
    in_refs, out_refs = refs[:RADIX], refs[RADIX:]
    total = sum(ref[...].astype(jnp.float32) for ref in in_refs).astype(jnp.bfloat16)
    width = out_refs[0].shape[1]
    for place in range(RADIX):
        for step, out_ref in enumerate(out_refs):

            @pl.when((place_ref[0] + step) % RADIX == place)
            def _():
                out_ref[...] = total[:, place * width : (place + 1) * width]


def add_split(place, parts):
    rows, width = parts[0].shape
    part = jax.ShapeDtypeStruct((rows, width // RADIX), jnp.bfloat16)
    return pl.pallas_call(
        add_split_kernel,
        in_specs=[SMEM] + [VMEM] * RADIX,
        out_shape=(part,) * RADIX,
        compiler_params=PARAMS,
        name="add_split",
    )(place, *parts)


def add_kernel(*refs):
    refs[-1][...] = sum(ref[...].astype(jnp.float32) for ref in refs[:-1]).astype(jnp.bfloat16)


def add_parts(parts):
    return pl.pallas_call(
        add_kernel,
        out_shape=jax.ShapeDtypeStruct(parts[0].shape, jnp.bfloat16),
        compiler_params=PARAMS,
        name="add_parts",
    )(*parts)


def join_kernel(place_ref, *refs):
    in_refs, out_ref = refs[:RADIX], refs[RADIX]
    width = in_refs[0].shape[1]
    for place in range(RADIX):
        for step, ref in enumerate(in_refs):

            @pl.when((place_ref[0] + RADIX - step) % RADIX == place)
            def _():
                out_ref[:, place * width : (place + 1) * width] = ref[...]


def join(place, parts):
    rows, width = parts[0].shape
    return pl.pallas_call(
        join_kernel,
        in_specs=[SMEM] + [VMEM] * RADIX,
        out_shape=jax.ShapeDtypeStruct((rows, width * RADIX), jnp.bfloat16),
        compiler_params=PARAMS,
        name="join",
    )(place, *parts)


def update_kernel(replicas, fragment_ref, place_ref, *refs):
    part_refs = refs[:RADIX]
    base_ref, momentum_ref, params_out, momentum_out = refs[RADIX:]
    rows = part_refs[0].shape[0]
    for place in range(RADIX):
        for step, ref in enumerate(part_refs):

            @pl.when((place_ref[0] + RADIX - step) % RADIX == place)
            def _():
                span = pl.ds(place * rows, rows)
                delta = ref[...].astype(jnp.float32) / replicas
                new_momentum = momentum_rate * momentum_ref[span, :] + delta
                momentum_out[span, :] = new_momentum
                params_out[span, :] = base_ref[0, span, :] - outer_rate * (
                    delta + momentum_rate * new_momentum
                )


def update(replicas, place, parts, outer_params, momentum, fragment):
    shape = momentum.shape
    part = parts[0].shape

    def whole(block):
        return pl.BlockSpec(block, lambda i, fragment_ref, place_ref: (0,) * len(block))

    return pl.pallas_call(
        functools.partial(update_kernel, replicas),
        grid_spec=pltpu.PrefetchScalarGridSpec(
            num_scalar_prefetch=2,
            grid=(1,),
            in_specs=[whole(part)] * RADIX
            + [
                pl.BlockSpec(
                    (1,) + shape, lambda i, fragment_ref, place_ref: (fragment_ref[0], 0, 0)
                ),
                whole(shape),
            ],
            out_specs=(whole(shape), whole(shape)),
        ),
        out_shape=(
            jax.ShapeDtypeStruct(shape, jnp.float32),
            jax.ShapeDtypeStruct(shape, jnp.float32),
        ),
        compiler_params=PARAMS,
        name="update",
    )(fragment, place, *parts, outer_params, momentum)


def shift(part, axis, step):
    size = lax.axis_size(axis)
    return lax.ppermute(part, axis, [(i, (i + step) % size) for i in range(size)])


def scatter_stage(parts, axis):
    return [parts[0]] + [shift(parts[step], axis, step) for step in range(1, RADIX)]


def gather_stage(part, axis):
    return [part] + [shift(part, axis, step) for step in range(1, RADIX)]


def place_on(axis):
    return lax.axis_index(axis).astype(jnp.int32).reshape(1)


def replica_sum(pseudo_values, block_scales):
    near, far = place_on("z_near"), place_on("z_far")
    parts = scatter_stage(dequant(near, pseudo_values, block_scales), "z_near")
    parts = scatter_stage(add_split(far, parts), "z_far")
    return add_parts(parts)


def outer_step(part, outer_params, momentum, fragment):
    near, far = place_on("z_near"), place_on("z_far")
    part = add_parts([part, shift(part, "y_far", 1)])
    part = join(far, gather_stage(part, "z_far"))
    parts = gather_stage(part, "z_near")
    replicas = lax.axis_size(("y_far", "z_far", "z_near"))
    return update(replicas, near, parts, outer_params, momentum, fragment)


def exchange(rows, experts):
    width = rows.shape[1]
    return lax.all_to_all(
        rows.reshape(experts, CAP, width), "chip", split_axis=0, concat_axis=0, tiled=True
    ).reshape(experts * CAP, width)


def shards(
    tokens,
    expert_ids,
    route_weights,
    w_gate,
    w_up,
    w_down,
    pseudo_values,
    block_scales,
    outer_params,
    momentum,
    fragment,
):
    experts = lax.axis_size("chip")
    buffer, combine = route(tokens, expert_ids, route_weights, experts)
    mine = exchange(buffer, experts)
    own = (w_gate, w_up, w_down)
    other = [shift(w, "core", 1) for w in own]
    part = replica_sum(pseudo_values, block_scales)
    mine, part = lax.optimization_barrier((mine, part))
    returned = exchange(expert_rows(mine, own, other), experts)
    moe_out = combine_rows(combine, returned)
    new_params, new_momentum = outer_step(part, outer_params, momentum, fragment)
    return (moe_out, new_params, new_momentum)


def solution(mesh):
    reps, exps = mesh.devices.shape
    fine = Mesh(
        mesh.devices.reshape(reps // (RADIX * RADIX), RADIX, RADIX, exps // 2, 2),
        ("y_far", "z_far", "z_near", "chip", "core"),
    )
    rep = ("y_far", "z_far", "z_near")
    exp = ("chip", "core")
    return jax.shard_map(
        shards,
        mesh=fine,
        in_specs=(
            P(rep + exp, None),
            P(rep + exp, None),
            P(rep + exp, None),
            P(exp, None, None),
            P(exp, None, None),
            P(exp, None, None),
            P(rep, exp, None),
            P(rep, exp, None),
            P(None, exp, None),
            P(exp, None),
            P(),
        ),
        out_specs=(P(rep + exp, None), P(exp, None), P(exp, None)),
        check_vma=False,
    )
```

time: 155 us -> 143 us (0.923); the launches traced: 152 us -> 142 us
  starting transfers between devices: 35.5 us -> 85.8 us
  blocking collectives: 33.2 us -> 0 us
  waiting for transfers between devices: 56 us -> 37.1 us
  matrix products: 13.8 us -> 0 us
  Pallas kernels: 0.55 us -> 10.7 us
  other arithmetic: 4.59 us -> 0 us
    ppermute x2 -> x16, starting transfers between devices: 4.02 us -> 61.5 us  [shift(): lax.ppermute(part, axis, [(i, (i + step) % size) for i in range(size)])]
    all_to_all x3 -> x2, waiting for transfers between devices: 56 us -> 0.01 us  [exchange(): lax.all_to_all(rows.reshape(experts, CAP, width), 'chip', split_axis=0, c...]
    ppermute x2 -> x16, waiting for transfers between devices: 0.01 us -> 37.1 us  [shift(): lax.ppermute(part, axis, [(i, (i + step) % size) for i in range(size)])]
    all_to_all x1 -> x0, blocking collectives: 33.2 us -> none  [shards(): lax.all_to_all(buffer.reshape(experts, CAP, width), 'chip', split_axis=0,...]
    dot_general x5 -> x0, matrix products: 13.8 us -> none  [the longest x2 8.11 us: expert_half(): jnp.dot(hidden, w_down, preferred_element_type=jnp.float32)]
    pallas_call x0 -> x8, Pallas kernels: none -> 10.1 us  [the longest x1 6.86 us: expert_rows(): pl.pallas_call(expert_kernel, out_shape=jax.ShapeDtypeStruct(rows.shape,...]
    all_to_all x3 -> x2, starting transfers between devices: 31.5 us -> 24.3 us  [exchange(): lax.all_to_all(rows.reshape(experts, CAP, width), 'chip', split_axis=0, c...]
    unnamed x12 -> x22, local copies, waits for them, and re-layouts: 2.54 us -> 7.39 us
  transfers between devices with their start and end apart: 5 -> 18, of which waited for: 3 -> 9; matrix products, arithmetic and copies ran while one was open for 14% -> 0% of each run, Pallas kernels for 0% -> 1%
where the time goes in v2:
time: 143 us; the launch traced here: 142 us
  starting transfers between devices  85.8 us (60%)
  waiting for transfers between devices  37.1 us (26%)
  Pallas kernels  10.7 us (7%)
  local copies, waits for them, and re-layouts  7.39 us (5%)
  between operations  1.57 us (1%)
    ppermute x16, starting transfers between devices, shift(): lax.ppermute(part, axis, [(i, (i + step) % size) for i in range(size)])  61.5 us
    ppermute x16, waiting for transfers between devices, shift(): lax.ppermute(part, axis, [(i, (i + step) % size) for i in range(size)])  37.1 us
    all_to_all x2, starting transfers between devices, exchange(): lax.all_to_all(rows.reshape(experts, CAP, width), 'chip', split_axis=0, c...  24.3 us
    unnamed x22, local copies, waits for them, and re-layouts  7.39 us
    pallas_call x1, Pallas kernels, expert_rows(): pl.pallas_call(expert_kernel, out_shape=jax.ShapeDtypeStruct(rows.shape,...  6.86 us
  transfers between devices with their start and end apart: 18, of which 9 were waited for; matrix products, arithmetic and copies ran while one was open for 0% of the time, Pallas kernels for 1%

profile of v2, /device:TPU:6, one launch (start us, length us, event | category | flops | bytes accessed | tf_op | source)
XLA Modules:
  0.0 142.5 jit_solution(3014223416716720682)
XLA Ops:
  4.7 16.6 %all-to-all-start = ((bf16[16,16,2048]{2,1,0:T(8,128)(2,1)}), bf16[16,16,2048]{2,1,0:T(8,128)(2,1)S(1)}, u32[]{:S(2)}, u32[]{:S(2)}) async-start(bf16[16,16,2048]{2,1,0:T(8,128)(2,1)} %bitcast.13), calls=%async_computation | async-start | bytes 2097152 | tf_op jit(solution)/shard_map/all_to_all | solution.py:287
  21.4 1.9 %collective-permute-start.6 = (bf16[1,2048,384]{2,1,0:T(8,128)(2,1)S(1)}, bf16[1,2048,384]{2,1,0:T(8,128)(2,1)}, u32[]{:S(2)}, u32[]{:S(2)}) collective-permute-start(bf16[1,2048,384]{2,1,0:T(8,128)(2,1)S(1)} %copy-done.1), channel_id=1, source_target_pairs={{0,1},{1,0},{2,3},{3,2},{4,5},{5,4},{6,7},{7,6},{8,9},{9,8},{10,11... | collective-permute-start | bytes 4718600 | tf_op jit(solution)/shard_map/ppermute | solution.py:254
  23.3 2.4 %collective-permute-start.7 = (bf16[1,2048,384]{2,1,0:T(8,128)(2,1)}, bf16[1,2048,384]{2,1,0:T(8,128)(2,1)}, u32[]{:S(2)}, u32[]{:S(2)}) collective-permute-start(bf16[1,2048,384]{2,1,0:T(8,128)(2,1)} %u0_ref.1), channel_id=1, source_target_pairs={{0,1},{1,0},{2,3},{3,2},{4,5},{5,4},{6,7},{7,6},{8,9},{9,8},{10,11... | collective-permute-start | bytes 4718600 | tf_op jit(solution)/shard_map/ppermute | solution.py:254
  25.7 1.9 %collective-permute-start.8 = (bf16[1,384,2048]{2,1,0:T(8,128)(2,1)}, bf16[1,384,2048]{2,1,0:T(8,128)(2,1)}, u32[]{:S(2)}, u32[]{:S(2)}) collective-permute-start(bf16[1,384,2048]{2,1,0:T(8,128)(2,1)} %d0_ref.1), channel_id=1, source_target_pairs={{0,1},{1,0},{2,3},{3,2},{4,5},{5,4},{6,7},{7,6},{8,9},{9,8},{10,11... | collective-permute-start | bytes 4718600 | tf_op jit(solution)/shard_map/ppermute | solution.py:254
  28.3 1.9 %collective-permute-start = (bf16[16,2048]{1,0:T(8,128)(2,1)S(1)}, bf16[16,2048]{1,0:T(8,128)(2,1)S(1)}, u32[]{:S(2)}, u32[]{:S(2)}) collective-permute-start(bf16[16,2048]{1,0:T(8,128)(2,1)S(1)} %get-tuple-element.20), channel_id=1, source_target_pairs={{0,32},{32,64},{64,96},{96,0},{1,33},{33,65},{65,97},{97,1},{2,34}... | collective-permute-start | bytes 196616 | tf_op jit(solution)/shard_map/ppermute | solution.py:254
  32.2 4.4 %collective-permute-done.refs_1_ = bf16[16,2048]{1,0:T(8,128)(2,1)S(1)} collective-permute-done((bf16[16,2048]{1,0:T(8,128)(2,1)S(1)}, bf16[16,2048]{1,0:T(8,128)(2,1)S(1)}, u32[]{:S(2)}, u32[]{:S(2)}) %collective-permute-start) | collective-permute-done | bytes 65568 | tf_op jit(solution)/shard_map/ppermute | solution.py:254
  39.3 3.4 %collective-permute-done.2.refs_3_ = bf16[16,2048]{1,0:T(8,128)(2,1)S(1)} collective-permute-done((bf16[16,2048]{1,0:T(8,128)(2,1)S(1)}, bf16[16,2048]{1,0:T(8,128)(2,1)S(1)}, u32[]{:S(2)}, u32[]{:S(2)}) %collective-permute-start.2) | collective-permute-done | bytes 65568 | tf_op jit(solution)/shard_map/ppermute | solution.py:254
  42.9 4.5 %collective-permute-start.3 = (bf16[16,512]{1,0:T(8,128)(2,1)S(1)}, bf16[16,512]{1,0:T(8,128)(2,1)S(1)}, u32[]{:S(2)}, u32[]{:S(2)}) collective-permute-start(bf16[16,512]{1,0:T(8,128)(2,1)S(1)} %get-tuple-element.24), channel_id=1, source_target_pairs={{0,128},{128,256},{256,384},{384,0},{1,129},{129,257},{257,385},{3... | collective-permute-start | bytes 49160 | tf_op jit(solution)/shard_map/ppermute | solution.py:254
  47.4 12.1 %collective-permute-start.4 = (bf16[16,512]{1,0:T(8,128)(2,1)S(1)}, bf16[16,512]{1,0:T(8,128)(2,1)S(1)}, u32[]{:S(2)}, u32[]{:S(2)}) collective-permute-start(bf16[16,512]{1,0:T(8,128)(2,1)S(1)} %get-tuple-element.25), channel_id=1, source_target_pairs={{0,256},{128,384},{256,0},{384,128},{1,257},{129,385},{257,1},{385... | collective-permute-start | bytes 49160 | tf_op jit(solution)/shard_map/ppermute | solution.py:254
  59.5 3.6 %collective-permute-start.5 = (bf16[16,512]{1,0:T(8,128)(2,1)S(1)}, bf16[16,512]{1,0:T(8,128)(2,1)S(1)}, u32[]{:S(2)}, u32[]{:S(2)}) collective-permute-start(bf16[16,512]{1,0:T(8,128)(2,1)S(1)} %get-tuple-element.26), channel_id=1, source_target_pairs={{0,384},{128,0},{256,128},{384,256},{1,385},{129,1},{257,129},{385... | collective-permute-start | bytes 49160 | tf_op jit(solution)/shard_map/ppermute | solution.py:254
  63.2 6.1 %collective-permute-done.5.refs_3_ = bf16[16,512]{1,0:T(8,128)(2,1)S(1)} collective-permute-done((bf16[16,512]{1,0:T(8,128)(2,1)S(1)}, bf16[16,512]{1,0:T(8,128)(2,1)S(1)}, u32[]{:S(2)}, u32[]{:S(2)}) %collective-permute-start.5) | collective-permute-done | bytes 16416 | tf_op jit(solution)/shard_map/ppermute | solution.py:254
  72.2 6.9 %expert_rows.1 = bf16[256,2048]{1,0:T(8,128)(2,1)} custom-call(bf16[256,2048]{1,0:T(8,128)(2,1)S(1)} %bitcast.12, bf16[1,2048,384]{2,1,0:T(8,128)(2,1)S(1)} %copy-done.1, bf16[1,2048,384]{2,1,0:T(8,128)(2,1)S(1)} %copy-done.2, bf16[1,384,2048]{2,1,0:T(8,128)(2,1)S(1)} %copy-done.3, bf16[1,2048,384]{2,1,0:T(8,128)(2,1)} %collective-permute-done.6.g1_ref, ...), custom_call_target="tpu_custom_call" | custom-call | tf_op jit(solution)/shard_map/expert_rows/pallas_call | solution.py:81
  79.1 7.6 %all-to-all-start.1 = ((bf16[16,16,2048]{2,1,0:T(8,128)(2,1)}), bf16[16,16,2048]{2,1,0:T(8,128)(2,1)S(1)}, u32[]{:S(2)}, u32[]{:S(2)}) async-start(bf16[16,16,2048]{2,1,0:T(8,128)(2,1)} %bitcast.8), calls=%async_computation.1 | async-start | bytes 2097152 | tf_op jit(solution)/shard_map/all_to_all | solution.py:287
  86.7 5.0 %collective-permute-start.9 = (bf16[16,512]{1,0:T(8,128)(2,1)S(1)}, bf16[16,512]{1,0:T(8,128)(2,1)S(1)}, u32[]{:S(2)}, u32[]{:S(2)}) collective-permute-start(bf16[16,512]{1,0:T(8,128)(2,1)S(1)} %add_parts.2.refs_0_), channel_id=1, source_target_pairs={{0,512},{512,0},{1,513},{513,1},{2,514},{514,2},{3,515},{515,3},{4... | collective-permute-start | bytes 49160 | tf_op jit(solution)/shard_map/ppermute | solution.py:254
  91.7 13.2 %collective-permute-done.9.refs_1_ = bf16[16,512]{1,0:T(8,128)(2,1)S(1)} collective-permute-done((bf16[16,512]{1,0:T(8,128)(2,1)S(1)}, bf16[16,512]{1,0:T(8,128)(2,1)S(1)}, u32[]{:S(2)}, u32[]{:S(2)}) %collective-permute-start.9) | collective-permute-done | bytes 16416 | tf_op jit(solution)/shard_map/ppermute | solution.py:254
  104.9 2.4 %collective-permute-start.10 = (bf16[16,512]{1,0:T(8,128)(2,1)S(1)}, bf16[16,512]{1,0:T(8,128)(2,1)S(1)}, u32[]{:S(2)}, u32[]{:S(2)}) collective-permute-start(bf16[16,512]{1,0:T(8,128)(2,1)S(1)} %add_parts.3.refs_0_), channel_id=1, source_target_pairs={{0,128},{128,256},{256,384},{384,0},{1,129},{129,257},{257,385},{3... | collective-permute-start | bytes 49160 | tf_op jit(solution)/shard_map/ppermute | solution.py:254
  107.3 8.5 %collective-permute-start.11 = (bf16[16,512]{1,0:T(8,128)(2,1)S(1)}, bf16[16,512]{1,0:T(8,128)(2,1)S(1)}, u32[]{:S(2)}, u32[]{:S(2)}) collective-permute-start(bf16[16,512]{1,0:T(8,128)(2,1)S(1)} %add_parts.3.refs_0_), channel_id=1, source_target_pairs={{0,256},{128,384},{256,0},{384,128},{1,257},{129,385},{257,1},{385... | collective-permute-start | bytes 49160 | tf_op jit(solution)/shard_map/ppermute | solution.py:254
  115.8 3.8 %collective-permute-start.12 = (bf16[16,512]{1,0:T(8,128)(2,1)S(1)}, bf16[16,512]{1,0:T(8,128)(2,1)S(1)}, u32[]{:S(2)}, u32[]{:S(2)}) collective-permute-start(bf16[16,512]{1,0:T(8,128)(2,1)S(1)} %add_parts.3.refs_0_), channel_id=1, source_target_pairs={{0,384},{128,0},{256,128},{384,256},{1,385},{129,1},{257,129},{385... | collective-permute-start | bytes 49160 | tf_op jit(solution)/shard_map/ppermute | solution.py:254
  119.6 2.1 %collective-permute-done.11.refs_2_ = bf16[16,512]{1,0:T(8,128)(2,1)S(1)} collective-permute-done((bf16[16,512]{1,0:T(8,128)(2,1)S(1)}, bf16[16,512]{1,0:T(8,128)(2,1)S(1)}, u32[]{:S(2)}, u32[]{:S(2)}) %collective-permute-start.11) | collective-permute-done | bytes 16416 | tf_op jit(solution)/shard_map/ppermute | solution.py:254
  121.7 3.8 %collective-permute-done.12.refs_3_ = bf16[16,512]{1,0:T(8,128)(2,1)S(1)} collective-permute-done((bf16[16,512]{1,0:T(8,128)(2,1)S(1)}, bf16[16,512]{1,0:T(8,128)(2,1)S(1)}, u32[]{:S(2)}, u32[]{:S(2)}) %collective-permute-start.12) | collective-permute-done | bytes 16416 | tf_op jit(solution)/shard_map/ppermute | solution.py:254
  125.5 1.9 %collective-permute-start.13 = (bf16[16,2048]{1,0:T(8,128)(2,1)S(1)}, bf16[16,2048]{1,0:T(8,128)(2,1)S(1)}, u32[]{:S(2)}, u32[]{:S(2)}) collective-permute-start(bf16[16,2048]{1,0:T(8,128)(2,1)S(1)} %join.1.refs_0_), channel_id=1, source_target_pairs={{0,32},{32,64},{64,96},{96,0},{1,33},{33,65},{65,97},{97,1},{2,34}... | collective-permute-start | bytes 196616 | tf_op jit(solution)/shard_map/ppermute | solution.py:254
  127.4 5.4 %collective-permute-start.14 = (bf16[16,2048]{1,0:T(8,128)(2,1)S(1)}, bf16[16,2048]{1,0:T(8,128)(2,1)S(1)}, u32[]{:S(2)}, u32[]{:S(2)}) collective-permute-start(bf16[16,2048]{1,0:T(8,128)(2,1)S(1)} %join.1.refs_0_), channel_id=1, source_target_pairs={{0,64},{32,96},{64,0},{96,32},{1,65},{33,97},{65,1},{97,33},{2,66}... | collective-permute-start | bytes 196616 | tf_op jit(solution)/shard_map/ppermute | solution.py:254
  132.8 2.2 %collective-permute-start.15 = (bf16[16,2048]{1,0:T(8,128)(2,1)S(1)}, bf16[16,2048]{1,0:T(8,128)(2,1)S(1)}, u32[]{:S(2)}, u32[]{:S(2)}) collective-permute-start(bf16[16,2048]{1,0:T(8,128)(2,1)S(1)} %join.1.refs_0_), channel_id=1, source_target_pairs={{0,96},{32,0},{64,32},{96,64},{1,97},{33,1},{65,33},{97,65},{2,98}... | collective-permute-start | bytes 196616 | tf_op jit(solution)/shard_map/ppermute | solution.py:254
  135.8 3.2 %collective-permute-done.15.refs_3_ = bf16[16,2048]{1,0:T(8,128)(2,1)S(1)} collective-permute-done((bf16[16,2048]{1,0:T(8,128)(2,1)S(1)}, bf16[16,2048]{1,0:T(8,128)(2,1)S(1)}, u32[]{:S(2)}, u32[]{:S(2)}) %collective-permute-start.15) | collective-permute-done | bytes 65568 | tf_op jit(solution)/shard_map/ppermute | solution.py:254
  (43 shorter events, 16.0 us)
Async XLA Ops:
  0.6 20.8 %copy-start.1 = (bf16[1,2048,384]{2,1,0:T(8,128)(2,1)S(1)}, bf16[1,2048,384]{2,1,0:T(8,128)(2,1)}, u32[]{:S(2)}) copy-start(bf16[1,2048,384]{2,1,0:T(8,128)(2,1)} %g0_ref.1) | copy-start | bytes 4718596
  3.2 24.5 %copy-start.7 = (bf16[1,64,2048]{2,1,0:T(8,128)(2,1)S(1)}, bf16[1,64,2048]{2,1,0:T(8,128)(2,1)}, u32[]{:S(2)}) copy-start(bf16[1,64,2048]{2,1,0:T(8,128)(2,1)} %values_ref.1) | copy-start | bytes 786436
  3.2 24.5 %copy-start.8 = (f32[1,64,16]{1,2,0:T(8,128)S(1)}, f32[1,64,16]{1,2,0:T(8,128)}, u32[]{:S(2)}) copy-start(f32[1,64,16]{1,2,0:T(8,128)} %param.18) | copy-start | bytes 12292
  4.7 64.6 %all-to-all-start = ((bf16[16,16,2048]{2,1,0:T(8,128)(2,1)}), bf16[16,16,2048]{2,1,0:T(8,128)(2,1)S(1)}, u32[]{:S(2)}, u32[]{:S(2)}) async-start(bf16[16,16,2048]{2,1,0:T(8,128)(2,1)} %bitcast.13), calls=%async_computation | async-start | bytes 2097152 | tf_op jit(solution)/shard_map/all_to_all | solution.py:287
  21.4 48.0 %collective-permute-start.6 = (bf16[1,2048,384]{2,1,0:T(8,128)(2,1)S(1)}, bf16[1,2048,384]{2,1,0:T(8,128)(2,1)}, u32[]{:S(2)}, u32[]{:S(2)}) collective-permute-start(bf16[1,2048,384]{2,1,0:T(8,128)(2,1)S(1)} %copy-done.1), channel_id=1, source_target_pairs={{0,1},{1,0},{2,3},{3,2},{4,5},{5,4},{6,7},{7,6},{8,9},{9,8},{10,11... | collective-permute-start | bytes 4718600 | tf_op jit(solution)/shard_map/ppermute | solution.py:254
  23.3 46.0 %collective-permute-start.7 = (bf16[1,2048,384]{2,1,0:T(8,128)(2,1)}, bf16[1,2048,384]{2,1,0:T(8,128)(2,1)}, u32[]{:S(2)}, u32[]{:S(2)}) collective-permute-start(bf16[1,2048,384]{2,1,0:T(8,128)(2,1)} %u0_ref.1), channel_id=1, source_target_pairs={{0,1},{1,0},{2,3},{3,2},{4,5},{5,4},{6,7},{7,6},{8,9},{9,8},{10,11... | collective-permute-start | bytes 4718600 | tf_op jit(solution)/shard_map/ppermute | solution.py:254
  25.7 43.6 %collective-permute-start.8 = (bf16[1,384,2048]{2,1,0:T(8,128)(2,1)}, bf16[1,384,2048]{2,1,0:T(8,128)(2,1)}, u32[]{:S(2)}, u32[]{:S(2)}) collective-permute-start(bf16[1,384,2048]{2,1,0:T(8,128)(2,1)} %d0_ref.1), channel_id=1, source_target_pairs={{0,1},{1,0},{2,3},{3,2},{4,5},{5,4},{6,7},{7,6},{8,9},{9,8},{10,11... | collective-permute-start | bytes 4718600 | tf_op jit(solution)/shard_map/ppermute | solution.py:254
  28.3 8.2 %collective-permute-start = (bf16[16,2048]{1,0:T(8,128)(2,1)S(1)}, bf16[16,2048]{1,0:T(8,128)(2,1)S(1)}, u32[]{:S(2)}, u32[]{:S(2)}) collective-permute-start(bf16[16,2048]{1,0:T(8,128)(2,1)S(1)} %get-tuple-element.20), channel_id=1, source_target_pairs={{0,32},{32,64},{64,96},{96,0},{1,33},{33,65},{65,97},{97,1},{2,34}... | collective-permute-start | bytes 196616 | tf_op jit(solution)/shard_map/ppermute | solution.py:254
  30.2 9.1 %collective-permute-start.1 = (bf16[16,2048]{1,0:T(8,128)(2,1)S(1)}, bf16[16,2048]{1,0:T(8,128)(2,1)S(1)}, u32[]{:S(2)}, u32[]{:S(2)}) collective-permute-start(bf16[16,2048]{1,0:T(8,128)(2,1)S(1)} %get-tuple-element.21), channel_id=1, source_target_pairs={{0,64},{32,96},{64,0},{96,32},{1,65},{33,97},{65,1},{97,33},{2,66}... | collective-permute-start | bytes 196616 | tf_op jit(solution)/shard_map/ppermute | solution.py:254
  36.5 6.1 %collective-permute-start.2 = (bf16[16,2048]{1,0:T(8,128)(2,1)S(1)}, bf16[16,2048]{1,0:T(8,128)(2,1)S(1)}, u32[]{:S(2)}, u32[]{:S(2)}) collective-permute-start(bf16[16,2048]{1,0:T(8,128)(2,1)S(1)} %get-tuple-element.22), channel_id=1, source_target_pairs={{0,96},{32,0},{64,32},{96,64},{1,97},{33,1},{65,33},{97,65},{2,98}... | collective-permute-start | bytes 196616 | tf_op jit(solution)/shard_map/ppermute | solution.py:254
  42.9 16.6 %collective-permute-start.3 = (bf16[16,512]{1,0:T(8,128)(2,1)S(1)}, bf16[16,512]{1,0:T(8,128)(2,1)S(1)}, u32[]{:S(2)}, u32[]{:S(2)}) collective-permute-start(bf16[16,512]{1,0:T(8,128)(2,1)S(1)} %get-tuple-element.24), channel_id=1, source_target_pairs={{0,128},{128,256},{256,384},{384,0},{1,129},{129,257},{257,385},{3... | collective-permute-start | bytes 49160 | tf_op jit(solution)/shard_map/ppermute | solution.py:254
  47.4 15.8 %collective-permute-start.4 = (bf16[16,512]{1,0:T(8,128)(2,1)S(1)}, bf16[16,512]{1,0:T(8,128)(2,1)S(1)}, u32[]{:S(2)}, u32[]{:S(2)}) collective-permute-start(bf16[16,512]{1,0:T(8,128)(2,1)S(1)} %get-tuple-element.25), channel_id=1, source_target_pairs={{0,256},{128,384},{256,0},{384,128},{1,257},{129,385},{257,1},{385... | collective-permute-start | bytes 49160 | tf_op jit(solution)/shard_map/ppermute | solution.py:254
  59.5 9.8 %collective-permute-start.5 = (bf16[16,512]{1,0:T(8,128)(2,1)S(1)}, bf16[16,512]{1,0:T(8,128)(2,1)S(1)}, u32[]{:S(2)}, u32[]{:S(2)}) collective-permute-start(bf16[16,512]{1,0:T(8,128)(2,1)S(1)} %get-tuple-element.26), channel_id=1, source_target_pairs={{0,384},{128,0},{256,128},{384,256},{1,385},{129,1},{257,129},{385... | collective-permute-start | bytes 49160 | tf_op jit(solution)/shard_map/ppermute | solution.py:254
  69.4 1.4 copy-start.2
  70.8 1.4 copy-start.3
  79.1 59.9 %copy-start = (f32[3,64,2048]{2,1,0:T(8,128)S(1)}, f32[3,64,2048]{2,1,0:T(8,128)}, u32[]{:S(2)}) copy-start(f32[3,64,2048]{2,1,0:T(8,128)} %refs_4_.1) | copy-start | bytes 4718596
  79.1 62.3 %all-to-all-start.1 = ((bf16[16,16,2048]{2,1,0:T(8,128)(2,1)}), bf16[16,16,2048]{2,1,0:T(8,128)(2,1)S(1)}, u32[]{:S(2)}, u32[]{:S(2)}) async-start(bf16[16,16,2048]{2,1,0:T(8,128)(2,1)} %bitcast.8), calls=%async_computation.1 | async-start | bytes 2097152 | tf_op jit(solution)/shard_map/all_to_all | solution.py:287
  86.7 18.2 %collective-permute-start.9 = (bf16[16,512]{1,0:T(8,128)(2,1)S(1)}, bf16[16,512]{1,0:T(8,128)(2,1)S(1)}, u32[]{:S(2)}, u32[]{:S(2)}) collective-permute-start(bf16[16,512]{1,0:T(8,128)(2,1)S(1)} %add_parts.2.refs_0_), channel_id=1, source_target_pairs={{0,512},{512,0},{1,513},{513,1},{2,514},{514,2},{3,515},{515,3},{4... | collective-permute-start | bytes 49160 | tf_op jit(solution)/shard_map/ppermute | solution.py:254
  104.9 14.7 %collective-permute-start.10 = (bf16[16,512]{1,0:T(8,128)(2,1)S(1)}, bf16[16,512]{1,0:T(8,128)(2,1)S(1)}, u32[]{:S(2)}, u32[]{:S(2)}) collective-permute-start(bf16[16,512]{1,0:T(8,128)(2,1)S(1)} %add_parts.3.refs_0_), channel_id=1, source_target_pairs={{0,128},{128,256},{256,384},{384,0},{1,129},{129,257},{257,385},{3... | collective-permute-start | bytes 49160 | tf_op jit(solution)/shard_map/ppermute | solution.py:254
  107.3 14.3 %collective-permute-start.11 = (bf16[16,512]{1,0:T(8,128)(2,1)S(1)}, bf16[16,512]{1,0:T(8,128)(2,1)S(1)}, u32[]{:S(2)}, u32[]{:S(2)}) collective-permute-start(bf16[16,512]{1,0:T(8,128)(2,1)S(1)} %add_parts.3.refs_0_), channel_id=1, source_target_pairs={{0,256},{128,384},{256,0},{384,128},{1,257},{129,385},{257,1},{385... | collective-permute-start | bytes 49160 | tf_op jit(solution)/shard_map/ppermute | solution.py:254
  115.8 9.7 %collective-permute-start.12 = (bf16[16,512]{1,0:T(8,128)(2,1)S(1)}, bf16[16,512]{1,0:T(8,128)(2,1)S(1)}, u32[]{:S(2)}, u32[]{:S(2)}) collective-permute-start(bf16[16,512]{1,0:T(8,128)(2,1)S(1)} %add_parts.3.refs_0_), channel_id=1, source_target_pairs={{0,384},{128,0},{256,128},{384,256},{1,385},{129,1},{257,129},{385... | collective-permute-start | bytes 49160 | tf_op jit(solution)/shard_map/ppermute | solution.py:254
  125.5 10.2 %collective-permute-start.13 = (bf16[16,2048]{1,0:T(8,128)(2,1)S(1)}, bf16[16,2048]{1,0:T(8,128)(2,1)S(1)}, u32[]{:S(2)}, u32[]{:S(2)}) collective-permute-start(bf16[16,2048]{1,0:T(8,128)(2,1)S(1)} %join.1.refs_0_), channel_id=1, source_target_pairs={{0,32},{32,64},{64,96},{96,0},{1,33},{33,65},{65,97},{97,1},{2,34}... | collective-permute-start | bytes 196616 | tf_op jit(solution)/shard_map/ppermute | solution.py:254
  127.4 8.4 %collective-permute-start.14 = (bf16[16,2048]{1,0:T(8,128)(2,1)S(1)}, bf16[16,2048]{1,0:T(8,128)(2,1)S(1)}, u32[]{:S(2)}, u32[]{:S(2)}) collective-permute-start(bf16[16,2048]{1,0:T(8,128)(2,1)S(1)} %join.1.refs_0_), channel_id=1, source_target_pairs={{0,64},{32,96},{64,0},{96,32},{1,65},{33,97},{65,1},{97,33},{2,66}... | collective-permute-start | bytes 196616 | tf_op jit(solution)/shard_map/ppermute | solution.py:254
  132.8 6.2 %collective-permute-start.15 = (bf16[16,2048]{1,0:T(8,128)(2,1)S(1)}, bf16[16,2048]{1,0:T(8,128)(2,1)S(1)}, u32[]{:S(2)}, u32[]{:S(2)}) collective-permute-start(bf16[16,2048]{1,0:T(8,128)(2,1)S(1)} %join.1.refs_0_), channel_id=1, source_target_pairs={{0,96},{32,0},{64,32},{96,64},{1,97},{33,1},{65,33},{97,65},{2,98}... | collective-permute-start | bytes 196616 | tf_op jit(solution)/shard_map/ppermute | solution.py:254
  (5 other events, 4.6 us)

commit v3 on v2

v3 whole, which is shorter than its diff:
```python
import functools

import jax
import jax.numpy as jnp
from jax import lax
from jax.experimental import pallas as pl
from jax.experimental.pallas import tpu as pltpu
from jax.sharding import Mesh
from jax.sharding import PartitionSpec as P

CAP = 16
PIECE_ROWS = 16

momentum_rate = 0.9
outer_rate = 0.7

PARAMS = pltpu.CompilerParams(vmem_limit_bytes=20 * 1024 * 1024)
VMEM = pl.BlockSpec(memory_space=pltpu.VMEM)
SMEM = pl.BlockSpec(memory_space=pltpu.SMEM)


def route_kernel(experts, ids_ref, weights_ref, tokens_ref, buffer_ref, combine_ref):
    topk, rows = ids_ref.shape
    ids = ids_ref[...]
    weights = weights_ref[...]
    expert = lax.broadcasted_iota(jnp.int32, (experts, rows), 0)
    named = jnp.zeros((experts, rows), jnp.float32)
    weight = jnp.zeros((experts, rows), jnp.float32)
    for k in range(topk):
        hit = ids[k : k + 1, :] == expert
        named = named + hit.astype(jnp.float32)
        weight = weight + jnp.where(hit, weights[k : k + 1, :], 0.0)
    earlier = lax.broadcasted_iota(jnp.int32, (rows, rows), 0) < lax.broadcasted_iota(
        jnp.int32, (rows, rows), 1
    )
    rank = jnp.dot(
        named.astype(jnp.bfloat16),
        earlier.astype(jnp.bfloat16),
        preferred_element_type=jnp.float32,
    ).astype(jnp.int32)
    rank = jnp.where(named > 0.5, rank, CAP)
    place = lax.broadcasted_iota(jnp.int32, (experts, CAP, rows), 1)
    chosen = rank[:, None, :] == place
    pick = jnp.where(chosen, 1.0, 0.0).reshape(experts * CAP, rows)
    combine_ref[...] = (
        jnp.where(chosen, jnp.broadcast_to(weight[:, None, :], chosen.shape), 0.0)
        .reshape(experts * CAP, rows)
        .astype(jnp.bfloat16)
    )
    buffer_ref[...] = jnp.dot(
        pick.astype(jnp.bfloat16), tokens_ref[...], preferred_element_type=jnp.float32
    ).astype(jnp.bfloat16)


def route(tokens, expert_ids, route_weights, experts):
    rows, width = tokens.shape
    return pl.pallas_call(
        functools.partial(route_kernel, experts),
        out_shape=(
            jax.ShapeDtypeStruct((experts * CAP, width), jnp.bfloat16),
            jax.ShapeDtypeStruct((experts * CAP, rows), jnp.bfloat16),
        ),
        compiler_params=PARAMS,
        name="route",
    )(expert_ids.T, route_weights.T, tokens)


def expert_kernel(rows_ref, g0_ref, u0_ref, d0_ref, g1_ref, u1_ref, d1_ref, out_ref):
    rows = rows_ref[...]
    total = None
    for gate_ref, up_ref, down_ref in ((g0_ref, u0_ref, d0_ref), (g1_ref, u1_ref, d1_ref)):
        gate = jnp.dot(rows, gate_ref[0], preferred_element_type=jnp.float32)
        up = jnp.dot(rows, up_ref[0], preferred_element_type=jnp.float32)
        hidden = (gate / (1.0 + jnp.exp(-gate)) * up).astype(jnp.bfloat16)
        part = jnp.dot(hidden, down_ref[0], preferred_element_type=jnp.float32)
        total = part if total is None else total + part
    out_ref[...] = total.astype(jnp.bfloat16)


def expert_rows(rows, own, other):
    return pl.pallas_call(
        expert_kernel,
        out_shape=jax.ShapeDtypeStruct(rows.shape, jnp.bfloat16),
        compiler_params=PARAMS,
        name="expert_rows",
    )(rows, *own, *other)


def combine_kernel(combine_ref, rows_ref, out_ref):
    out_ref[...] = lax.dot_general(
        combine_ref[...],
        rows_ref[...],
        (((0,), (0,)), ((), ())),
        preferred_element_type=jnp.float32,
    ).astype(jnp.bfloat16)


def combine_rows(combine, rows):
    return pl.pallas_call(
        combine_kernel,
        out_shape=jax.ShapeDtypeStruct((combine.shape[1], rows.shape[1]), jnp.bfloat16),
        compiler_params=PARAMS,
        name="combine_rows",
    )(combine, rows)


def dequant_kernel(values_ref, scales_ref, out_ref):
    replicas, rows, span = out_ref.shape
    width = values_ref.shape[2]
    blocks = scales_ref.shape[0]
    column = lax.broadcasted_iota(jnp.int32, (blocks, width), 1) // (width // blocks)
    spread = (column == lax.broadcasted_iota(jnp.int32, (blocks, width), 0)).astype(jnp.bfloat16)
    scales = scales_ref[...]
    high = scales.astype(jnp.bfloat16)
    rest = scales - high.astype(jnp.float32)
    middle = rest.astype(jnp.bfloat16)
    low = (rest - middle.astype(jnp.float32)).astype(jnp.bfloat16)
    wide = sum(
        lax.dot_general(
            part, spread, (((0,), (0,)), ((), ())), preferred_element_type=jnp.float32
        )
        for part in (high, middle, low)
    )
    whole = (values_ref[0].astype(jnp.float32) * wide).astype(jnp.bfloat16)
    across = width // span
    for piece in range(replicas):
        row, column = piece // across * rows, piece % across * span
        out_ref[piece] = whole[row : row + rows, column : column + span]


def dequant(values, scales, replicas):
    _, rows, width = values.shape
    shape = (replicas, PIECE_ROWS, rows * width // (replicas * PIECE_ROWS))
    return pl.pallas_call(
        dequant_kernel,
        out_shape=jax.ShapeDtypeStruct(shape, jnp.bfloat16),
        compiler_params=PARAMS,
        name="dequant",
    )(values, scales[0].T)


def total_kernel(parts_ref, out_ref):
    total = jnp.sum(parts_ref[...].astype(jnp.float32), axis=0).astype(jnp.bfloat16)
    out_ref[...] = jnp.broadcast_to(total[None], out_ref.shape)


def total_spread(parts):
    return pl.pallas_call(
        total_kernel,
        out_shape=jax.ShapeDtypeStruct(parts.shape, jnp.bfloat16),
        compiler_params=PARAMS,
        name="total_spread",
    )(parts)


def update_kernel(fragment_ref, totals_ref, base_ref, momentum_ref, params_out, momentum_out):
    replicas, rows, span = totals_ref.shape
    across = momentum_ref.shape[1] // span
    for piece in range(replicas):
        at = (
            pl.ds(piece // across * rows, rows),
            pl.ds(piece % across * span, span),
        )
        delta = totals_ref[piece].astype(jnp.float32) / replicas
        new_momentum = momentum_rate * momentum_ref[at] + delta
        momentum_out[at] = new_momentum
        params_out[at] = base_ref[(0,) + at] - outer_rate * (delta + momentum_rate * new_momentum)


def update(totals, outer_params, momentum, fragment):
    shape = momentum.shape

    def whole(block):
        return pl.BlockSpec(block, lambda i, fragment_ref: (0,) * len(block))

    return pl.pallas_call(
        update_kernel,
        grid_spec=pltpu.PrefetchScalarGridSpec(
            num_scalar_prefetch=1,
            grid=(1,),
            in_specs=[
                whole(totals.shape),
                pl.BlockSpec((1,) + shape, lambda i, fragment_ref: (fragment_ref[0], 0, 0)),
                whole(shape),
            ],
            out_specs=(whole(shape), whole(shape)),
        ),
        out_shape=(
            jax.ShapeDtypeStruct(shape, jnp.float32),
            jax.ShapeDtypeStruct(shape, jnp.float32),
        ),
        compiler_params=PARAMS,
        name="update",
    )(fragment, totals, outer_params, momentum)


def shift(part, axis, step):
    size = lax.axis_size(axis)
    return lax.ppermute(part, axis, [(i, (i + step) % size) for i in range(size)])


def swap_pieces(pieces):
    return lax.all_to_all(pieces, "rep", split_axis=0, concat_axis=0, tiled=True)


def exchange(rows, experts):
    width = rows.shape[1]
    return lax.all_to_all(
        rows.reshape(experts, CAP, width), "chip", split_axis=0, concat_axis=0, tiled=True
    ).reshape(experts * CAP, width)


def shards(
    tokens,
    expert_ids,
    route_weights,
    w_gate,
    w_up,
    w_down,
    pseudo_values,
    block_scales,
    outer_params,
    momentum,
    fragment,
):
    experts = lax.axis_size("chip")
    buffer, combine = route(tokens, expert_ids, route_weights, experts)
    mine = exchange(buffer, experts)
    own = (w_gate, w_up, w_down)
    other = [shift(w, "core", 1) for w in own]
    parts = swap_pieces(dequant(pseudo_values, block_scales, lax.axis_size("rep")))
    mine, parts = lax.optimization_barrier((mine, parts))
    returned = exchange(expert_rows(mine, own, other), experts)
    moe_out = combine_rows(combine, returned)
    totals = swap_pieces(total_spread(parts))
    new_params, new_momentum = update(totals, outer_params, momentum, fragment)
    return (moe_out, new_params, new_momentum)


def solution(mesh):
    reps, exps = mesh.devices.shape
    fine = Mesh(mesh.devices.reshape(reps, exps // 2, 2), ("rep", "chip", "core"))
    exp = ("chip", "core")
    return jax.shard_map(
        shards,
        mesh=fine,
        in_specs=(
            P(("rep",) + exp, None),
            P(("rep",) + exp, None),
            P(("rep",) + exp, None),
            P(exp, None, None),
            P(exp, None, None),
            P(exp, None, None),
            P("rep", exp, None),
            P("rep", exp, None),
            P(None, exp, None),
            P(exp, None),
            P(),
        ),
        out_specs=(P(("rep",) + exp, None), P(exp, None), P(exp, None)),
        check_vma=False,
    )
```

time: 143 us -> 147 us (1.028); the launches traced: 142 us -> 145 us
  waiting for transfers between devices: 37.1 us -> 76.1 us
  starting transfers between devices: 85.8 us -> 47.8 us
    ppermute x16 -> x3, starting transfers between devices: 61.5 us -> 6.25 us  [shift(): lax.ppermute(part, axis, [(i, (i + step) % size) for i in range(size)])]
    all_to_all x2, waiting for transfers between devices: 0.01 us -> 38.4 us  [exchange(): lax.all_to_all(rows.reshape(experts, CAP, width), 'chip', split_axis=0, c...]
    all_to_all x0 -> x2, waiting for transfers between devices: none -> 37.7 us  [swap_pieces(): lax.all_to_all(pieces, 'rep', split_axis=0, concat_axis=0, tiled=True)]
    ppermute x16 -> x3, waiting for transfers between devices: 37.1 us -> 0.01 us  [shift(): lax.ppermute(part, axis, [(i, (i + step) % size) for i in range(size)])]
    all_to_all x0 -> x2, starting transfers between devices: none -> 29.9 us  [swap_pieces(): lax.all_to_all(pieces, 'rep', split_axis=0, concat_axis=0, tiled=True)]
    all_to_all x2, starting transfers between devices: 24.3 us -> 11.6 us  [exchange(): lax.all_to_all(rows.reshape(experts, CAP, width), 'chip', split_axis=0, c...]
    pallas_call x6 -> x3, Pallas kernels: 2.13 us -> 2.96 us  [the longest x1 1.1 us: update(): pl.pallas_call(update_kernel, grid_spec=pltpu.PrefetchScalarGridSpec(num_...]
  transfers between devices with their start and end apart: 18 -> 7, of which waited for: 9 -> 4; matrix products, arithmetic and copies ran while one was open for 0% -> 0% of each run, Pallas kernels for 1% -> 6%
where the time goes in v3:
time: 147 us; the launch traced here: 145 us
  waiting for transfers between devices  76.1 us (52%)
  starting transfers between devices  47.8 us (33%)
  Pallas kernels  11.5 us (8%)
  local copies, waits for them, and re-layouts  7.85 us (5%)
    all_to_all x2, waiting for transfers between devices, exchange(): lax.all_to_all(rows.reshape(experts, CAP, width), 'chip', split_axis=0, c...  38.4 us
    all_to_all x2, waiting for transfers between devices, swap_pieces(): lax.all_to_all(pieces, 'rep', split_axis=0, concat_axis=0, tiled=True)  37.7 us
    all_to_all x2, starting transfers between devices, swap_pieces(): lax.all_to_all(pieces, 'rep', split_axis=0, concat_axis=0, tiled=True)  29.9 us
    all_to_all x2, starting transfers between devices, exchange(): lax.all_to_all(rows.reshape(experts, CAP, width), 'chip', split_axis=0, c...  11.6 us
    unnamed x22, local copies, waits for them, and re-layouts  7.85 us
    pallas_call x1, Pallas kernels, expert_rows(): pl.pallas_call(expert_kernel, out_shape=jax.ShapeDtypeStruct(rows.shape,...  6.85 us
    ppermute x3, starting transfers between devices, shift(): lax.ppermute(part, axis, [(i, (i + step) % size) for i in range(size)])  6.25 us
  transfers between devices with their start and end apart: 7, of which 4 were waited for; matrix products, arithmetic and copies ran while one was open for 0% of the time, Pallas kernels for 6%

profile of v3, /device:TPU:6, one launch (start us, length us, event | category | flops | bytes accessed | tf_op | source)
XLA Modules:
  0.0 144.6 jit_solution(8736670676662307813)
XLA Ops:
  0.6 0.9 copy-done.7
  1.6 0.7 copy-done.8
  2.3 1.1 dequant.1
  3.4 24.5 %all-to-all-start.1 = ((bf16[32,16,256]{2,1,0:T(8,128)(2,1)}), bf16[32,16,256]{2,1,0:T(8,128)(2,1)S(1)}, u32[]{:S(2)}, u32[]{:S(2)}) async-start(bf16[32,16,256]{2,1,0:T(8,128)(2,1)} %dequant.1), calls=%async_computation.1 | async-start | bytes 524288 | tf_op jit(solution)/shard_map/all_to_all | solution.py:203
  27.9 1.0 copy-done.6
  29.0 0.7 copy-done.9
  29.7 0.7 copy-done.10
  30.9 1.0 copy-done.4
  31.9 22.2 %all-to-all-done.1.parts_ref = bf16[32,16,256]{2,1,0:T(8,128)(2,1)S(1)} async-done(((bf16[32,16,256]{2,1,0:T(8,128)(2,1)}), bf16[32,16,256]{2,1,0:T(8,128)(2,1)S(1)}, u32[]{:S(2)}, u32[]{:S(2)}) %all-to-all-start.1) | async-done | bytes 262176 | tf_op jit(solution)/shard_map/all_to_all | solution.py:203
  54.1 5.1 %all-to-all-start = ((bf16[16,16,2048]{2,1,0:T(8,128)(2,1)}), bf16[16,16,2048]{2,1,0:T(8,128)(2,1)S(1)}, u32[]{:S(2)}, u32[]{:S(2)}) async-start(bf16[16,16,2048]{2,1,0:T(8,128)(2,1)} %bitcast.11), calls=%async_computation | async-start | bytes 2097152 | tf_op jit(solution)/shard_map/all_to_all | solution.py:208
  59.2 1.9 %collective-permute-start = (bf16[1,2048,384]{2,1,0:T(8,128)(2,1)S(1)}, bf16[1,2048,384]{2,1,0:T(8,128)(2,1)}, u32[]{:S(2)}, u32[]{:S(2)}) collective-permute-start(bf16[1,2048,384]{2,1,0:T(8,128)(2,1)S(1)} %copy-done.1), channel_id=1, source_target_pairs={{0,1},{1,0},{2,3},{3,2},{4,5},{5,4},{6,7},{7,6},{8,9},{9,8},{10,11... | collective-permute-start | bytes 4718600 | tf_op jit(solution)/shard_map/ppermute | solution.py:199
  61.1 2.4 %collective-permute-start.1 = (bf16[1,2048,384]{2,1,0:T(8,128)(2,1)}, bf16[1,2048,384]{2,1,0:T(8,128)(2,1)}, u32[]{:S(2)}, u32[]{:S(2)}) collective-permute-start(bf16[1,2048,384]{2,1,0:T(8,128)(2,1)} %u0_ref.1), channel_id=1, source_target_pairs={{0,1},{1,0},{2,3},{3,2},{4,5},{5,4},{6,7},{7,6},{8,9},{9,8},{10,11... | collective-permute-start | bytes 4718600 | tf_op jit(solution)/shard_map/ppermute | solution.py:199
  63.6 1.9 %collective-permute-start.2 = (bf16[1,384,2048]{2,1,0:T(8,128)(2,1)}, bf16[1,384,2048]{2,1,0:T(8,128)(2,1)}, u32[]{:S(2)}, u32[]{:S(2)}) collective-permute-start(bf16[1,384,2048]{2,1,0:T(8,128)(2,1)} %d0_ref.1), channel_id=1, source_target_pairs={{0,1},{1,0},{2,3},{3,2},{4,5},{5,4},{6,7},{7,6},{8,9},{9,8},{10,11... | collective-permute-start | bytes 4718600 | tf_op jit(solution)/shard_map/ppermute | solution.py:199
  65.5 16.7 %all-to-all-done = bf16[16,16,2048]{2,1,0:T(8,128)(2,1)S(1)} async-done(((bf16[16,16,2048]{2,1,0:T(8,128)(2,1)}), bf16[16,16,2048]{2,1,0:T(8,128)(2,1)S(1)}, u32[]{:S(2)}, u32[]{:S(2)}) %all-to-all-start) | async-done | bytes 1048608 | tf_op jit(solution)/shard_map/all_to_all | solution.py:208
  82.2 0.8 total_spread.1
  82.9 5.3 %all-to-all-start.3 = ((bf16[32,16,256]{2,1,0:T(8,128)(2,1)}), bf16[32,16,256]{2,1,0:T(8,128)(2,1)S(1)}, u32[]{:S(2)}, u32[]{:S(2)}) async-start(bf16[32,16,256]{2,1,0:T(8,128)(2,1)} %total_spread.1), calls=%async_computation.3 | async-start | bytes 524288 | tf_op jit(solution)/shard_map/all_to_all | solution.py:203
  88.3 1.4 copy-done.2
  89.7 1.4 copy-done.3
  91.1 6.8 %expert_rows.1 = bf16[256,2048]{1,0:T(8,128)(2,1)} custom-call(bf16[256,2048]{1,0:T(8,128)(2,1)S(1)} %bitcast.10, bf16[1,2048,384]{2,1,0:T(8,128)(2,1)S(1)} %copy-done.1, bf16[1,2048,384]{2,1,0:T(8,128)(2,1)S(1)} %copy-done.2, bf16[1,384,2048]{2,1,0:T(8,128)(2,1)S(1)} %copy-done.3, bf16[1,2048,384]{2,1,0:T(8,128)(2,1)} %collective-permute-done.g1_ref, ...), custom_call_target="tpu_custom_call" | custom-call | tf_op jit(solution)/shard_map/expert_rows/pallas_call | solution.py:81
  98.0 15.6 %all-to-all-done.3.totals_ref = bf16[32,16,256]{2,1,0:T(8,128)(2,1)S(1)} async-done(((bf16[32,16,256]{2,1,0:T(8,128)(2,1)}), bf16[32,16,256]{2,1,0:T(8,128)(2,1)S(1)}, u32[]{:S(2)}, u32[]{:S(2)}) %all-to-all-start.3) | async-done | bytes 262176 | tf_op jit(solution)/shard_map/all_to_all | solution.py:203
  113.5 6.5 %all-to-all-start.2 = ((bf16[16,16,2048]{2,1,0:T(8,128)(2,1)}), bf16[16,16,2048]{2,1,0:T(8,128)(2,1)S(1)}, u32[]{:S(2)}, u32[]{:S(2)}) async-start(bf16[16,16,2048]{2,1,0:T(8,128)(2,1)} %bitcast.6), calls=%async_computation.2 | async-start | bytes 2097152 | tf_op jit(solution)/shard_map/all_to_all | solution.py:208
  120.7 1.1 update.1
  121.8 21.7 %all-to-all-done.2 = bf16[16,16,2048]{2,1,0:T(8,128)(2,1)S(1)} async-done(((bf16[16,16,2048]{2,1,0:T(8,128)(2,1)}), bf16[16,16,2048]{2,1,0:T(8,128)(2,1)S(1)}, u32[]{:S(2)}, u32[]{:S(2)}) %all-to-all-start.2) | async-done | bytes 1048608 | tf_op jit(solution)/shard_map/all_to_all | solution.py:208
  143.5 1.1 combine_rows.1
  (18 shorter events, 0.6 us)
Async XLA Ops:
  0.6 1.0 copy-start.7
  1.6 0.7 copy-start.8
  3.4 55.8 %copy-start.1 = (bf16[1,2048,384]{2,1,0:T(8,128)(2,1)S(1)}, bf16[1,2048,384]{2,1,0:T(8,128)(2,1)}, u32[]{:S(2)}) copy-start(bf16[1,2048,384]{2,1,0:T(8,128)(2,1)} %g0_ref.1) | copy-start | bytes 4718596
  3.4 50.7 %all-to-all-start.1 = ((bf16[32,16,256]{2,1,0:T(8,128)(2,1)}), bf16[32,16,256]{2,1,0:T(8,128)(2,1)S(1)}, u32[]{:S(2)}, u32[]{:S(2)}) async-start(bf16[32,16,256]{2,1,0:T(8,128)(2,1)} %dequant.1), calls=%async_computation.1 | async-start | bytes 524288 | tf_op jit(solution)/shard_map/all_to_all | solution.py:203
  27.9 1.0 copy-start.6
  29.0 0.7 copy-start.9
  29.7 0.7 copy-start.10
  30.9 1.0 copy-start.4
  54.1 28.1 %all-to-all-start = ((bf16[16,16,2048]{2,1,0:T(8,128)(2,1)}), bf16[16,16,2048]{2,1,0:T(8,128)(2,1)S(1)}, u32[]{:S(2)}, u32[]{:S(2)}) async-start(bf16[16,16,2048]{2,1,0:T(8,128)(2,1)} %bitcast.11), calls=%async_computation | async-start | bytes 2097152 | tf_op jit(solution)/shard_map/all_to_all | solution.py:208
  59.2 29.1 %collective-permute-start = (bf16[1,2048,384]{2,1,0:T(8,128)(2,1)S(1)}, bf16[1,2048,384]{2,1,0:T(8,128)(2,1)}, u32[]{:S(2)}, u32[]{:S(2)}) collective-permute-start(bf16[1,2048,384]{2,1,0:T(8,128)(2,1)S(1)} %copy-done.1), channel_id=1, source_target_pairs={{0,1},{1,0},{2,3},{3,2},{4,5},{5,4},{6,7},{7,6},{8,9},{9,8},{10,11... | collective-permute-start | bytes 4718600 | tf_op jit(solution)/shard_map/ppermute | solution.py:199
  61.1 27.1 %collective-permute-start.1 = (bf16[1,2048,384]{2,1,0:T(8,128)(2,1)}, bf16[1,2048,384]{2,1,0:T(8,128)(2,1)}, u32[]{:S(2)}, u32[]{:S(2)}) collective-permute-start(bf16[1,2048,384]{2,1,0:T(8,128)(2,1)} %u0_ref.1), channel_id=1, source_target_pairs={{0,1},{1,0},{2,3},{3,2},{4,5},{5,4},{6,7},{7,6},{8,9},{9,8},{10,11... | collective-permute-start | bytes 4718600 | tf_op jit(solution)/shard_map/ppermute | solution.py:199
  63.6 24.7 %collective-permute-start.2 = (bf16[1,384,2048]{2,1,0:T(8,128)(2,1)}, bf16[1,384,2048]{2,1,0:T(8,128)(2,1)}, u32[]{:S(2)}, u32[]{:S(2)}) collective-permute-start(bf16[1,384,2048]{2,1,0:T(8,128)(2,1)} %d0_ref.1), channel_id=1, source_target_pairs={{0,1},{1,0},{2,3},{3,2},{4,5},{5,4},{6,7},{7,6},{8,9},{9,8},{10,11... | collective-permute-start | bytes 4718600 | tf_op jit(solution)/shard_map/ppermute | solution.py:199
  82.9 30.6 %all-to-all-start.3 = ((bf16[32,16,256]{2,1,0:T(8,128)(2,1)}), bf16[32,16,256]{2,1,0:T(8,128)(2,1)S(1)}, u32[]{:S(2)}, u32[]{:S(2)}) async-start(bf16[32,16,256]{2,1,0:T(8,128)(2,1)} %total_spread.1), calls=%async_computation.3 | async-start | bytes 524288 | tf_op jit(solution)/shard_map/all_to_all | solution.py:203
  88.3 1.4 copy-start.2
  89.7 1.4 copy-start.3
  98.0 22.7 %copy-start = (f32[3,64,2048]{2,1,0:T(8,128)S(1)}, f32[3,64,2048]{2,1,0:T(8,128)}, u32[]{:S(2)}) copy-start(f32[3,64,2048]{2,1,0:T(8,128)} %base_ref.1) | copy-start | bytes 4718596
  98.0 22.7 %copy-start.5 = (f32[64,2048]{1,0:T(8,128)S(1)}, f32[64,2048]{1,0:T(8,128)}, u32[]{:S(2)}) copy-start(f32[64,2048]{1,0:T(8,128)} %momentum_ref.1) | copy-start | bytes 1572868
  113.5 30.0 %all-to-all-start.2 = ((bf16[16,16,2048]{2,1,0:T(8,128)(2,1)}), bf16[16,16,2048]{2,1,0:T(8,128)(2,1)S(1)}, u32[]{:S(2)}, u32[]{:S(2)}) async-start(bf16[16,16,2048]{2,1,0:T(8,128)(2,1)} %bitcast.6), calls=%async_computation.2 | async-start | bytes 2097152 | tf_op jit(solution)/shard_map/all_to_all | solution.py:208

commit v4 on v2

--- a/solution.py
+++ b/solution.py
@@ -16,6 +16,7 @@
 
 PARAMS = pltpu.CompilerParams(vmem_limit_bytes=20 * 1024 * 1024)
 VMEM = pl.BlockSpec(memory_space=pltpu.VMEM)
+HBM = pl.BlockSpec(memory_space=pltpu.HBM)
 SMEM = pl.BlockSpec(memory_space=pltpu.SMEM)
 
 
@@ -65,22 +66,39 @@
     )(expert_ids.T, route_weights.T, tokens)
 
 
-def expert_kernel(rows_ref, g0_ref, u0_ref, d0_ref, g1_ref, u1_ref, d1_ref, out_ref):
+def expert_kernel(rows_ref, gate_ref, up_ref, down_ref, *refs):
+    sources, out_ref, targets, sems = refs[:3], refs[3], refs[4:7], refs[7]
+    fetches = [
+        pltpu.make_async_copy(source, target, sems.at[i])
+        for i, (source, target) in enumerate(zip(sources, targets))
+    ]
+    for fetch in fetches:
+        fetch.start()
     rows = rows_ref[...]
-    total = None
-    for gate_ref, up_ref, down_ref in ((g0_ref, u0_ref, d0_ref), (g1_ref, u1_ref, d1_ref)):
+
+    def part(gate_ref, up_ref, down_ref, waits):
+        for wait in waits[:1]:
+            wait.wait()
         gate = jnp.dot(rows, gate_ref[0], preferred_element_type=jnp.float32)
+        for wait in waits[1:2]:
+            wait.wait()
         up = jnp.dot(rows, up_ref[0], preferred_element_type=jnp.float32)
         hidden = (gate / (1.0 + jnp.exp(-gate)) * up).astype(jnp.bfloat16)
-        part = jnp.dot(hidden, down_ref[0], preferred_element_type=jnp.float32)
-        total = part if total is None else total + part
+        for wait in waits[2:]:
+            wait.wait()
+        return jnp.dot(hidden, down_ref[0], preferred_element_type=jnp.float32)
+
+    total = part(gate_ref, up_ref, down_ref, []) + part(*targets, fetches)
     out_ref[...] = total.astype(jnp.bfloat16)
 
 
 def expert_rows(rows, own, other):
     return pl.pallas_call(
         expert_kernel,
+        in_specs=[VMEM] * 4 + [HBM] * 3,
         out_shape=jax.ShapeDtypeStruct(rows.shape, jnp.bfloat16),
+        scratch_shapes=[pltpu.VMEM(x.shape, x.dtype) for x in other]
+        + [pltpu.SemaphoreType.DMA((3,))],
         compiler_params=PARAMS,
         name="expert_rows",
     )(rows, *own, *other)
@@ -266,16 +284,8 @@
     return lax.axis_index(axis).astype(jnp.int32).reshape(1)
 
 
-def replica_sum(pseudo_values, block_scales):
-    near, far = place_on("z_near"), place_on("z_far")
-    parts = scatter_stage(dequant(near, pseudo_values, block_scales), "z_near")
-    parts = scatter_stage(add_split(far, parts), "z_far")
-    return add_parts(parts)
-
-
 def outer_step(part, outer_params, momentum, fragment):
     near, far = place_on("z_near"), place_on("z_far")
-    part = add_parts([part, shift(part, "y_far", 1)])
     part = join(far, gather_stage(part, "z_far"))
     parts = gather_stage(part, "z_near")
     replicas = lax.axis_size(("y_far", "z_far", "z_near"))
@@ -306,10 +316,16 @@
     buffer, combine = route(tokens, expert_ids, route_weights, experts)
     mine = exchange(buffer, experts)
     own = (w_gate, w_up, w_down)
+    near, far = place_on("z_near"), place_on("z_far")
+    parts = scatter_stage(dequant(near, pseudo_values, block_scales), "z_near")
+    parts = scatter_stage(add_split(far, parts), "z_far")
     other = [shift(w, "core", 1) for w in own]
-    part = replica_sum(pseudo_values, block_scales)
+    part = add_parts(parts)
     mine, part = lax.optimization_barrier((mine, part))
-    returned = exchange(expert_rows(mine, own, other), experts)
+    rows = expert_rows(mine, own, other)
+    rows, apart = lax.optimization_barrier((rows, shift(part, "y_far", 1)))
+    part = add_parts([part, apart])
+    returned = exchange(rows, experts)
     moe_out = combine_rows(combine, returned)
     new_params, new_momentum = outer_step(part, outer_params, momentum, fragment)
     return (moe_out, new_params, new_momentum)

time: 143 us -> 128 us (0.90)
  waiting for transfers between devices: 37.1 us -> 24.2 us
  Pallas kernels: 10.7 us -> 9.2 us
    ppermute x16, waiting for transfers between devices: 37.1 us -> 24.2 us  [shift(): lax.ppermute(part, axis, [(i, (i + step) % size) for i in range(size)])]
    pallas_call x1, Pallas kernels: 6.86 us -> 5.39 us  [expert_rows(): pl.pallas_call(expert_kernel, in_specs=[VMEM] * 4 + [HBM] * 3, out_shape=...]
  transfers between devices with their start and end apart: 18 -> 18, of which waited for: 9 -> 8; matrix products, arithmetic and copies ran while one was open for 0% -> 0% of each run, Pallas kernels for 1% -> 6%
where the time goes in v4:
time: 128 us; the launch traced here: 127 us
  starting transfers between devices  85.5 us (67%)
  waiting for transfers between devices  24.2 us (19%)
  Pallas kernels  9.2 us (7%)
  local copies, waits for them, and re-layouts  6.36 us (5%)
  between operations  1.6 us (1%)
    ppermute x16, starting transfers between devices, shift(): lax.ppermute(part, axis, [(i, (i + step) % size) for i in range(size)])  61.2 us
    all_to_all x2, starting transfers between devices, exchange(): lax.all_to_all(rows.reshape(experts, CAP, width), 'chip', split_axis=0, c...  24.3 us
    ppermute x16, waiting for transfers between devices, shift(): lax.ppermute(part, axis, [(i, (i + step) % size) for i in range(size)])  24.2 us
    unnamed x22, local copies, waits for them, and re-layouts  6.36 us
    pallas_call x1, Pallas kernels, expert_rows(): pl.pallas_call(expert_kernel, in_specs=[VMEM] * 4 + [HBM] * 3, out_shape=...  5.39 us
  transfers between devices with their start and end apart: 18, of which 8 were waited for; matrix products, arithmetic and copies ran while one was open for 0% of the time, Pallas kernels for 6%

profile of v4, /device:TPU:6, one launch (start us, length us, event | category | flops | bytes accessed | tf_op | source)
XLA Modules:
  0.0 126.9 jit_solution(4252894457067336179)
XLA Ops:
  4.7 16.6 %all-to-all-start = ((bf16[16,16,2048]{2,1,0:T(8,128)(2,1)}), bf16[16,16,2048]{2,1,0:T(8,128)(2,1)S(1)}, u32[]{:S(2)}, u32[]{:S(2)}) async-start(bf16[16,16,2048]{2,1,0:T(8,128)(2,1)} %bitcast.13), calls=%async_computation | async-start | bytes 2097152 | tf_op jit(solution)/shard_map/all_to_all | solution.py:297
  21.4 1.9 %collective-permute-start.6 = (bf16[1,2048,384]{2,1,0:T(8,128)(2,1)S(1)}, bf16[1,2048,384]{2,1,0:T(8,128)(2,1)}, u32[]{:S(2)}, u32[]{:S(2)}) collective-permute-start(bf16[1,2048,384]{2,1,0:T(8,128)(2,1)S(1)} %copy-done.1), channel_id=1, source_target_pairs={{0,1},{1,0},{2,3},{3,2},{4,5},{5,4},{6,7},{7,6},{8,9},{9,8},{10,11... | collective-permute-start | bytes 4718600 | tf_op jit(solution)/shard_map/ppermute | solution.py:272
  23.3 2.4 %collective-permute-start.7 = (bf16[1,2048,384]{2,1,0:T(8,128)(2,1)}, bf16[1,2048,384]{2,1,0:T(8,128)(2,1)}, u32[]{:S(2)}, u32[]{:S(2)}) collective-permute-start(bf16[1,2048,384]{2,1,0:T(8,128)(2,1)} %up_ref.1), channel_id=1, source_target_pairs={{0,1},{1,0},{2,3},{3,2},{4,5},{5,4},{6,7},{7,6},{8,9},{9,8},{10,11... | collective-permute-start | bytes 4718600 | tf_op jit(solution)/shard_map/ppermute | solution.py:272
  25.7 1.9 %collective-permute-start.8 = (bf16[1,384,2048]{2,1,0:T(8,128)(2,1)}, bf16[1,384,2048]{2,1,0:T(8,128)(2,1)}, u32[]{:S(2)}, u32[]{:S(2)}) collective-permute-start(bf16[1,384,2048]{2,1,0:T(8,128)(2,1)} %down_ref.1), channel_id=1, source_target_pairs={{0,1},{1,0},{2,3},{3,2},{4,5},{5,4},{6,7},{7,6},{8,9},{9,8},{10,11... | collective-permute-start | bytes 4718600 | tf_op jit(solution)/shard_map/ppermute | solution.py:272
  28.3 1.9 %collective-permute-start = (bf16[16,2048]{1,0:T(8,128)(2,1)S(1)}, bf16[16,2048]{1,0:T(8,128)(2,1)S(1)}, u32[]{:S(2)}, u32[]{:S(2)}) collective-permute-start(bf16[16,2048]{1,0:T(8,128)(2,1)S(1)} %get-tuple-element.22), channel_id=1, source_target_pairs={{0,32},{32,64},{64,96},{96,0},{1,33},{33,65},{65,97},{97,1},{2,34}... | collective-permute-start | bytes 196616 | tf_op jit(solution)/shard_map/ppermute | solution.py:272
  30.2 1.9 %collective-permute-start.1 = (bf16[16,2048]{1,0:T(8,128)(2,1)S(1)}, bf16[16,2048]{1,0:T(8,128)(2,1)S(1)}, u32[]{:S(2)}, u32[]{:S(2)}) collective-permute-start(bf16[16,2048]{1,0:T(8,128)(2,1)S(1)} %get-tuple-element.23), channel_id=1, source_target_pairs={{0,64},{32,96},{64,0},{96,32},{1,65},{33,97},{65,1},{97,33},{2,66}... | collective-permute-start | bytes 196616 | tf_op jit(solution)/shard_map/ppermute | solution.py:272
  32.2 4.4 %collective-permute-done.refs_1_ = bf16[16,2048]{1,0:T(8,128)(2,1)S(1)} collective-permute-done((bf16[16,2048]{1,0:T(8,128)(2,1)S(1)}, bf16[16,2048]{1,0:T(8,128)(2,1)S(1)}, u32[]{:S(2)}, u32[]{:S(2)}) %collective-permute-start) | collective-permute-done | bytes 65568 | tf_op jit(solution)/shard_map/ppermute | solution.py:272
  36.5 1.9 %collective-permute-start.2 = (bf16[16,2048]{1,0:T(8,128)(2,1)S(1)}, bf16[16,2048]{1,0:T(8,128)(2,1)S(1)}, u32[]{:S(2)}, u32[]{:S(2)}) collective-permute-start(bf16[16,2048]{1,0:T(8,128)(2,1)S(1)} %get-tuple-element.24), channel_id=1, source_target_pairs={{0,96},{32,0},{64,32},{96,64},{1,97},{33,1},{65,33},{97,65},{2,98}... | collective-permute-start | bytes 196616 | tf_op jit(solution)/shard_map/ppermute | solution.py:272
  39.3 3.4 %collective-permute-done.2.refs_3_ = bf16[16,2048]{1,0:T(8,128)(2,1)S(1)} collective-permute-done((bf16[16,2048]{1,0:T(8,128)(2,1)S(1)}, bf16[16,2048]{1,0:T(8,128)(2,1)S(1)}, u32[]{:S(2)}, u32[]{:S(2)}) %collective-permute-start.2) | collective-permute-done | bytes 65568 | tf_op jit(solution)/shard_map/ppermute | solution.py:272
  42.9 4.5 %collective-permute-start.3 = (bf16[16,512]{1,0:T(8,128)(2,1)S(1)}, bf16[16,512]{1,0:T(8,128)(2,1)S(1)}, u32[]{:S(2)}, u32[]{:S(2)}) collective-permute-start(bf16[16,512]{1,0:T(8,128)(2,1)S(1)} %get-tuple-element.26), channel_id=1, source_target_pairs={{0,128},{128,256},{256,384},{384,0},{1,129},{129,257},{257,385},{3... | collective-permute-start | bytes 49160 | tf_op jit(solution)/shard_map/ppermute | solution.py:272
  47.4 12.1 %collective-permute-start.4 = (bf16[16,512]{1,0:T(8,128)(2,1)S(1)}, bf16[16,512]{1,0:T(8,128)(2,1)S(1)}, u32[]{:S(2)}, u32[]{:S(2)}) collective-permute-start(bf16[16,512]{1,0:T(8,128)(2,1)S(1)} %get-tuple-element.27), channel_id=1, source_target_pairs={{0,256},{128,384},{256,0},{384,128},{1,257},{129,385},{257,1},{385... | collective-permute-start | bytes 49160 | tf_op jit(solution)/shard_map/ppermute | solution.py:272
  59.5 3.6 %collective-permute-start.5 = (bf16[16,512]{1,0:T(8,128)(2,1)S(1)}, bf16[16,512]{1,0:T(8,128)(2,1)S(1)}, u32[]{:S(2)}, u32[]{:S(2)}) collective-permute-start(bf16[16,512]{1,0:T(8,128)(2,1)S(1)} %get-tuple-element.28), channel_id=1, source_target_pairs={{0,384},{128,0},{256,128},{384,256},{1,385},{129,1},{257,129},{385... | collective-permute-start | bytes 49160 | tf_op jit(solution)/shard_map/ppermute | solution.py:272
  63.2 6.1 %collective-permute-done.5.refs_3_ = bf16[16,512]{1,0:T(8,128)(2,1)S(1)} collective-permute-done((bf16[16,512]{1,0:T(8,128)(2,1)S(1)}, bf16[16,512]{1,0:T(8,128)(2,1)S(1)}, u32[]{:S(2)}, u32[]{:S(2)}) %collective-permute-start.5) | collective-permute-done | bytes 16416 | tf_op jit(solution)/shard_map/ppermute | solution.py:272
  69.3 5.0 %collective-permute-start.9 = (bf16[16,512]{1,0:T(8,128)(2,1)S(1)}, bf16[16,512]{1,0:T(8,128)(2,1)S(1)}, u32[]{:S(2)}, u32[]{:S(2)}) collective-permute-start(bf16[16,512]{1,0:T(8,128)(2,1)S(1)} %add_parts.2.refs_0_), channel_id=1, source_target_pairs={{0,512},{512,0},{1,513},{513,1},{2,514},{514,2},{3,515},{515,3},{4... | collective-permute-start | bytes 49160 | tf_op jit(solution)/shard_map/ppermute | solution.py:272
  77.2 5.4 %expert_rows.1 = bf16[256,2048]{1,0:T(8,128)(2,1)} custom-call(bf16[256,2048]{1,0:T(8,128)(2,1)S(1)} %bitcast.12, bf16[1,2048,384]{2,1,0:T(8,128)(2,1)S(1)} %copy-done.1, bf16[1,2048,384]{2,1,0:T(8,128)(2,1)S(1)} %copy-done.2, bf16[1,384,2048]{2,1,0:T(8,128)(2,1)S(1)} %copy-done.3, bf16[1,2048,384]{2,1,0:T(8,128)(2,1)} %collective-permute-done.6.refs_0_, ...), custom_call_target="tpu_custom_call" | custom-call | tf_op jit(solution)/shard_map/expert_rows/pallas_call | solution.py:96
  82.7 7.6 %all-to-all-start.1 = ((bf16[16,16,2048]{2,1,0:T(8,128)(2,1)}), bf16[16,16,2048]{2,1,0:T(8,128)(2,1)S(1)}, u32[]{:S(2)}, u32[]{:S(2)}) async-start(bf16[16,16,2048]{2,1,0:T(8,128)(2,1)} %bitcast.8), calls=%async_computation.1 | async-start | bytes 2097152 | tf_op jit(solution)/shard_map/all_to_all | solution.py:297
  90.3 1.9 %collective-permute-start.10 = (bf16[16,512]{1,0:T(8,128)(2,1)S(1)}, bf16[16,512]{1,0:T(8,128)(2,1)S(1)}, u32[]{:S(2)}, u32[]{:S(2)}) collective-permute-start(bf16[16,512]{1,0:T(8,128)(2,1)S(1)} %add_parts.3.refs_0_), channel_id=1, source_target_pairs={{0,128},{128,256},{256,384},{384,0},{1,129},{129,257},{257,385},{3... | collective-permute-start | bytes 49160 | tf_op jit(solution)/shard_map/ppermute | solution.py:272
  92.2 9.0 %collective-permute-start.11 = (bf16[16,512]{1,0:T(8,128)(2,1)S(1)}, bf16[16,512]{1,0:T(8,128)(2,1)S(1)}, u32[]{:S(2)}, u32[]{:S(2)}) collective-permute-start(bf16[16,512]{1,0:T(8,128)(2,1)S(1)} %add_parts.3.refs_0_), channel_id=1, source_target_pairs={{0,256},{128,384},{256,0},{384,128},{1,257},{129,385},{257,1},{385... | collective-permute-start | bytes 49160 | tf_op jit(solution)/shard_map/ppermute | solution.py:272
  101.2 3.4 %collective-permute-start.12 = (bf16[16,512]{1,0:T(8,128)(2,1)S(1)}, bf16[16,512]{1,0:T(8,128)(2,1)S(1)}, u32[]{:S(2)}, u32[]{:S(2)}) collective-permute-start(bf16[16,512]{1,0:T(8,128)(2,1)S(1)} %add_parts.3.refs_0_), channel_id=1, source_target_pairs={{0,384},{128,0},{256,128},{384,256},{1,385},{129,1},{257,129},{385... | collective-permute-start | bytes 49160 | tf_op jit(solution)/shard_map/ppermute | solution.py:272
  106.6 4.3 %collective-permute-done.12.refs_3_ = bf16[16,512]{1,0:T(8,128)(2,1)S(1)} collective-permute-done((bf16[16,512]{1,0:T(8,128)(2,1)S(1)}, bf16[16,512]{1,0:T(8,128)(2,1)S(1)}, u32[]{:S(2)}, u32[]{:S(2)}) %collective-permute-start.12) | collective-permute-done | bytes 16416 | tf_op jit(solution)/shard_map/ppermute | solution.py:272
  110.9 1.9 %collective-permute-start.13 = (bf16[16,2048]{1,0:T(8,128)(2,1)S(1)}, bf16[16,2048]{1,0:T(8,128)(2,1)S(1)}, u32[]{:S(2)}, u32[]{:S(2)}) collective-permute-start(bf16[16,2048]{1,0:T(8,128)(2,1)S(1)} %join.1.refs_0_), channel_id=1, source_target_pairs={{0,32},{32,64},{64,96},{96,0},{1,33},{33,65},{65,97},{97,1},{2,34}... | collective-permute-start | bytes 196616 | tf_op jit(solution)/shard_map/ppermute | solution.py:272
  112.8 5.4 %collective-permute-start.14 = (bf16[16,2048]{1,0:T(8,128)(2,1)S(1)}, bf16[16,2048]{1,0:T(8,128)(2,1)S(1)}, u32[]{:S(2)}, u32[]{:S(2)}) collective-permute-start(bf16[16,2048]{1,0:T(8,128)(2,1)S(1)} %join.1.refs_0_), channel_id=1, source_target_pairs={{0,64},{32,96},{64,0},{96,32},{1,65},{33,97},{65,1},{97,33},{2,66}... | collective-permute-start | bytes 196616 | tf_op jit(solution)/shard_map/ppermute | solution.py:272
  118.3 2.2 %collective-permute-start.15 = (bf16[16,2048]{1,0:T(8,128)(2,1)S(1)}, bf16[16,2048]{1,0:T(8,128)(2,1)S(1)}, u32[]{:S(2)}, u32[]{:S(2)}) collective-permute-start(bf16[16,2048]{1,0:T(8,128)(2,1)S(1)} %join.1.refs_0_), channel_id=1, source_target_pairs={{0,96},{32,0},{64,32},{96,64},{1,97},{33,1},{65,33},{97,65},{2,98}... | collective-permute-start | bytes 196616 | tf_op jit(solution)/shard_map/ppermute | solution.py:272
  121.2 3.2 %collective-permute-done.15.refs_3_ = bf16[16,2048]{1,0:T(8,128)(2,1)S(1)} collective-permute-done((bf16[16,2048]{1,0:T(8,128)(2,1)S(1)}, bf16[16,2048]{1,0:T(8,128)(2,1)S(1)}, u32[]{:S(2)}, u32[]{:S(2)}) %collective-permute-start.15) | collective-permute-done | bytes 65568 | tf_op jit(solution)/shard_map/ppermute | solution.py:272
  (43 shorter events, 13.0 us)
Async XLA Ops:
  0.6 20.8 %copy-start.1 = (bf16[1,2048,384]{2,1,0:T(8,128)(2,1)S(1)}, bf16[1,2048,384]{2,1,0:T(8,128)(2,1)}, u32[]{:S(2)}) copy-start(bf16[1,2048,384]{2,1,0:T(8,128)(2,1)} %gate_ref.1) | copy-start | bytes 4718596
  3.2 24.5 %copy-start.7 = (bf16[1,64,2048]{2,1,0:T(8,128)(2,1)S(1)}, bf16[1,64,2048]{2,1,0:T(8,128)(2,1)}, u32[]{:S(2)}) copy-start(bf16[1,64,2048]{2,1,0:T(8,128)(2,1)} %values_ref.1) | copy-start | bytes 786436
  3.2 24.5 %copy-start.8 = (f32[1,64,16]{1,2,0:T(8,128)S(1)}, f32[1,64,16]{1,2,0:T(8,128)}, u32[]{:S(2)}) copy-start(f32[1,64,16]{1,2,0:T(8,128)} %param.18) | copy-start | bytes 12292
  4.7 64.6 %all-to-all-start = ((bf16[16,16,2048]{2,1,0:T(8,128)(2,1)}), bf16[16,16,2048]{2,1,0:T(8,128)(2,1)S(1)}, u32[]{:S(2)}, u32[]{:S(2)}) async-start(bf16[16,16,2048]{2,1,0:T(8,128)(2,1)} %bitcast.13), calls=%async_computation | async-start | bytes 2097152 | tf_op jit(solution)/shard_map/all_to_all | solution.py:297
  21.4 53.0 %collective-permute-start.6 = (bf16[1,2048,384]{2,1,0:T(8,128)(2,1)S(1)}, bf16[1,2048,384]{2,1,0:T(8,128)(2,1)}, u32[]{:S(2)}, u32[]{:S(2)}) collective-permute-start(bf16[1,2048,384]{2,1,0:T(8,128)(2,1)S(1)} %copy-done.1), channel_id=1, source_target_pairs={{0,1},{1,0},{2,3},{3,2},{4,5},{5,4},{6,7},{7,6},{8,9},{9,8},{10,11... | collective-permute-start | bytes 4718600 | tf_op jit(solution)/shard_map/ppermute | solution.py:272
  23.3 51.1 %collective-permute-start.7 = (bf16[1,2048,384]{2,1,0:T(8,128)(2,1)}, bf16[1,2048,384]{2,1,0:T(8,128)(2,1)}, u32[]{:S(2)}, u32[]{:S(2)}) collective-permute-start(bf16[1,2048,384]{2,1,0:T(8,128)(2,1)} %up_ref.1), channel_id=1, source_target_pairs={{0,1},{1,0},{2,3},{3,2},{4,5},{5,4},{6,7},{7,6},{8,9},{9,8},{10,11... | collective-permute-start | bytes 4718600 | tf_op jit(solution)/shard_map/ppermute | solution.py:272
  25.7 48.7 %collective-permute-start.8 = (bf16[1,384,2048]{2,1,0:T(8,128)(2,1)}, bf16[1,384,2048]{2,1,0:T(8,128)(2,1)}, u32[]{:S(2)}, u32[]{:S(2)}) collective-permute-start(bf16[1,384,2048]{2,1,0:T(8,128)(2,1)} %down_ref.1), channel_id=1, source_target_pairs={{0,1},{1,0},{2,3},{3,2},{4,5},{5,4},{6,7},{7,6},{8,9},{9,8},{10,11... | collective-permute-start | bytes 4718600 | tf_op jit(solution)/shard_map/ppermute | solution.py:272
  28.3 8.2 %collective-permute-start = (bf16[16,2048]{1,0:T(8,128)(2,1)S(1)}, bf16[16,2048]{1,0:T(8,128)(2,1)S(1)}, u32[]{:S(2)}, u32[]{:S(2)}) collective-permute-start(bf16[16,2048]{1,0:T(8,128)(2,1)S(1)} %get-tuple-element.22), channel_id=1, source_target_pairs={{0,32},{32,64},{64,96},{96,0},{1,33},{33,65},{65,97},{97,1},{2,34}... | collective-permute-start | bytes 196616 | tf_op jit(solution)/shard_map/ppermute | solution.py:272
  30.2 9.1 %collective-permute-start.1 = (bf16[16,2048]{1,0:T(8,128)(2,1)S(1)}, bf16[16,2048]{1,0:T(8,128)(2,1)S(1)}, u32[]{:S(2)}, u32[]{:S(2)}) collective-permute-start(bf16[16,2048]{1,0:T(8,128)(2,1)S(1)} %get-tuple-element.23), channel_id=1, source_target_pairs={{0,64},{32,96},{64,0},{96,32},{1,65},{33,97},{65,1},{97,33},{2,66}... | collective-permute-start | bytes 196616 | tf_op jit(solution)/shard_map/ppermute | solution.py:272
  36.5 6.1 %collective-permute-start.2 = (bf16[16,2048]{1,0:T(8,128)(2,1)S(1)}, bf16[16,2048]{1,0:T(8,128)(2,1)S(1)}, u32[]{:S(2)}, u32[]{:S(2)}) collective-permute-start(bf16[16,2048]{1,0:T(8,128)(2,1)S(1)} %get-tuple-element.24), channel_id=1, source_target_pairs={{0,96},{32,0},{64,32},{96,64},{1,97},{33,1},{65,33},{97,65},{2,98}... | collective-permute-start | bytes 196616 | tf_op jit(solution)/shard_map/ppermute | solution.py:272
  42.9 16.6 %collective-permute-start.3 = (bf16[16,512]{1,0:T(8,128)(2,1)S(1)}, bf16[16,512]{1,0:T(8,128)(2,1)S(1)}, u32[]{:S(2)}, u32[]{:S(2)}) collective-permute-start(bf16[16,512]{1,0:T(8,128)(2,1)S(1)} %get-tuple-element.26), channel_id=1, source_target_pairs={{0,128},{128,256},{256,384},{384,0},{1,129},{129,257},{257,385},{3... | collective-permute-start | bytes 49160 | tf_op jit(solution)/shard_map/ppermute | solution.py:272
  47.4 15.8 %collective-permute-start.4 = (bf16[16,512]{1,0:T(8,128)(2,1)S(1)}, bf16[16,512]{1,0:T(8,128)(2,1)S(1)}, u32[]{:S(2)}, u32[]{:S(2)}) collective-permute-start(bf16[16,512]{1,0:T(8,128)(2,1)S(1)} %get-tuple-element.27), channel_id=1, source_target_pairs={{0,256},{128,384},{256,0},{384,128},{1,257},{129,385},{257,1},{385... | collective-permute-start | bytes 49160 | tf_op jit(solution)/shard_map/ppermute | solution.py:272
  59.5 9.8 %collective-permute-start.5 = (bf16[16,512]{1,0:T(8,128)(2,1)S(1)}, bf16[16,512]{1,0:T(8,128)(2,1)S(1)}, u32[]{:S(2)}, u32[]{:S(2)}) collective-permute-start(bf16[16,512]{1,0:T(8,128)(2,1)S(1)} %get-tuple-element.28), channel_id=1, source_target_pairs={{0,384},{128,0},{256,128},{384,256},{1,385},{129,1},{257,129},{385... | collective-permute-start | bytes 49160 | tf_op jit(solution)/shard_map/ppermute | solution.py:272
  69.3 13.3 %collective-permute-start.9 = (bf16[16,512]{1,0:T(8,128)(2,1)S(1)}, bf16[16,512]{1,0:T(8,128)(2,1)S(1)}, u32[]{:S(2)}, u32[]{:S(2)}) collective-permute-start(bf16[16,512]{1,0:T(8,128)(2,1)S(1)} %add_parts.2.refs_0_), channel_id=1, source_target_pairs={{0,512},{512,0},{1,513},{513,1},{2,514},{514,2},{3,515},{515,3},{4... | collective-permute-start | bytes 49160 | tf_op jit(solution)/shard_map/ppermute | solution.py:272
  74.4 1.4 %copy-start.2 = (bf16[1,2048,384]{2,1,0:T(8,128)(2,1)S(1)}, bf16[1,2048,384]{2,1,0:T(8,128)(2,1)}, u32[]{:S(2)}) copy-start(bf16[1,2048,384]{2,1,0:T(8,128)(2,1)} %up_ref.1) | copy-start | bytes 4718596
  82.6 41.8 %copy-start = (f32[3,64,2048]{2,1,0:T(8,128)S(1)}, f32[3,64,2048]{2,1,0:T(8,128)}, u32[]{:S(2)}) copy-start(f32[3,64,2048]{2,1,0:T(8,128)} %refs_4_.1) | copy-start | bytes 4718596
  82.6 41.8 %copy-start.6 = (f32[64,2048]{1,0:T(8,128)S(1)}, f32[64,2048]{1,0:T(8,128)}, u32[]{:S(2)}) copy-start(f32[64,2048]{1,0:T(8,128)} %refs_5_.1) | copy-start | bytes 1572868
  82.7 43.1 %all-to-all-start.1 = ((bf16[16,16,2048]{2,1,0:T(8,128)(2,1)}), bf16[16,16,2048]{2,1,0:T(8,128)(2,1)S(1)}, u32[]{:S(2)}, u32[]{:S(2)}) async-start(bf16[16,16,2048]{2,1,0:T(8,128)(2,1)} %bitcast.8), calls=%async_computation.1 | async-start | bytes 2097152 | tf_op jit(solution)/shard_map/all_to_all | solution.py:297
  90.3 14.4 %collective-permute-start.10 = (bf16[16,512]{1,0:T(8,128)(2,1)S(1)}, bf16[16,512]{1,0:T(8,128)(2,1)S(1)}, u32[]{:S(2)}, u32[]{:S(2)}) collective-permute-start(bf16[16,512]{1,0:T(8,128)(2,1)S(1)} %add_parts.3.refs_0_), channel_id=1, source_target_pairs={{0,128},{128,256},{256,384},{384,0},{1,129},{129,257},{257,385},{3... | collective-permute-start | bytes 49160 | tf_op jit(solution)/shard_map/ppermute | solution.py:272
  92.2 14.4 %collective-permute-start.11 = (bf16[16,512]{1,0:T(8,128)(2,1)S(1)}, bf16[16,512]{1,0:T(8,128)(2,1)S(1)}, u32[]{:S(2)}, u32[]{:S(2)}) collective-permute-start(bf16[16,512]{1,0:T(8,128)(2,1)S(1)} %add_parts.3.refs_0_), channel_id=1, source_target_pairs={{0,256},{128,384},{256,0},{384,128},{1,257},{129,385},{257,1},{385... | collective-permute-start | bytes 49160 | tf_op jit(solution)/shard_map/ppermute | solution.py:272
  101.2 9.7 %collective-permute-start.12 = (bf16[16,512]{1,0:T(8,128)(2,1)S(1)}, bf16[16,512]{1,0:T(8,128)(2,1)S(1)}, u32[]{:S(2)}, u32[]{:S(2)}) collective-permute-start(bf16[16,512]{1,0:T(8,128)(2,1)S(1)} %add_parts.3.refs_0_), channel_id=1, source_target_pairs={{0,384},{128,0},{256,128},{384,256},{1,385},{129,1},{257,129},{385... | collective-permute-start | bytes 49160 | tf_op jit(solution)/shard_map/ppermute | solution.py:272
  110.9 10.2 %collective-permute-start.13 = (bf16[16,2048]{1,0:T(8,128)(2,1)S(1)}, bf16[16,2048]{1,0:T(8,128)(2,1)S(1)}, u32[]{:S(2)}, u32[]{:S(2)}) collective-permute-start(bf16[16,2048]{1,0:T(8,128)(2,1)S(1)} %join.1.refs_0_), channel_id=1, source_target_pairs={{0,32},{32,64},{64,96},{96,0},{1,33},{33,65},{65,97},{97,1},{2,34}... | collective-permute-start | bytes 196616 | tf_op jit(solution)/shard_map/ppermute | solution.py:272
  112.8 8.4 %collective-permute-start.14 = (bf16[16,2048]{1,0:T(8,128)(2,1)S(1)}, bf16[16,2048]{1,0:T(8,128)(2,1)S(1)}, u32[]{:S(2)}, u32[]{:S(2)}) collective-permute-start(bf16[16,2048]{1,0:T(8,128)(2,1)S(1)} %join.1.refs_0_), channel_id=1, source_target_pairs={{0,64},{32,96},{64,0},{96,32},{1,65},{33,97},{65,1},{97,33},{2,66}... | collective-permute-start | bytes 196616 | tf_op jit(solution)/shard_map/ppermute | solution.py:272
  118.3 6.2 %collective-permute-start.15 = (bf16[16,2048]{1,0:T(8,128)(2,1)S(1)}, bf16[16,2048]{1,0:T(8,128)(2,1)S(1)}, u32[]{:S(2)}, u32[]{:S(2)}) collective-permute-start(bf16[16,2048]{1,0:T(8,128)(2,1)S(1)} %join.1.refs_0_), channel_id=1, source_target_pairs={{0,96},{32,0},{64,32},{96,64},{1,97},{33,1},{65,33},{97,65},{2,98}... | collective-permute-start | bytes 196616 | tf_op jit(solution)/shard_map/ppermute | solution.py:272
  (5 other events, 4.9 us)

commit v5 on v4

--- a/solution.py
+++ b/solution.py
@@ -122,7 +122,7 @@
     )(combine, rows)
 
 
-def dequant_kernel(place_ref, values_ref, scales_ref, *out_refs):
+def dequant_kernel(z_ref, values_ref, scales_ref, *out_refs):
     rows, width = out_refs[0].shape
     blocks = scales_ref.shape[0]
     column = lax.broadcasted_iota(jnp.int32, (blocks, width), 1) // (width // blocks)
@@ -143,12 +143,12 @@
         block = whole[place * rows : (place + 1) * rows]
         for step, out_ref in enumerate(out_refs):
 
-            @pl.when((place_ref[0] + step) % RADIX == place)
+            @pl.when((z_ref[0] + step) % RADIX == place)
             def _():
                 out_ref[...] = block
 
 
-def dequant(place, values, scales):
+def dequant(z, values, scales):
     _, rows, width = values.shape
     part = jax.ShapeDtypeStruct((rows // RADIX, width), jnp.bfloat16)
     return pl.pallas_call(
@@ -157,22 +157,22 @@
         out_shape=(part,) * RADIX,
         compiler_params=PARAMS,
         name="dequant",
-    )(place, values, scales[0].T)
-
-
-def add_split_kernel(place_ref, *refs):
+    )(z, values, scales[0].T)
+
+
+def add_split_kernel(z_ref, *refs):
     in_refs, out_refs = refs[:RADIX], refs[RADIX:]
     total = sum(ref[...].astype(jnp.float32) for ref in in_refs).astype(jnp.bfloat16)
     width = out_refs[0].shape[1]
     for place in range(RADIX):
         for step, out_ref in enumerate(out_refs):
 
-            @pl.when((place_ref[0] + step) % RADIX == place)
+            @pl.when((z_ref[0] // RADIX + step) % RADIX == place)
             def _():
                 out_ref[...] = total[:, place * width : (place + 1) * width]
 
 
-def add_split(place, parts):
+def add_split(z, parts):
     rows, width = parts[0].shape
     part = jax.ShapeDtypeStruct((rows, width // RADIX), jnp.bfloat16)
     return pl.pallas_call(
@@ -181,7 +181,7 @@
         out_shape=(part,) * RADIX,
         compiler_params=PARAMS,
         name="add_split",
-    )(place, *parts)
+    )(z, *parts)
 
 
 def add_kernel(*refs):
@@ -197,63 +197,47 @@
     )(*parts)
 
 
-def join_kernel(place_ref, *refs):
-    in_refs, out_ref = refs[:RADIX], refs[RADIX]
-    width = in_refs[0].shape[1]
-    for place in range(RADIX):
-        for step, ref in enumerate(in_refs):
-
-            @pl.when((place_ref[0] + RADIX - step) % RADIX == place)
-            def _():
-                out_ref[:, place * width : (place + 1) * width] = ref[...]
-
-
-def join(place, parts):
-    rows, width = parts[0].shape
-    return pl.pallas_call(
-        join_kernel,
-        in_specs=[SMEM] + [VMEM] * RADIX,
-        out_shape=jax.ShapeDtypeStruct((rows, width * RADIX), jnp.bfloat16),
-        compiler_params=PARAMS,
-        name="join",
-    )(place, *parts)
-
-
-def update_kernel(replicas, fragment_ref, place_ref, *refs):
-    part_refs = refs[:RADIX]
-    base_ref, momentum_ref, params_out, momentum_out = refs[RADIX:]
-    rows = part_refs[0].shape[0]
-    for place in range(RADIX):
-        for step, ref in enumerate(part_refs):
-
-            @pl.when((place_ref[0] + RADIX - step) % RADIX == place)
-            def _():
-                span = pl.ds(place * rows, rows)
-                delta = ref[...].astype(jnp.float32) / replicas
-                new_momentum = momentum_rate * momentum_ref[span, :] + delta
-                momentum_out[span, :] = new_momentum
-                params_out[span, :] = base_ref[0, span, :] - outer_rate * (
-                    delta + momentum_rate * new_momentum
-                )
-
-
-def update(replicas, place, parts, outer_params, momentum, fragment):
+def total_kernel(one_ref, other_ref, out_ref):
+    total = (one_ref[...].astype(jnp.float32) + other_ref[...].astype(jnp.float32)).astype(
+        jnp.bfloat16
+    )
+    out_ref[...] = jnp.broadcast_to(total[None], out_ref.shape)
+
+
+def total_spread(one, other, copies):
+    return pl.pallas_call(
+        total_kernel,
+        out_shape=jax.ShapeDtypeStruct((copies,) + one.shape, jnp.bfloat16),
+        compiler_params=PARAMS,
+        name="total_spread",
+    )(one, other)
+
+
+def update_kernel(replicas, fragment_ref, totals_ref, base_ref, momentum_ref, params_out, momentum_out):
+    pieces, rows, span = totals_ref.shape
+    for piece in range(pieces):
+        far, near = piece // RADIX, piece % RADIX
+        at = (pl.ds(near * rows, rows), pl.ds(far * span, span))
+        delta = totals_ref[piece].astype(jnp.float32) / replicas
+        new_momentum = momentum_rate * momentum_ref[at] + delta
+        momentum_out[at] = new_momentum
+        params_out[at] = base_ref[(0,) + at] - outer_rate * (delta + momentum_rate * new_momentum)
+
+
+def update(replicas, totals, outer_params, momentum, fragment):
     shape = momentum.shape
-    part = parts[0].shape
 
     def whole(block):
-        return pl.BlockSpec(block, lambda i, fragment_ref, place_ref: (0,) * len(block))
+        return pl.BlockSpec(block, lambda i, fragment_ref: (0,) * len(block))
 
     return pl.pallas_call(
         functools.partial(update_kernel, replicas),
         grid_spec=pltpu.PrefetchScalarGridSpec(
-            num_scalar_prefetch=2,
+            num_scalar_prefetch=1,
             grid=(1,),
-            in_specs=[whole(part)] * RADIX
-            + [
-                pl.BlockSpec(
-                    (1,) + shape, lambda i, fragment_ref, place_ref: (fragment_ref[0], 0, 0)
-                ),
+            in_specs=[
+                whole(totals.shape),
+                pl.BlockSpec((1,) + shape, lambda i, fragment_ref: (fragment_ref[0], 0, 0)),
                 whole(shape),
             ],
             out_specs=(whole(shape), whole(shape)),
@@ -264,7 +248,7 @@
         ),
         compiler_params=PARAMS,
         name="update",
-    )(fragment, place, *parts, outer_params, momentum)
+    )(fragment, totals, outer_params, momentum)
 
 
 def shift(part, axis, step):
@@ -272,24 +256,23 @@
     return lax.ppermute(part, axis, [(i, (i + step) % size) for i in range(size)])
 
 
-def scatter_stage(parts, axis):
-    return [parts[0]] + [shift(parts[step], axis, step) for step in range(1, RADIX)]
-
-
-def gather_stage(part, axis):
-    return [part] + [shift(part, axis, step) for step in range(1, RADIX)]
-
-
-def place_on(axis):
-    return lax.axis_index(axis).astype(jnp.int32).reshape(1)
-
-
-def outer_step(part, outer_params, momentum, fragment):
-    near, far = place_on("z_near"), place_on("z_far")
-    part = join(far, gather_stage(part, "z_far"))
-    parts = gather_stage(part, "z_near")
-    replicas = lax.axis_size(("y_far", "z_far", "z_near"))
-    return update(replicas, near, parts, outer_params, momentum, fragment)
+def near_shift(part, step):
+    def target(i):
+        return i // RADIX * RADIX + (i + step) % RADIX
+
+    return lax.ppermute(part, "z", [(i, target(i)) for i in range(lax.axis_size("z"))])
+
+
+def far_shift(part, step):
+    return shift(part, "z", RADIX * step)
+
+
+def scatter_stage(parts, move):
+    return [parts[0]] + [move(parts[step], step) for step in range(1, RADIX)]
+
+
+def gather_z(parts):
+    return lax.all_to_all(parts, "z", split_axis=0, concat_axis=0, tiled=True)
 
 
 def exchange(rows, experts):
@@ -316,28 +299,31 @@
     buffer, combine = route(tokens, expert_ids, route_weights, experts)
     mine = exchange(buffer, experts)
     own = (w_gate, w_up, w_down)
-    near, far = place_on("z_near"), place_on("z_far")
-    parts = scatter_stage(dequant(near, pseudo_values, block_scales), "z_near")
-    parts = scatter_stage(add_split(far, parts), "z_far")
+    z = lax.axis_index("z").astype(jnp.int32).reshape(1)
+    parts = scatter_stage(dequant(z, pseudo_values, block_scales), near_shift)
+    parts = add_split(z, parts)
     other = [shift(w, "core", 1) for w in own]
-    part = add_parts(parts)
-    mine, part = lax.optimization_barrier((mine, part))
+    mine, parts = lax.optimization_barrier((mine, parts))
     rows = expert_rows(mine, own, other)
-    rows, apart = lax.optimization_barrier((rows, shift(part, "y_far", 1)))
-    part = add_parts([part, apart])
+    rows, parts = lax.optimization_barrier((rows, parts))
     returned = exchange(rows, experts)
+    part = add_parts(scatter_stage(parts, far_shift))
+    returned, part = lax.optimization_barrier((returned, part))
+    spread = total_spread(part, shift(part, "y_far", 1), lax.axis_size("z"))
     moe_out = combine_rows(combine, returned)
-    new_params, new_momentum = outer_step(part, outer_params, momentum, fragment)
+    new_params, new_momentum = update(
+        lax.axis_size(("y_far", "z")), gather_z(spread), outer_params, momentum, fragment
+    )
     return (moe_out, new_params, new_momentum)
 
 
 def solution(mesh):
     reps, exps = mesh.devices.shape
     fine = Mesh(
-        mesh.devices.reshape(reps // (RADIX * RADIX), RADIX, RADIX, exps // 2, 2),
-        ("y_far", "z_far", "z_near", "chip", "core"),
-    )
-    rep = ("y_far", "z_far", "z_near")
+        mesh.devices.reshape(reps // (RADIX * RADIX), RADIX * RADIX, exps // 2, 2),
+        ("y_far", "z", "chip", "core"),
+    )
+    rep = ("y_far", "z")
     exp = ("chip", "core")
     return jax.shard_map(
         shards,

time: 128 us -> 127 us (level)
  the two profiles are of different devices: /device:TPU:6 before, /device:TPU:64 now
where the time goes in v5:
time: 127 us; the launch traced here: 126 us
  starting transfers between devices  80.9 us (64%)
  waiting for transfers between devices  27.4 us (22%)
  Pallas kernels  9.8 us (8%)
  local copies, waits for them, and re-layouts  6.36 us (5%)
  between operations  1.57 us (1%)
    ppermute x7, starting transfers between devices, shift(): lax.ppermute(part, axis, [(i, (i + step) % size) for i in range(size)])  35.5 us
    ppermute x3, starting transfers between devices, near_shift(): lax.ppermute(part, 'z', [(i, target(i)) for i in range(lax.axis_size('z'))])  18.6 us
    all_to_all x2, starting transfers between devices, exchange(): lax.all_to_all(rows.reshape(experts, CAP, width), 'chip', split_axis=0, c...  14.9 us
    all_to_all x1, waiting for transfers between devices, gather_z(): return lax.all_to_all(parts, 'z', split_axis=0, concat_axis=0, tiled=True)  14.8 us
    all_to_all x1, starting transfers between devices, gather_z(): return lax.all_to_all(parts, 'z', split_axis=0, concat_axis=0, tiled=True)  11.8 us
    ppermute x7, waiting for transfers between devices, shift(): lax.ppermute(part, axis, [(i, (i + step) % size) for i in range(size)])  10.4 us
    unnamed x22, local copies, waits for them, and re-layouts  6.36 us
    pallas_call x1, Pallas kernels, expert_rows(): pl.pallas_call(expert_kernel, in_specs=[VMEM] * 4 + [HBM] * 3, out_shape=...  5.39 us
  transfers between devices with their start and end apart: 13, of which 4 were waited for; matrix products, arithmetic and copies ran while one was open for 0% of the time, Pallas kernels for 2%

profile of v5, /device:TPU:64, one launch (start us, length us, event | category | flops | bytes accessed | tf_op | source)
XLA Modules:
  0.0 126.0 jit_solution(135667794289778633)
XLA Ops:
  0.7 1.2 copy-done.6
  3.8 1.0 copy-done.4
  4.7 7.4 %all-to-all-start = ((bf16[16,16,2048]{2,1,0:T(8,128)(2,1)}), bf16[16,16,2048]{2,1,0:T(8,128)(2,1)S(1)}, u32[]{:S(2)}, u32[]{:S(2)}) async-start(bf16[16,16,2048]{2,1,0:T(8,128)(2,1)} %bitcast.12), calls=%async_computation | async-start | bytes 2097152 | tf_op jit(solution)/shard_map/all_to_all | solution.py:280
  12.2 1.9 %collective-permute-start.3 = (bf16[1,2048,384]{2,1,0:T(8,128)(2,1)S(1)}, bf16[1,2048,384]{2,1,0:T(8,128)(2,1)}, u32[]{:S(2)}, u32[]{:S(2)}) collective-permute-start(bf16[1,2048,384]{2,1,0:T(8,128)(2,1)S(1)} %copy-done.1), channel_id=1, source_target_pairs={{0,1},{1,0},{2,3},{3,2},{4,5},{5,4},{6,7},{7,6},{8,9},{9,8},{10,11... | collective-permute-start | bytes 4718600 | tf_op jit(solution)/shard_map/ppermute | solution.py:256
  14.1 2.4 %collective-permute-start.4 = (bf16[1,2048,384]{2,1,0:T(8,128)(2,1)}, bf16[1,2048,384]{2,1,0:T(8,128)(2,1)}, u32[]{:S(2)}, u32[]{:S(2)}) collective-permute-start(bf16[1,2048,384]{2,1,0:T(8,128)(2,1)} %up_ref.1), channel_id=1, source_target_pairs={{0,1},{1,0},{2,3},{3,2},{4,5},{5,4},{6,7},{7,6},{8,9},{9,8},{10,11... | collective-permute-start | bytes 4718600 | tf_op jit(solution)/shard_map/ppermute | solution.py:256
  16.6 1.9 %collective-permute-start.5 = (bf16[1,384,2048]{2,1,0:T(8,128)(2,1)}, bf16[1,384,2048]{2,1,0:T(8,128)(2,1)}, u32[]{:S(2)}, u32[]{:S(2)}) collective-permute-start(bf16[1,384,2048]{2,1,0:T(8,128)(2,1)} %down_ref.1), channel_id=1, source_target_pairs={{0,1},{1,0},{2,3},{3,2},{4,5},{5,4},{6,7},{7,6},{8,9},{9,8},{10,11... | collective-permute-start | bytes 4718600 | tf_op jit(solution)/shard_map/ppermute | solution.py:256
  19.1 4.3 %collective-permute-start = (bf16[16,2048]{1,0:T(8,128)(2,1)S(1)}, bf16[16,2048]{1,0:T(8,128)(2,1)S(1)}, u32[]{:S(2)}, u32[]{:S(2)}) collective-permute-start(bf16[16,2048]{1,0:T(8,128)(2,1)S(1)} %get-tuple-element.30), channel_id=1, source_target_pairs={{0,32},{32,64},{64,96},{96,0},{128,160},{160,192},{192,224},{224,1... | collective-permute-start | bytes 196616 | tf_op jit(solution)/shard_map/ppermute | solution.py:263
  23.4 10.4 %collective-permute-start.1 = (bf16[16,2048]{1,0:T(8,128)(2,1)S(1)}, bf16[16,2048]{1,0:T(8,128)(2,1)S(1)}, u32[]{:S(2)}, u32[]{:S(2)}) collective-permute-start(bf16[16,2048]{1,0:T(8,128)(2,1)S(1)} %get-tuple-element.31), channel_id=1, source_target_pairs={{0,64},{32,96},{64,0},{96,32},{128,192},{160,224},{192,128},{224,1... | collective-permute-start | bytes 196616 | tf_op jit(solution)/shard_map/ppermute | solution.py:263
  33.8 3.9 %collective-permute-start.2 = (bf16[16,2048]{1,0:T(8,128)(2,1)S(1)}, bf16[16,2048]{1,0:T(8,128)(2,1)S(1)}, u32[]{:S(2)}, u32[]{:S(2)}) collective-permute-start(bf16[16,2048]{1,0:T(8,128)(2,1)S(1)} %get-tuple-element.32), channel_id=1, source_target_pairs={{0,96},{32,0},{64,32},{96,64},{128,224},{160,128},{192,160},{224,1... | collective-permute-start | bytes 196616 | tf_op jit(solution)/shard_map/ppermute | solution.py:263
  37.8 2.2 %collective-permute-done.2.refs_3_ = bf16[16,2048]{1,0:T(8,128)(2,1)S(1)} collective-permute-done((bf16[16,2048]{1,0:T(8,128)(2,1)S(1)}, bf16[16,2048]{1,0:T(8,128)(2,1)S(1)}, u32[]{:S(2)}, u32[]{:S(2)}) %collective-permute-start.2) | collective-permute-done | bytes 65568 | tf_op jit(solution)/shard_map/ppermute | solution.py:263
  40.4 1.4 %copy-done.2 = bf16[1,2048,384]{2,1,0:T(8,128)(2,1)S(1)} copy-done((bf16[1,2048,384]{2,1,0:T(8,128)(2,1)S(1)}, bf16[1,2048,384]{2,1,0:T(8,128)(2,1)}, u32[]{:S(2)}) %copy-start.2) | copy-done | bytes 1572888
  41.8 1.4 %copy-done.3 = bf16[1,384,2048]{2,1,0:T(8,128)(2,1)S(1)} copy-done((bf16[1,384,2048]{2,1,0:T(8,128)(2,1)S(1)}, bf16[1,384,2048]{2,1,0:T(8,128)(2,1)}, u32[]{:S(2)}) %copy-start.3) | copy-done | bytes 1572888
  43.2 5.4 %expert_rows.1 = bf16[256,2048]{1,0:T(8,128)(2,1)} custom-call(bf16[256,2048]{1,0:T(8,128)(2,1)S(1)} %bitcast.11, bf16[1,2048,384]{2,1,0:T(8,128)(2,1)S(1)} %copy-done.1, bf16[1,2048,384]{2,1,0:T(8,128)(2,1)S(1)} %copy-done.2, bf16[1,384,2048]{2,1,0:T(8,128)(2,1)S(1)} %copy-done.3, bf16[1,2048,384]{2,1,0:T(8,128)(2,1)} %collective-permute-done.3.refs_0_, ...), custom_call_target="tpu_custom_call" | custom-call | tf_op jit(solution)/shard_map/expert_rows/pallas_call | solution.py:96
  48.6 7.5 %all-to-all-start.1 = ((bf16[16,16,2048]{2,1,0:T(8,128)(2,1)}), bf16[16,16,2048]{2,1,0:T(8,128)(2,1)S(1)}, u32[]{:S(2)}, u32[]{:S(2)}) async-start(bf16[16,16,2048]{2,1,0:T(8,128)(2,1)} %bitcast.7), calls=%async_computation.1 | async-start | bytes 2097152 | tf_op jit(solution)/shard_map/all_to_all | solution.py:280
  56.0 6.9 %collective-permute-start.6 = (bf16[16,512]{1,0:T(8,128)(2,1)S(1)}, bf16[16,512]{1,0:T(8,128)(2,1)S(1)}, u32[]{:S(2)}, u32[]{:S(2)}) collective-permute-start(bf16[16,512]{1,0:T(8,128)(2,1)S(1)} %get-tuple-element.44), channel_id=1, source_target_pairs={{0,128},{32,160},{64,192},{96,224},{128,256},{160,288},{192,320},{... | collective-permute-start | bytes 49160 | tf_op jit(solution)/shard_map/ppermute | solution.py:256
  63.0 13.7 %collective-permute-start.7 = (bf16[16,512]{1,0:T(8,128)(2,1)S(1)}, bf16[16,512]{1,0:T(8,128)(2,1)S(1)}, u32[]{:S(2)}, u32[]{:S(2)}) collective-permute-start(bf16[16,512]{1,0:T(8,128)(2,1)S(1)} %get-tuple-element.45), channel_id=1, source_target_pairs={{0,256},{32,288},{64,320},{96,352},{128,384},{160,416},{192,448},{... | collective-permute-start | bytes 49160 | tf_op jit(solution)/shard_map/ppermute | solution.py:256
  76.6 3.6 %collective-permute-start.8 = (bf16[16,512]{1,0:T(8,128)(2,1)S(1)}, bf16[16,512]{1,0:T(8,128)(2,1)S(1)}, u32[]{:S(2)}, u32[]{:S(2)}) collective-permute-start(bf16[16,512]{1,0:T(8,128)(2,1)S(1)} %get-tuple-element.46), channel_id=1, source_target_pairs={{0,384},{32,416},{64,448},{96,480},{128,0},{160,32},{192,64},{224,... | collective-permute-start | bytes 49160 | tf_op jit(solution)/shard_map/ppermute | solution.py:256
  80.3 5.9 %collective-permute-done.8.refs_3_ = bf16[16,512]{1,0:T(8,128)(2,1)S(1)} collective-permute-done((bf16[16,512]{1,0:T(8,128)(2,1)S(1)}, bf16[16,512]{1,0:T(8,128)(2,1)S(1)}, u32[]{:S(2)}, u32[]{:S(2)}) %collective-permute-start.8) | collective-permute-done | bytes 16416 | tf_op jit(solution)/shard_map/ppermute | solution.py:256
  86.2 5.0 %collective-permute-start.9 = (bf16[16,512]{1,0:T(8,128)(2,1)S(1)}, bf16[16,512]{1,0:T(8,128)(2,1)S(1)}, u32[]{:S(2)}, u32[]{:S(2)}) collective-permute-start(bf16[16,512]{1,0:T(8,128)(2,1)S(1)} %add_parts.1.one_ref), channel_id=1, source_target_pairs={{0,512},{512,0},{1,513},{513,1},{2,514},{514,2},{3,515},{515,3},{4... | collective-permute-start | bytes 49160 | tf_op jit(solution)/shard_map/ppermute | solution.py:256
  91.2 4.5 %collective-permute-done.9.other_ref = bf16[16,512]{1,0:T(8,128)(2,1)S(1)} collective-permute-done((bf16[16,512]{1,0:T(8,128)(2,1)S(1)}, bf16[16,512]{1,0:T(8,128)(2,1)S(1)}, u32[]{:S(2)}, u32[]{:S(2)}) %collective-permute-start.9) | collective-permute-done | bytes 16416 | tf_op jit(solution)/shard_map/ppermute | solution.py:256
  96.5 11.8 %all-to-all-start.2 = ((bf16[16,16,512]{2,1,0:T(8,128)(2,1)}), bf16[16,16,512]{2,1,0:T(8,128)(2,1)S(1)}, u32[]{:S(2)}, u32[]{:S(2)}) async-start(bf16[16,16,512]{2,1,0:T(8,128)(2,1)} %total_spread.1), calls=%async_computation.2 | async-start | bytes 524288 | tf_op jit(solution)/shard_map/all_to_all | solution.py:275
  109.0 1.1 combine_rows.1
  110.1 14.8 %all-to-all-done.2.totals_ref = bf16[16,16,512]{2,1,0:T(8,128)(2,1)S(1)} async-done(((bf16[16,16,512]{2,1,0:T(8,128)(2,1)}), bf16[16,16,512]{2,1,0:T(8,128)(2,1)S(1)}, u32[]{:S(2)}, u32[]{:S(2)}) %all-to-all-start.2) | async-done | bytes 262176 | tf_op jit(solution)/shard_map/all_to_all | solution.py:275
  124.9 1.1 update.1
  (32 shorter events, 3.6 us)
Async XLA Ops:
  0.6 11.6 %copy-start.1 = (bf16[1,2048,384]{2,1,0:T(8,128)(2,1)S(1)}, bf16[1,2048,384]{2,1,0:T(8,128)(2,1)}, u32[]{:S(2)}) copy-start(bf16[1,2048,384]{2,1,0:T(8,128)(2,1)} %gate_ref.1) | copy-start | bytes 4718596
  0.6 1.2 copy-start.6
  1.8 0.7 copy-start.9
  2.5 0.7 copy-start.10
  3.2 15.3 %copy-start.7 = (bf16[1,64,2048]{2,1,0:T(8,128)(2,1)S(1)}, bf16[1,64,2048]{2,1,0:T(8,128)(2,1)}, u32[]{:S(2)}) copy-start(bf16[1,64,2048]{2,1,0:T(8,128)(2,1)} %values_ref.1) | copy-start | bytes 786436
  3.2 15.3 %copy-start.8 = (f32[1,64,16]{1,2,0:T(8,128)S(1)}, f32[1,64,16]{1,2,0:T(8,128)}, u32[]{:S(2)}) copy-start(f32[1,64,16]{1,2,0:T(8,128)} %param.18) | copy-start | bytes 12292
  3.7 1.0 copy-start.4
  4.7 35.6 %all-to-all-start = ((bf16[16,16,2048]{2,1,0:T(8,128)(2,1)}), bf16[16,16,2048]{2,1,0:T(8,128)(2,1)S(1)}, u32[]{:S(2)}, u32[]{:S(2)}) async-start(bf16[16,16,2048]{2,1,0:T(8,128)(2,1)} %bitcast.12), calls=%async_computation | async-start | bytes 2097152 | tf_op jit(solution)/shard_map/all_to_all | solution.py:280
  12.2 28.1 %collective-permute-start.3 = (bf16[1,2048,384]{2,1,0:T(8,128)(2,1)S(1)}, bf16[1,2048,384]{2,1,0:T(8,128)(2,1)}, u32[]{:S(2)}, u32[]{:S(2)}) collective-permute-start(bf16[1,2048,384]{2,1,0:T(8,128)(2,1)S(1)} %copy-done.1), channel_id=1, source_target_pairs={{0,1},{1,0},{2,3},{3,2},{4,5},{5,4},{6,7},{7,6},{8,9},{9,8},{10,11... | collective-permute-start | bytes 4718600 | tf_op jit(solution)/shard_map/ppermute | solution.py:256
  14.1 26.2 %collective-permute-start.4 = (bf16[1,2048,384]{2,1,0:T(8,128)(2,1)}, bf16[1,2048,384]{2,1,0:T(8,128)(2,1)}, u32[]{:S(2)}, u32[]{:S(2)}) collective-permute-start(bf16[1,2048,384]{2,1,0:T(8,128)(2,1)} %up_ref.1), channel_id=1, source_target_pairs={{0,1},{1,0},{2,3},{3,2},{4,5},{5,4},{6,7},{7,6},{8,9},{9,8},{10,11... | collective-permute-start | bytes 4718600 | tf_op jit(solution)/shard_map/ppermute | solution.py:256
  16.6 23.8 %collective-permute-start.5 = (bf16[1,384,2048]{2,1,0:T(8,128)(2,1)}, bf16[1,384,2048]{2,1,0:T(8,128)(2,1)}, u32[]{:S(2)}, u32[]{:S(2)}) collective-permute-start(bf16[1,384,2048]{2,1,0:T(8,128)(2,1)} %down_ref.1), channel_id=1, source_target_pairs={{0,1},{1,0},{2,3},{3,2},{4,5},{5,4},{6,7},{7,6},{8,9},{9,8},{10,11... | collective-permute-start | bytes 4718600 | tf_op jit(solution)/shard_map/ppermute | solution.py:256
  19.1 14.7 %collective-permute-start = (bf16[16,2048]{1,0:T(8,128)(2,1)S(1)}, bf16[16,2048]{1,0:T(8,128)(2,1)S(1)}, u32[]{:S(2)}, u32[]{:S(2)}) collective-permute-start(bf16[16,2048]{1,0:T(8,128)(2,1)S(1)} %get-tuple-element.30), channel_id=1, source_target_pairs={{0,32},{32,64},{64,96},{96,0},{128,160},{160,192},{192,224},{224,1... | collective-permute-start | bytes 196616 | tf_op jit(solution)/shard_map/ppermute | solution.py:263
  23.4 14.4 %collective-permute-start.1 = (bf16[16,2048]{1,0:T(8,128)(2,1)S(1)}, bf16[16,2048]{1,0:T(8,128)(2,1)S(1)}, u32[]{:S(2)}, u32[]{:S(2)}) collective-permute-start(bf16[16,2048]{1,0:T(8,128)(2,1)S(1)} %get-tuple-element.31), channel_id=1, source_target_pairs={{0,64},{32,96},{64,0},{96,32},{128,192},{160,224},{192,128},{224,1... | collective-permute-start | bytes 196616 | tf_op jit(solution)/shard_map/ppermute | solution.py:263
  33.8 6.2 %collective-permute-start.2 = (bf16[16,2048]{1,0:T(8,128)(2,1)S(1)}, bf16[16,2048]{1,0:T(8,128)(2,1)S(1)}, u32[]{:S(2)}, u32[]{:S(2)}) collective-permute-start(bf16[16,2048]{1,0:T(8,128)(2,1)S(1)} %get-tuple-element.32), channel_id=1, source_target_pairs={{0,96},{32,0},{64,32},{96,64},{128,224},{160,128},{192,160},{224,1... | collective-permute-start | bytes 196616 | tf_op jit(solution)/shard_map/ppermute | solution.py:263
  40.3 1.4 %copy-start.2 = (bf16[1,2048,384]{2,1,0:T(8,128)(2,1)S(1)}, bf16[1,2048,384]{2,1,0:T(8,128)(2,1)}, u32[]{:S(2)}) copy-start(bf16[1,2048,384]{2,1,0:T(8,128)(2,1)} %up_ref.1) | copy-start | bytes 4718596
  41.8 1.4 %copy-start.3 = (bf16[1,384,2048]{2,1,0:T(8,128)(2,1)S(1)}, bf16[1,384,2048]{2,1,0:T(8,128)(2,1)}, u32[]{:S(2)}) copy-start(bf16[1,384,2048]{2,1,0:T(8,128)(2,1)} %down_ref.1) | copy-start | bytes 4718596
  48.6 37.6 %all-to-all-start.1 = ((bf16[16,16,2048]{2,1,0:T(8,128)(2,1)}), bf16[16,16,2048]{2,1,0:T(8,128)(2,1)S(1)}, u32[]{:S(2)}, u32[]{:S(2)}) async-start(bf16[16,16,2048]{2,1,0:T(8,128)(2,1)} %bitcast.7), calls=%async_computation.1 | async-start | bytes 2097152 | tf_op jit(solution)/shard_map/all_to_all | solution.py:280
  56.0 68.8 %copy-start = (f32[3,64,2048]{2,1,0:T(8,128)S(1)}, f32[3,64,2048]{2,1,0:T(8,128)}, u32[]{:S(2)}) copy-start(f32[3,64,2048]{2,1,0:T(8,128)} %base_ref.1) | copy-start | bytes 4718596
  56.0 68.8 %copy-start.5 = (f32[64,2048]{1,0:T(8,128)S(1)}, f32[64,2048]{1,0:T(8,128)}, u32[]{:S(2)}) copy-start(f32[64,2048]{1,0:T(8,128)} %momentum_ref.1) | copy-start | bytes 1572868
  56.0 24.2 %collective-permute-start.6 = (bf16[16,512]{1,0:T(8,128)(2,1)S(1)}, bf16[16,512]{1,0:T(8,128)(2,1)S(1)}, u32[]{:S(2)}, u32[]{:S(2)}) collective-permute-start(bf16[16,512]{1,0:T(8,128)(2,1)S(1)} %get-tuple-element.44), channel_id=1, source_target_pairs={{0,128},{32,160},{64,192},{96,224},{128,256},{160,288},{192,320},{... | collective-permute-start | bytes 49160 | tf_op jit(solution)/shard_map/ppermute | solution.py:256
  63.0 17.3 %collective-permute-start.7 = (bf16[16,512]{1,0:T(8,128)(2,1)S(1)}, bf16[16,512]{1,0:T(8,128)(2,1)S(1)}, u32[]{:S(2)}, u32[]{:S(2)}) collective-permute-start(bf16[16,512]{1,0:T(8,128)(2,1)S(1)} %get-tuple-element.45), channel_id=1, source_target_pairs={{0,256},{32,288},{64,320},{96,352},{128,384},{160,416},{192,448},{... | collective-permute-start | bytes 49160 | tf_op jit(solution)/shard_map/ppermute | solution.py:256
  76.6 9.5 %collective-permute-start.8 = (bf16[16,512]{1,0:T(8,128)(2,1)S(1)}, bf16[16,512]{1,0:T(8,128)(2,1)S(1)}, u32[]{:S(2)}, u32[]{:S(2)}) collective-permute-start(bf16[16,512]{1,0:T(8,128)(2,1)S(1)} %get-tuple-element.46), channel_id=1, source_target_pairs={{0,384},{32,416},{64,448},{96,480},{128,0},{160,32},{192,64},{224,... | collective-permute-start | bytes 49160 | tf_op jit(solution)/shard_map/ppermute | solution.py:256
  86.2 9.5 %collective-permute-start.9 = (bf16[16,512]{1,0:T(8,128)(2,1)S(1)}, bf16[16,512]{1,0:T(8,128)(2,1)S(1)}, u32[]{:S(2)}, u32[]{:S(2)}) collective-permute-start(bf16[16,512]{1,0:T(8,128)(2,1)S(1)} %add_parts.1.one_ref), channel_id=1, source_target_pairs={{0,512},{512,0},{1,513},{513,1},{2,514},{514,2},{3,515},{515,3},{4... | collective-permute-start | bytes 49160 | tf_op jit(solution)/shard_map/ppermute | solution.py:256
  96.5 28.4 %all-to-all-start.2 = ((bf16[16,16,512]{2,1,0:T(8,128)(2,1)}), bf16[16,16,512]{2,1,0:T(8,128)(2,1)S(1)}, u32[]{:S(2)}, u32[]{:S(2)}) async-start(bf16[16,16,512]{2,1,0:T(8,128)(2,1)} %total_spread.1), calls=%async_computation.2 | async-start | bytes 524288 | tf_op jit(solution)/shard_map/all_to_all | solution.py:275

commit v6 on v5

--- a/solution.py
+++ b/solution.py
@@ -122,7 +122,7 @@
     )(combine, rows)
 
 
-def dequant_kernel(z_ref, values_ref, scales_ref, *out_refs):
+def dequant_kernel(place_ref, values_ref, scales_ref, *out_refs):
     rows, width = out_refs[0].shape
     blocks = scales_ref.shape[0]
     column = lax.broadcasted_iota(jnp.int32, (blocks, width), 1) // (width // blocks)
@@ -143,12 +143,12 @@
         block = whole[place * rows : (place + 1) * rows]
         for step, out_ref in enumerate(out_refs):
 
-            @pl.when((z_ref[0] + step) % RADIX == place)
+            @pl.when((place_ref[0] + step) % RADIX == place)
             def _():
                 out_ref[...] = block
 
 
-def dequant(z, values, scales):
+def dequant(place, values, scales):
     _, rows, width = values.shape
     part = jax.ShapeDtypeStruct((rows // RADIX, width), jnp.bfloat16)
     return pl.pallas_call(
@@ -157,31 +157,7 @@
         out_shape=(part,) * RADIX,
         compiler_params=PARAMS,
         name="dequant",
-    )(z, values, scales[0].T)
-
-
-def add_split_kernel(z_ref, *refs):
-    in_refs, out_refs = refs[:RADIX], refs[RADIX:]
-    total = sum(ref[...].astype(jnp.float32) for ref in in_refs).astype(jnp.bfloat16)
-    width = out_refs[0].shape[1]
-    for place in range(RADIX):
-        for step, out_ref in enumerate(out_refs):
-
-            @pl.when((z_ref[0] // RADIX + step) % RADIX == place)
-            def _():
-                out_ref[...] = total[:, place * width : (place + 1) * width]
-
-
-def add_split(z, parts):
-    rows, width = parts[0].shape
-    part = jax.ShapeDtypeStruct((rows, width // RADIX), jnp.bfloat16)
-    return pl.pallas_call(
-        add_split_kernel,
-        in_specs=[SMEM] + [VMEM] * RADIX,
-        out_shape=(part,) * RADIX,
-        compiler_params=PARAMS,
-        name="add_split",
-    )(z, *parts)
+    )(place, values, scales[0].T)
 
 
 def add_kernel(*refs):
@@ -197,31 +173,30 @@
     )(*parts)
 
 
-def total_kernel(one_ref, other_ref, out_ref):
-    total = (one_ref[...].astype(jnp.float32) + other_ref[...].astype(jnp.float32)).astype(
-        jnp.bfloat16
-    )
+def total_kernel(parts_ref, out_ref):
+    total = jnp.sum(parts_ref[...].astype(jnp.float32), axis=0).astype(jnp.bfloat16)
     out_ref[...] = jnp.broadcast_to(total[None], out_ref.shape)
 
 
-def total_spread(one, other, copies):
+def total_spread(parts):
     return pl.pallas_call(
         total_kernel,
-        out_shape=jax.ShapeDtypeStruct((copies,) + one.shape, jnp.bfloat16),
+        out_shape=jax.ShapeDtypeStruct((RADIX,) + parts.shape[1:], jnp.bfloat16),
         compiler_params=PARAMS,
         name="total_spread",
-    )(one, other)
+    )(parts)
 
 
 def update_kernel(replicas, fragment_ref, totals_ref, base_ref, momentum_ref, params_out, momentum_out):
-    pieces, rows, span = totals_ref.shape
+    pieces, rows, _ = totals_ref.shape
     for piece in range(pieces):
-        far, near = piece // RADIX, piece % RADIX
-        at = (pl.ds(near * rows, rows), pl.ds(far * span, span))
+        at = pl.ds(piece * rows, rows)
         delta = totals_ref[piece].astype(jnp.float32) / replicas
-        new_momentum = momentum_rate * momentum_ref[at] + delta
-        momentum_out[at] = new_momentum
-        params_out[at] = base_ref[(0,) + at] - outer_rate * (delta + momentum_rate * new_momentum)
+        new_momentum = momentum_rate * momentum_ref[at, :] + delta
+        momentum_out[at, :] = new_momentum
+        params_out[at, :] = base_ref[0, at, :] - outer_rate * (
+            delta + momentum_rate * new_momentum
+        )
 
 
 def update(replicas, totals, outer_params, momentum, fragment):
@@ -256,23 +231,12 @@
     return lax.ppermute(part, axis, [(i, (i + step) % size) for i in range(size)])
 
 
-def near_shift(part, step):
-    def target(i):
-        return i // RADIX * RADIX + (i + step) % RADIX
-
-    return lax.ppermute(part, "z", [(i, target(i)) for i in range(lax.axis_size("z"))])
-
-
-def far_shift(part, step):
-    return shift(part, "z", RADIX * step)
-
-
-def scatter_stage(parts, move):
-    return [parts[0]] + [move(parts[step], step) for step in range(1, RADIX)]
-
-
-def gather_z(parts):
-    return lax.all_to_all(parts, "z", split_axis=0, concat_axis=0, tiled=True)
+def scatter_stage(parts, axis):
+    return [parts[0]] + [shift(parts[step], axis, step) for step in range(1, RADIX)]
+
+
+def place_on(axis):
+    return lax.axis_index(axis).astype(jnp.int32).reshape(1)
 
 
 def exchange(rows, experts):
@@ -299,20 +263,20 @@
     buffer, combine = route(tokens, expert_ids, route_weights, experts)
     mine = exchange(buffer, experts)
     own = (w_gate, w_up, w_down)
-    z = lax.axis_index("z").astype(jnp.int32).reshape(1)
-    parts = scatter_stage(dequant(z, pseudo_values, block_scales), near_shift)
-    parts = add_split(z, parts)
+    near = place_on("z_near")
+    part = add_parts(scatter_stage(dequant(near, pseudo_values, block_scales), "z_near"))
     other = [shift(w, "core", 1) for w in own]
-    mine, parts = lax.optimization_barrier((mine, parts))
+    mine, part = lax.optimization_barrier((mine, part))
     rows = expert_rows(mine, own, other)
-    rows, parts = lax.optimization_barrier((rows, parts))
+    rows, apart = lax.optimization_barrier((rows, shift(part, "y_far", 1)))
+    part = add_parts([part, apart])
     returned = exchange(rows, experts)
-    part = add_parts(scatter_stage(parts, far_shift))
-    returned, part = lax.optimization_barrier((returned, part))
-    spread = total_spread(part, shift(part, "y_far", 1), lax.axis_size("z"))
+    spread = total_spread(lax.all_gather(part, "z_far", axis=0))
+    returned, spread = lax.optimization_barrier((returned, spread))
+    totals = lax.all_to_all(spread, "z_near", split_axis=0, concat_axis=0, tiled=True)
     moe_out = combine_rows(combine, returned)
     new_params, new_momentum = update(
-        lax.axis_size(("y_far", "z")), gather_z(spread), outer_params, momentum, fragment
+        lax.axis_size(("y_far", "z_far", "z_near")), totals, outer_params, momentum, fragment
     )
     return (moe_out, new_params, new_momentum)
 
@@ -320,10 +284,10 @@
 def solution(mesh):
     reps, exps = mesh.devices.shape
     fine = Mesh(
-        mesh.devices.reshape(reps // (RADIX * RADIX), RADIX * RADIX, exps // 2, 2),
-        ("y_far", "z", "chip", "core"),
-    )
-    rep = ("y_far", "z")
+        mesh.devices.reshape(reps // (RADIX * RADIX), RADIX, RADIX, exps // 2, 2),
+        ("y_far", "z_far", "z_near", "chip", "core"),
+    )
+    rep = ("y_far", "z_far", "z_near")
     exp = ("chip", "core")
     return jax.shard_map(
         shards,

time: 127 us -> 103 us (0.81)
  the two profiles are of different devices: /device:TPU:64 before, /device:TPU:6 now
where the time goes in v6:
time: 103 us; the launch traced here: 102 us
  starting transfers between devices  43.2 us (42%)
  blocking collectives  27.3 us (27%)
  waiting for transfers between devices  14.2 us (14%)
  Pallas kernels  9.53 us (9%)
  local copies, waits for them, and re-layouts  6.34 us (6%)
  between operations  1.48 us (1%)
    all_gather x1, blocking collectives, shards(): spread = total_spread(lax.all_gather(part, 'z_far', axis=0))  27.3 us
    all_to_all x2, starting transfers between devices, exchange(): lax.all_to_all(rows.reshape(experts, CAP, width), 'chip', split_axis=0, c...  23.6 us
    ppermute x7, starting transfers between devices, shift(): lax.ppermute(part, axis, [(i, (i + step) % size) for i in range(size)])  13.9 us
    ppermute x7, waiting for transfers between devices, shift(): lax.ppermute(part, axis, [(i, (i + step) % size) for i in range(size)])  9.22 us
    unnamed x22, local copies, waits for them, and re-layouts  6.34 us
    all_to_all x1, starting transfers between devices, shards(): lax.all_to_all(spread, 'z_near', split_axis=0, concat_axis=0, tiled=True)  5.73 us
    pallas_call x1, Pallas kernels, expert_rows(): pl.pallas_call(expert_kernel, in_specs=[VMEM] * 4 + [HBM] * 3, out_shape=...  5.37 us
    all_to_all x1, waiting for transfers between devices, shards(): lax.all_to_all(spread, 'z_near', split_axis=0, concat_axis=0, tiled=True)  5 us
  transfers between devices with their start and end apart: 10, of which 5 were waited for; matrix products, arithmetic and copies ran while one was open for 0% of the time, Pallas kernels for 8%

profile of v6, /device:TPU:6, one launch (start us, length us, event | category | flops | bytes accessed | tf_op | source)
XLA Modules:
  0.0 102.1 jit_solution(8127608116402924769)
XLA Ops:
  0.7 1.2 %copy-done.6 = bf16[128,2048]{1,0:T(8,128)(2,1)S(1)} copy-done((bf16[128,2048]{1,0:T(8,128)(2,1)S(1)}, bf16[128,2048]{1,0:T(8,128)(2,1)}, u32[]{:S(2)}) %copy-start.6) | copy-done | bytes 524312
  1.8 0.7 copy-done.9
  3.7 1.0 copy-done.4
  4.7 16.6 %all-to-all-start = ((bf16[16,16,2048]{2,1,0:T(8,128)(2,1)}), bf16[16,16,2048]{2,1,0:T(8,128)(2,1)S(1)}, u32[]{:S(2)}, u32[]{:S(2)}) async-start(bf16[16,16,2048]{2,1,0:T(8,128)(2,1)} %bitcast.14), calls=%async_computation | async-start | bytes 2097152 | tf_op jit(solution)/shard_map/all_to_all | solution.py:244
  21.4 1.9 %collective-permute-start.3 = (bf16[1,2048,384]{2,1,0:T(8,128)(2,1)S(1)}, bf16[1,2048,384]{2,1,0:T(8,128)(2,1)}, u32[]{:S(2)}, u32[]{:S(2)}) collective-permute-start(bf16[1,2048,384]{2,1,0:T(8,128)(2,1)S(1)} %copy-done.1), channel_id=1, source_target_pairs={{0,1},{1,0},{2,3},{3,2},{4,5},{5,4},{6,7},{7,6},{8,9},{9,8},{10,11... | collective-permute-start | bytes 4718600 | tf_op jit(solution)/shard_map/ppermute | solution.py:231
  23.3 2.4 %collective-permute-start.4 = (bf16[1,2048,384]{2,1,0:T(8,128)(2,1)}, bf16[1,2048,384]{2,1,0:T(8,128)(2,1)}, u32[]{:S(2)}, u32[]{:S(2)}) collective-permute-start(bf16[1,2048,384]{2,1,0:T(8,128)(2,1)} %up_ref.1), channel_id=1, source_target_pairs={{0,1},{1,0},{2,3},{3,2},{4,5},{5,4},{6,7},{7,6},{8,9},{9,8},{10,11... | collective-permute-start | bytes 4718600 | tf_op jit(solution)/shard_map/ppermute | solution.py:231
  25.7 1.9 %collective-permute-start.5 = (bf16[1,384,2048]{2,1,0:T(8,128)(2,1)}, bf16[1,384,2048]{2,1,0:T(8,128)(2,1)}, u32[]{:S(2)}, u32[]{:S(2)}) collective-permute-start(bf16[1,384,2048]{2,1,0:T(8,128)(2,1)} %down_ref.1), channel_id=1, source_target_pairs={{0,1},{1,0},{2,3},{3,2},{4,5},{5,4},{6,7},{7,6},{8,9},{9,8},{10,11... | collective-permute-start | bytes 4718600 | tf_op jit(solution)/shard_map/ppermute | solution.py:231
  28.3 1.9 %collective-permute-start = (bf16[16,2048]{1,0:T(8,128)(2,1)S(1)}, bf16[16,2048]{1,0:T(8,128)(2,1)S(1)}, u32[]{:S(2)}, u32[]{:S(2)}) collective-permute-start(bf16[16,2048]{1,0:T(8,128)(2,1)S(1)} %get-tuple-element.20), channel_id=1, source_target_pairs={{0,32},{32,64},{64,96},{96,0},{1,33},{33,65},{65,97},{97,1},{2,34}... | collective-permute-start | bytes 196616 | tf_op jit(solution)/shard_map/ppermute | solution.py:231
  30.2 1.9 %collective-permute-start.1 = (bf16[16,2048]{1,0:T(8,128)(2,1)S(1)}, bf16[16,2048]{1,0:T(8,128)(2,1)S(1)}, u32[]{:S(2)}, u32[]{:S(2)}) collective-permute-start(bf16[16,2048]{1,0:T(8,128)(2,1)S(1)} %get-tuple-element.21), channel_id=1, source_target_pairs={{0,64},{32,96},{64,0},{96,32},{1,65},{33,97},{65,1},{97,33},{2,66}... | collective-permute-start | bytes 196616 | tf_op jit(solution)/shard_map/ppermute | solution.py:231
  32.1 4.4 %collective-permute-done.refs_1_ = bf16[16,2048]{1,0:T(8,128)(2,1)S(1)} collective-permute-done((bf16[16,2048]{1,0:T(8,128)(2,1)S(1)}, bf16[16,2048]{1,0:T(8,128)(2,1)S(1)}, u32[]{:S(2)}, u32[]{:S(2)}) %collective-permute-start) | collective-permute-done | bytes 65568 | tf_op jit(solution)/shard_map/ppermute | solution.py:231
  36.5 1.9 %collective-permute-start.2 = (bf16[16,2048]{1,0:T(8,128)(2,1)S(1)}, bf16[16,2048]{1,0:T(8,128)(2,1)S(1)}, u32[]{:S(2)}, u32[]{:S(2)}) collective-permute-start(bf16[16,2048]{1,0:T(8,128)(2,1)S(1)} %get-tuple-element.22), channel_id=1, source_target_pairs={{0,96},{32,0},{64,32},{96,64},{1,97},{33,1},{65,33},{97,65},{2,98}... | collective-permute-start | bytes 196616 | tf_op jit(solution)/shard_map/ppermute | solution.py:231
  38.4 0.9 collective-permute-done.1.refs_2_
  39.3 3.4 %collective-permute-done.2.refs_3_ = bf16[16,2048]{1,0:T(8,128)(2,1)S(1)} collective-permute-done((bf16[16,2048]{1,0:T(8,128)(2,1)S(1)}, bf16[16,2048]{1,0:T(8,128)(2,1)S(1)}, u32[]{:S(2)}, u32[]{:S(2)}) %collective-permute-start.2) | collective-permute-done | bytes 65568 | tf_op jit(solution)/shard_map/ppermute | solution.py:231
  42.7 1.9 %collective-permute-start.6 = (bf16[16,2048]{1,0:T(8,128)(2,1)S(1)}, bf16[16,2048]{1,0:T(8,128)(2,1)S(1)}, u32[]{:S(2)}, u32[]{:S(2)}) collective-permute-start(bf16[16,2048]{1,0:T(8,128)(2,1)S(1)} %add_parts.2.refs_0_), channel_id=1, source_target_pairs={{0,512},{512,0},{1,513},{513,1},{2,514},{514,2},{3,515},{515,3},{4... | collective-permute-start | bytes 196616 | tf_op jit(solution)/shard_map/ppermute | solution.py:231
  44.7 1.4 %copy-done.2 = bf16[1,2048,384]{2,1,0:T(8,128)(2,1)S(1)} copy-done((bf16[1,2048,384]{2,1,0:T(8,128)(2,1)S(1)}, bf16[1,2048,384]{2,1,0:T(8,128)(2,1)}, u32[]{:S(2)}) %copy-start.2) | copy-done | bytes 1572888
  46.1 1.4 %copy-done.3 = bf16[1,384,2048]{2,1,0:T(8,128)(2,1)S(1)} copy-done((bf16[1,384,2048]{2,1,0:T(8,128)(2,1)S(1)}, bf16[1,384,2048]{2,1,0:T(8,128)(2,1)}, u32[]{:S(2)}) %copy-start.3) | copy-done | bytes 1572888
  47.5 5.4 %expert_rows.1 = bf16[256,2048]{1,0:T(8,128)(2,1)} custom-call(bf16[256,2048]{1,0:T(8,128)(2,1)S(1)} %bitcast.12, bf16[1,2048,384]{2,1,0:T(8,128)(2,1)S(1)} %copy-done.1, bf16[1,2048,384]{2,1,0:T(8,128)(2,1)S(1)} %copy-done.2, bf16[1,384,2048]{2,1,0:T(8,128)(2,1)S(1)} %copy-done.3, bf16[1,2048,384]{2,1,0:T(8,128)(2,1)} %collective-permute-done.3.refs_0_, ...), custom_call_target="tpu_custom_call" | custom-call | tf_op jit(solution)/shard_map/expert_rows/pallas_call | solution.py:96
  53.5 6.9 %all-to-all-start.1 = ((bf16[16,16,2048]{2,1,0:T(8,128)(2,1)}), bf16[16,16,2048]{2,1,0:T(8,128)(2,1)S(1)}, u32[]{:S(2)}, u32[]{:S(2)}) async-start(bf16[16,16,2048]{2,1,0:T(8,128)(2,1)} %bitcast.7), calls=%async_computation.1 | async-start | bytes 2097152 | tf_op jit(solution)/shard_map/all_to_all | solution.py:244
  60.4 27.3 %all-gather = bf16[64,2048]{1,0:T(8,128)(2,1)S(1)} all-gather(bf16[16,2048]{1,0:T(8,128)(2,1)S(1)} %add_parts.3), channel_id=2, replica_groups=mesh['y_far'=2,'z_far'=4,'z_near'=4,'chip'=16,'core'=2] {'z_far'}, dimensions={0}, use_global_device_ids=true | all-gather | bytes 327680 | tf_op jit(solution)/shard_map/all_gather | solution.py:274
  87.7 0.7 total_spread.1
  88.5 5.7 %all-to-all-start.2 = ((bf16[4,16,2048]{2,1,0:T(8,128)(2,1)}), bf16[4,16,2048]{2,1,0:T(8,128)(2,1)S(1)}, u32[]{:S(2)}, u32[]{:S(2)}) async-start(bf16[4,16,2048]{2,1,0:T(8,128)(2,1)} %total_spread.1), calls=%async_computation.2 | async-start | bytes 524288 | tf_op jit(solution)/shard_map/all_to_all | solution.py:276
  94.9 1.1 %combine_rows.1 = bf16[128,2048]{1,0:T(8,128)(2,1)} custom-call(bf16[256,128]{1,0:T(8,128)(2,1)S(1)} %get-tuple-element.17.combine_ref, bf16[256,2048]{1,0:T(8,128)(2,1)S(1)} %bitcast.11), custom_call_target="tpu_custom_call" | custom-call | tf_op jit(solution)/shard_map/combine_rows/pallas_call | solution.py:117
  96.0 5.0 %all-to-all-done.2.totals_ref = bf16[4,16,2048]{2,1,0:T(8,128)(2,1)S(1)} async-done(((bf16[4,16,2048]{2,1,0:T(8,128)(2,1)}), bf16[4,16,2048]{2,1,0:T(8,128)(2,1)S(1)}, u32[]{:S(2)}, u32[]{:S(2)}) %all-to-all-start.2) | async-done | bytes 262176 | tf_op jit(solution)/shard_map/all_to_all | solution.py:276
  101.0 1.1 %update.1 = (f32[64,2048]{1,0:T(8,128)}, f32[64,2048]{1,0:T(8,128)}) custom-call(s32[1]{0:T(128)S(6)} %copy.14.fragment_ref, bf16[4,16,2048]{2,1,0:T(8,128)(2,1)S(1)} %all-to-all-done.2.totals_ref, f32[3,64,2048]{2,1,0:T(8,128)S(1)} %copy-done, f32[64,2048]{1,0:T(8,128)S(1)} %copy-done.5), custom_call_target="tpu_custom_call" | custom-call | tf_op jit(solution)/shard_map/update/pallas_call | solution.py:208
  (27 shorter events, 2.5 us)
Async XLA Ops:
  0.6 20.7 %copy-start.1 = (bf16[1,2048,384]{2,1,0:T(8,128)(2,1)S(1)}, bf16[1,2048,384]{2,1,0:T(8,128)(2,1)}, u32[]{:S(2)}) copy-start(bf16[1,2048,384]{2,1,0:T(8,128)(2,1)} %gate_ref.1) | copy-start | bytes 4718596
  0.6 1.2 %copy-start.6 = (bf16[128,2048]{1,0:T(8,128)(2,1)S(1)}, bf16[128,2048]{1,0:T(8,128)(2,1)}, u32[]{:S(2)}) copy-start(bf16[128,2048]{1,0:T(8,128)(2,1)} %tokens_ref.1) | copy-start | bytes 1572868
  1.8 0.7 copy-start.9
  2.5 0.7 copy-start.10
  3.2 24.5 %copy-start.7 = (bf16[1,64,2048]{2,1,0:T(8,128)(2,1)S(1)}, bf16[1,64,2048]{2,1,0:T(8,128)(2,1)}, u32[]{:S(2)}) copy-start(bf16[1,64,2048]{2,1,0:T(8,128)(2,1)} %values_ref.1) | copy-start | bytes 786436
  3.2 24.5 %copy-start.8 = (f32[1,64,16]{1,2,0:T(8,128)S(1)}, f32[1,64,16]{1,2,0:T(8,128)}, u32[]{:S(2)}) copy-start(f32[1,64,16]{1,2,0:T(8,128)} %param.18) | copy-start | bytes 12292
  3.7 1.0 copy-start.4
  4.7 38.0 %all-to-all-start = ((bf16[16,16,2048]{2,1,0:T(8,128)(2,1)}), bf16[16,16,2048]{2,1,0:T(8,128)(2,1)S(1)}, u32[]{:S(2)}, u32[]{:S(2)}) async-start(bf16[16,16,2048]{2,1,0:T(8,128)(2,1)} %bitcast.14), calls=%async_computation | async-start | bytes 2097152 | tf_op jit(solution)/shard_map/all_to_all | solution.py:244
  21.4 23.3 %collective-permute-start.3 = (bf16[1,2048,384]{2,1,0:T(8,128)(2,1)S(1)}, bf16[1,2048,384]{2,1,0:T(8,128)(2,1)}, u32[]{:S(2)}, u32[]{:S(2)}) collective-permute-start(bf16[1,2048,384]{2,1,0:T(8,128)(2,1)S(1)} %copy-done.1), channel_id=1, source_target_pairs={{0,1},{1,0},{2,3},{3,2},{4,5},{5,4},{6,7},{7,6},{8,9},{9,8},{10,11... | collective-permute-start | bytes 4718600 | tf_op jit(solution)/shard_map/ppermute | solution.py:231
  23.3 21.3 %collective-permute-start.4 = (bf16[1,2048,384]{2,1,0:T(8,128)(2,1)}, bf16[1,2048,384]{2,1,0:T(8,128)(2,1)}, u32[]{:S(2)}, u32[]{:S(2)}) collective-permute-start(bf16[1,2048,384]{2,1,0:T(8,128)(2,1)} %up_ref.1), channel_id=1, source_target_pairs={{0,1},{1,0},{2,3},{3,2},{4,5},{5,4},{6,7},{7,6},{8,9},{9,8},{10,11... | collective-permute-start | bytes 4718600 | tf_op jit(solution)/shard_map/ppermute | solution.py:231
  25.7 18.9 %collective-permute-start.5 = (bf16[1,384,2048]{2,1,0:T(8,128)(2,1)}, bf16[1,384,2048]{2,1,0:T(8,128)(2,1)}, u32[]{:S(2)}, u32[]{:S(2)}) collective-permute-start(bf16[1,384,2048]{2,1,0:T(8,128)(2,1)} %down_ref.1), channel_id=1, source_target_pairs={{0,1},{1,0},{2,3},{3,2},{4,5},{5,4},{6,7},{7,6},{8,9},{9,8},{10,11... | collective-permute-start | bytes 4718600 | tf_op jit(solution)/shard_map/ppermute | solution.py:231
  28.3 8.2 %collective-permute-start = (bf16[16,2048]{1,0:T(8,128)(2,1)S(1)}, bf16[16,2048]{1,0:T(8,128)(2,1)S(1)}, u32[]{:S(2)}, u32[]{:S(2)}) collective-permute-start(bf16[16,2048]{1,0:T(8,128)(2,1)S(1)} %get-tuple-element.20), channel_id=1, source_target_pairs={{0,32},{32,64},{64,96},{96,0},{1,33},{33,65},{65,97},{97,1},{2,34}... | collective-permute-start | bytes 196616 | tf_op jit(solution)/shard_map/ppermute | solution.py:231
  30.2 9.1 %collective-permute-start.1 = (bf16[16,2048]{1,0:T(8,128)(2,1)S(1)}, bf16[16,2048]{1,0:T(8,128)(2,1)S(1)}, u32[]{:S(2)}, u32[]{:S(2)}) collective-permute-start(bf16[16,2048]{1,0:T(8,128)(2,1)S(1)} %get-tuple-element.21), channel_id=1, source_target_pairs={{0,64},{32,96},{64,0},{96,32},{1,65},{33,97},{65,1},{97,33},{2,66}... | collective-permute-start | bytes 196616 | tf_op jit(solution)/shard_map/ppermute | solution.py:231
  36.5 6.1 %collective-permute-start.2 = (bf16[16,2048]{1,0:T(8,128)(2,1)S(1)}, bf16[16,2048]{1,0:T(8,128)(2,1)S(1)}, u32[]{:S(2)}, u32[]{:S(2)}) collective-permute-start(bf16[16,2048]{1,0:T(8,128)(2,1)S(1)} %get-tuple-element.22), channel_id=1, source_target_pairs={{0,96},{32,0},{64,32},{96,64},{1,97},{33,1},{65,33},{97,65},{2,98}... | collective-permute-start | bytes 196616 | tf_op jit(solution)/shard_map/ppermute | solution.py:231
  42.7 10.8 %collective-permute-start.6 = (bf16[16,2048]{1,0:T(8,128)(2,1)S(1)}, bf16[16,2048]{1,0:T(8,128)(2,1)S(1)}, u32[]{:S(2)}, u32[]{:S(2)}) collective-permute-start(bf16[16,2048]{1,0:T(8,128)(2,1)S(1)} %add_parts.2.refs_0_), channel_id=1, source_target_pairs={{0,512},{512,0},{1,513},{513,1},{2,514},{514,2},{3,515},{515,3},{4... | collective-permute-start | bytes 196616 | tf_op jit(solution)/shard_map/ppermute | solution.py:231
  44.7 1.4 %copy-start.2 = (bf16[1,2048,384]{2,1,0:T(8,128)(2,1)S(1)}, bf16[1,2048,384]{2,1,0:T(8,128)(2,1)}, u32[]{:S(2)}) copy-start(bf16[1,2048,384]{2,1,0:T(8,128)(2,1)} %up_ref.1) | copy-start | bytes 4718596
  46.1 1.4 %copy-start.3 = (bf16[1,384,2048]{2,1,0:T(8,128)(2,1)S(1)}, bf16[1,384,2048]{2,1,0:T(8,128)(2,1)}, u32[]{:S(2)}) copy-start(bf16[1,384,2048]{2,1,0:T(8,128)(2,1)} %down_ref.1) | copy-start | bytes 4718596
  53.5 35.0 %all-to-all-start.1 = ((bf16[16,16,2048]{2,1,0:T(8,128)(2,1)}), bf16[16,16,2048]{2,1,0:T(8,128)(2,1)S(1)}, u32[]{:S(2)}, u32[]{:S(2)}) async-start(bf16[16,16,2048]{2,1,0:T(8,128)(2,1)} %bitcast.7), calls=%async_computation.1 | async-start | bytes 2097152 | tf_op jit(solution)/shard_map/all_to_all | solution.py:244
  60.4 40.6 %copy-start = (f32[3,64,2048]{2,1,0:T(8,128)S(1)}, f32[3,64,2048]{2,1,0:T(8,128)}, u32[]{:S(2)}) copy-start(f32[3,64,2048]{2,1,0:T(8,128)} %base_ref.1) | copy-start | bytes 4718596
  60.4 40.6 %copy-start.5 = (f32[64,2048]{1,0:T(8,128)S(1)}, f32[64,2048]{1,0:T(8,128)}, u32[]{:S(2)}) copy-start(f32[64,2048]{1,0:T(8,128)} %momentum_ref.1) | copy-start | bytes 1572868
  88.5 12.5 %all-to-all-start.2 = ((bf16[4,16,2048]{2,1,0:T(8,128)(2,1)}), bf16[4,16,2048]{2,1,0:T(8,128)(2,1)S(1)}, u32[]{:S(2)}, u32[]{:S(2)}) async-start(bf16[4,16,2048]{2,1,0:T(8,128)(2,1)} %total_spread.1), calls=%async_computation.2 | async-start | bytes 524288 | tf_op jit(solution)/shard_map/all_to_all | solution.py:276

commit v7 on v6

--- a/solution.py
+++ b/solution.py
@@ -14,15 +14,27 @@
 momentum_rate = 0.9
 outer_rate = 0.7
 
+ROUTE_PARAMS = pltpu.CompilerParams(vmem_limit_bytes=62 * 1024 * 1024)
+EXPERT_PARAMS = pltpu.CompilerParams(vmem_limit_bytes=62 * 1024 * 1024)
 PARAMS = pltpu.CompilerParams(vmem_limit_bytes=20 * 1024 * 1024)
 VMEM = pl.BlockSpec(memory_space=pltpu.VMEM)
 HBM = pl.BlockSpec(memory_space=pltpu.HBM)
 SMEM = pl.BlockSpec(memory_space=pltpu.SMEM)
 
 
-def route_kernel(experts, ids_ref, weights_ref, tokens_ref, buffer_ref, combine_ref):
+def route_kernel(experts, *refs):
+    sources, (buffer_ref, combine_ref), targets, sems = refs[:3], refs[3:5], refs[5:8], refs[8]
+    fetches = [
+        pltpu.make_async_copy(source, target, sems.at[i])
+        for i, (source, target) in enumerate(zip(sources, targets))
+    ]
+    for fetch in fetches:
+        fetch.start()
+    ids_ref, weights_ref, tokens_ref = targets
     topk, rows = ids_ref.shape
+    fetches[0].wait()
     ids = ids_ref[...]
+    fetches[1].wait()
     weights = weights_ref[...]
     expert = lax.broadcasted_iota(jnp.int32, (experts, rows), 0)
     named = jnp.zeros((experts, rows), jnp.float32)
@@ -48,6 +60,7 @@
         .reshape(experts * CAP, rows)
         .astype(jnp.bfloat16)
     )
+    fetches[2].wait()
     buffer_ref[...] = jnp.dot(
         pick.astype(jnp.bfloat16), tokens_ref[...], preferred_element_type=jnp.float32
     ).astype(jnp.bfloat16)
@@ -55,19 +68,23 @@
 
 def route(tokens, expert_ids, route_weights, experts):
     rows, width = tokens.shape
+    operands = (expert_ids.T, route_weights.T, tokens)
     return pl.pallas_call(
         functools.partial(route_kernel, experts),
         out_shape=(
             jax.ShapeDtypeStruct((experts * CAP, width), jnp.bfloat16),
             jax.ShapeDtypeStruct((experts * CAP, rows), jnp.bfloat16),
         ),
-        compiler_params=PARAMS,
+        in_specs=[HBM] * len(operands),
+        scratch_shapes=[pltpu.VMEM(x.shape, x.dtype) for x in operands]
+        + [pltpu.SemaphoreType.DMA((len(operands),))],
+        compiler_params=ROUTE_PARAMS,
         name="route",
-    )(expert_ids.T, route_weights.T, tokens)
-
-
-def expert_kernel(rows_ref, gate_ref, up_ref, down_ref, *refs):
-    sources, out_ref, targets, sems = refs[:3], refs[3], refs[4:7], refs[7]
+    )(*operands)
+
+
+def expert_kernel(rows_ref, *refs):
+    sources, out_ref, targets, sems = refs[:6], refs[6], refs[7:13], refs[13]
     fetches = [
         pltpu.make_async_copy(source, target, sems.at[i])
         for i, (source, target) in enumerate(zip(sources, targets))
@@ -75,33 +92,30 @@
     for fetch in fetches:
         fetch.start()
     rows = rows_ref[...]
-
-    def part(gate_ref, up_ref, down_ref, waits):
-        for wait in waits[:1]:
-            wait.wait()
-        gate = jnp.dot(rows, gate_ref[0], preferred_element_type=jnp.float32)
-        for wait in waits[1:2]:
-            wait.wait()
-        up = jnp.dot(rows, up_ref[0], preferred_element_type=jnp.float32)
+    total = None
+    for first in (0, 3):
+        fetches[first].wait()
+        gate = jnp.dot(rows, targets[first][0], preferred_element_type=jnp.float32)
+        fetches[first + 1].wait()
+        up = jnp.dot(rows, targets[first + 1][0], preferred_element_type=jnp.float32)
         hidden = (gate / (1.0 + jnp.exp(-gate)) * up).astype(jnp.bfloat16)
-        for wait in waits[2:]:
-            wait.wait()
-        return jnp.dot(hidden, down_ref[0], preferred_element_type=jnp.float32)
-
-    total = part(gate_ref, up_ref, down_ref, []) + part(*targets, fetches)
+        fetches[first + 2].wait()
+        part = jnp.dot(hidden, targets[first + 2][0], preferred_element_type=jnp.float32)
+        total = part if total is None else total + part
     out_ref[...] = total.astype(jnp.bfloat16)
 
 
 def expert_rows(rows, own, other):
+    weights = own + other
     return pl.pallas_call(
         expert_kernel,
-        in_specs=[VMEM] * 4 + [HBM] * 3,
+        in_specs=[VMEM] + [HBM] * len(weights),
         out_shape=jax.ShapeDtypeStruct(rows.shape, jnp.bfloat16),
-        scratch_shapes=[pltpu.VMEM(x.shape, x.dtype) for x in other]
-        + [pltpu.SemaphoreType.DMA((3,))],
-        compiler_params=PARAMS,
+        scratch_shapes=[pltpu.VMEM(x.shape, x.dtype) for x in weights]
+        + [pltpu.SemaphoreType.DMA((len(weights),))],
+        compiler_params=EXPERT_PARAMS,
         name="expert_rows",
-    )(rows, *own, *other)
+    )(rows, *weights)
 
 
 def combine_kernel(combine_ref, rows_ref, out_ref):
@@ -265,10 +279,11 @@
     own = (w_gate, w_up, w_down)
     near = place_on("z_near")
     part = add_parts(scatter_stage(dequant(near, pseudo_values, block_scales), "z_near"))
-    other = [shift(w, "core", 1) for w in own]
+    apart = shift(part, "y_far", 1)
+    other = tuple(shift(w, "core", 1) for w in own)
     mine, part = lax.optimization_barrier((mine, part))
     rows = expert_rows(mine, own, other)
-    rows, apart = lax.optimization_barrier((rows, shift(part, "y_far", 1)))
+    rows, apart = lax.optimization_barrier((rows, apart))
     part = add_parts([part, apart])
     returned = exchange(rows, experts)
     spread = total_spread(lax.all_gather(part, "z_far", axis=0))

time: 103 us -> 98.5 us (0.956)
  the two profiles are of different devices: /device:TPU:6 before, /device:TPU:32 now
where the time goes in v7:
time: 98.5 us; the launch traced here: 97.9 us
  starting transfers between devices  47.8 us (49%)
  blocking collectives  22 us (22%)
  Pallas kernels  14 us (14%)
  waiting for transfers between devices  12.5 us (13%)
  between operations  1.51 us (2%)
    ppermute x7, starting transfers between devices, shift(): lax.ppermute(part, axis, [(i, (i + step) % size) for i in range(size)])  32 us
    all_gather x1, blocking collectives, shards(): spread = total_spread(lax.all_gather(part, 'z_far', axis=0))  22 us
    all_to_all x2, starting transfers between devices, exchange(): lax.all_to_all(rows.reshape(experts, CAP, width), 'chip', split_axis=0, c...  12.3 us
    pallas_call x1, Pallas kernels, expert_rows(): pl.pallas_call(expert_kernel, in_specs=[VMEM] + [HBM] * len(weights), out...  7.88 us
    all_to_all x1, waiting for transfers between devices, shards(): lax.all_to_all(spread, 'z_near', split_axis=0, concat_axis=0, tiled=True)  6.36 us
    all_to_all x1, starting transfers between devices, shards(): lax.all_to_all(spread, 'z_near', split_axis=0, concat_axis=0, tiled=True)  3.41 us
    all_to_all x2, waiting for transfers between devices, exchange(): lax.all_to_all(rows.reshape(experts, CAP, width), 'chip', split_axis=0, c...  3.38 us
    ppermute x7, waiting for transfers between devices, shift(): lax.ppermute(part, axis, [(i, (i + step) % size) for i in range(size)])  2.77 us
  transfers between devices with their start and end apart: 10, of which 4 were waited for; matrix products, arithmetic and copies ran while one was open for 0% of the time, Pallas kernels for 11%

profile of v7, /device:TPU:32, one launch (start us, length us, event | category | flops | bytes accessed | tf_op | source)
XLA Modules:
  0.0 97.9 jit_solution(18152439734372040209)
XLA Ops:
  0.7 2.6 %route.1 = (bf16[256,2048]{1,0:T(8,128)(2,1)}, bf16[256,128]{1,0:T(8,128)(2,1)}) custom-call(s32[8,128]{1,0:T(8,128)} %bitcast.16, f32[8,128]{1,0:T(8,128)} %bitcast.17, bf16[128,2048]{1,0:T(8,128)(2,1)} %refs_2_.2), custom_call_target="tpu_custom_call" | custom-call | tf_op jit(solution)/shard_map/route/pallas_call | solution.py:72
  3.2 4.8 %all-to-all-start = ((bf16[16,16,2048]{2,1,0:T(8,128)(2,1)}), bf16[16,16,2048]{2,1,0:T(8,128)(2,1)}, u32[]{:S(2)}, u32[]{:S(2)}) async-start(bf16[16,16,2048]{2,1,0:T(8,128)(2,1)} %bitcast.15), calls=%async_computation | async-start | bytes 2097152 | tf_op jit(solution)/shard_map/all_to_all | solution.py:258
  8.0 1.9 %collective-permute-start.3 = (bf16[1,2048,384]{2,1,0:T(8,128)(2,1)}, bf16[1,2048,384]{2,1,0:T(8,128)(2,1)}, u32[]{:S(2)}, u32[]{:S(2)}) collective-permute-start(bf16[1,2048,384]{2,1,0:T(8,128)(2,1)} %refs_0_.1), channel_id=1, source_target_pairs={{0,1},{1,0},{2,3},{3,2},{4,5},{5,4},{6,7},{7,6},{8,9},{9,8},{10,11... | collective-permute-start | bytes 4718600 | tf_op jit(solution)/shard_map/ppermute | solution.py:245
  10.0 2.4 %collective-permute-start.4 = (bf16[1,2048,384]{2,1,0:T(8,128)(2,1)}, bf16[1,2048,384]{2,1,0:T(8,128)(2,1)}, u32[]{:S(2)}, u32[]{:S(2)}) collective-permute-start(bf16[1,2048,384]{2,1,0:T(8,128)(2,1)} %refs_1_.1), channel_id=1, source_target_pairs={{0,1},{1,0},{2,3},{3,2},{4,5},{5,4},{6,7},{7,6},{8,9},{9,8},{10,11... | collective-permute-start | bytes 4718600 | tf_op jit(solution)/shard_map/ppermute | solution.py:245
  12.4 1.9 %collective-permute-start.5 = (bf16[1,384,2048]{2,1,0:T(8,128)(2,1)}, bf16[1,384,2048]{2,1,0:T(8,128)(2,1)}, u32[]{:S(2)}, u32[]{:S(2)}) collective-permute-start(bf16[1,384,2048]{2,1,0:T(8,128)(2,1)} %refs_2_.3), channel_id=1, source_target_pairs={{0,1},{1,0},{2,3},{3,2},{4,5},{5,4},{6,7},{7,6},{8,9},{9,8},{10,11... | collective-permute-start | bytes 4718600 | tf_op jit(solution)/shard_map/ppermute | solution.py:245
  14.3 0.6 dequant.1
  14.9 4.3 %collective-permute-start = (bf16[16,2048]{1,0:T(8,128)(2,1)S(1)}, bf16[16,2048]{1,0:T(8,128)(2,1)S(1)}, u32[]{:S(2)}, u32[]{:S(2)}) collective-permute-start(bf16[16,2048]{1,0:T(8,128)(2,1)S(1)} %get-tuple-element.20), channel_id=1, source_target_pairs={{0,32},{32,64},{64,96},{96,0},{1,33},{33,65},{65,97},{97,1},{2,34}... | collective-permute-start | bytes 196616 | tf_op jit(solution)/shard_map/ppermute | solution.py:245
  19.2 6.1 %collective-permute-start.1 = (bf16[16,2048]{1,0:T(8,128)(2,1)S(1)}, bf16[16,2048]{1,0:T(8,128)(2,1)S(1)}, u32[]{:S(2)}, u32[]{:S(2)}) collective-permute-start(bf16[16,2048]{1,0:T(8,128)(2,1)S(1)} %get-tuple-element.21), channel_id=1, source_target_pairs={{0,64},{32,96},{64,0},{96,32},{1,65},{33,97},{65,1},{97,33},{2,66}... | collective-permute-start | bytes 196616 | tf_op jit(solution)/shard_map/ppermute | solution.py:245
  25.3 0.3 collective-permute-done.refs_1_
  25.6 3.6 %collective-permute-start.2 = (bf16[16,2048]{1,0:T(8,128)(2,1)S(1)}, bf16[16,2048]{1,0:T(8,128)(2,1)S(1)}, u32[]{:S(2)}, u32[]{:S(2)}) collective-permute-start(bf16[16,2048]{1,0:T(8,128)(2,1)S(1)} %get-tuple-element.22), channel_id=1, source_target_pairs={{0,96},{32,0},{64,32},{96,64},{1,97},{33,1},{65,33},{97,65},{2,98}... | collective-permute-start | bytes 196616 | tf_op jit(solution)/shard_map/ppermute | solution.py:245
  29.2 2.5 %collective-permute-done.2.refs_3_ = bf16[16,2048]{1,0:T(8,128)(2,1)S(1)} collective-permute-done((bf16[16,2048]{1,0:T(8,128)(2,1)S(1)}, bf16[16,2048]{1,0:T(8,128)(2,1)S(1)}, u32[]{:S(2)}, u32[]{:S(2)}) %collective-permute-start.2) | collective-permute-done | bytes 65568 | tf_op jit(solution)/shard_map/ppermute | solution.py:245
  31.8 11.8 %collective-permute-start.6 = (bf16[16,2048]{1,0:T(8,128)(2,1)S(1)}, bf16[16,2048]{1,0:T(8,128)(2,1)S(1)}, u32[]{:S(2)}, u32[]{:S(2)}) collective-permute-start(bf16[16,2048]{1,0:T(8,128)(2,1)S(1)} %add_parts.2.refs_0_), channel_id=1, source_target_pairs={{0,512},{512,0},{1,513},{513,1},{2,514},{514,2},{3,515},{515,3},{4... | collective-permute-start | bytes 196616 | tf_op jit(solution)/shard_map/ppermute | solution.py:245
  43.6 7.9 %expert_rows.1 = bf16[256,2048]{1,0:T(8,128)(2,1)} custom-call(bf16[256,2048]{1,0:T(8,128)(2,1)} %bitcast.3.rows_ref, bf16[1,2048,384]{2,1,0:T(8,128)(2,1)} %refs_0_.1, bf16[1,2048,384]{2,1,0:T(8,128)(2,1)} %refs_1_.1, bf16[1,384,2048]{2,1,0:T(8,128)(2,1)} %refs_2_.3, bf16[1,2048,384]{2,1,0:T(8,128)(2,1)} %collective-permute-done.3.refs_3_, ...), custom_call_target="tpu_custom_call" | custom-call | tf_op jit(solution)/shard_map/expert_rows/pallas_call | solution.py:110
  51.5 0.0 copy-start.3
  51.5 7.5 %all-to-all-start.1 = ((bf16[16,16,2048]{2,1,0:T(8,128)(2,1)}), bf16[16,16,2048]{2,1,0:T(8,128)(2,1)S(1)}, u32[]{:S(2)}, u32[]{:S(2)}) async-start(bf16[16,16,2048]{2,1,0:T(8,128)(2,1)} %bitcast.14), calls=%async_computation.1 | async-start | bytes 2097152 | tf_op jit(solution)/shard_map/all_to_all | solution.py:258
  59.0 0.0 copy-start
  59.1 0.0 copy-start.1
  59.1 22.0 %all-gather = bf16[64,2048]{1,0:T(8,128)(2,1)S(1)} all-gather(bf16[16,2048]{1,0:T(8,128)(2,1)S(1)} %add_parts.3), channel_id=2, replica_groups=mesh['y_far'=2,'z_far'=4,'z_near'=4,'chip'=16,'core'=2] {'z_far'}, dimensions={0}, use_global_device_ids=true | all-gather | bytes 327680 | tf_op jit(solution)/shard_map/all_gather | solution.py:289
  81.1 0.7 total_spread.1
  81.8 3.4 %all-to-all-done.1 = bf16[16,16,2048]{2,1,0:T(8,128)(2,1)S(1)} async-done(((bf16[16,16,2048]{2,1,0:T(8,128)(2,1)}), bf16[16,16,2048]{2,1,0:T(8,128)(2,1)S(1)}, u32[]{:S(2)}, u32[]{:S(2)}) %all-to-all-start.1) | async-done | bytes 1048608 | tf_op jit(solution)/shard_map/all_to_all | solution.py:258
  85.2 3.4 %all-to-all-start.2 = ((bf16[4,16,2048]{2,1,0:T(8,128)(2,1)}), bf16[4,16,2048]{2,1,0:T(8,128)(2,1)S(1)}, u32[]{:S(2)}, u32[]{:S(2)}) async-start(bf16[4,16,2048]{2,1,0:T(8,128)(2,1)} %total_spread.1), calls=%async_computation.2 | async-start | bytes 524288 | tf_op jit(solution)/shard_map/all_to_all | solution.py:291
  89.3 1.1 %combine_rows.1 = bf16[128,2048]{1,0:T(8,128)(2,1)} custom-call(bf16[256,128]{1,0:T(8,128)(2,1)S(1)} %copy-done.3, bf16[256,2048]{1,0:T(8,128)(2,1)S(1)} %bitcast.11), custom_call_target="tpu_custom_call" | custom-call | tf_op jit(solution)/shard_map/combine_rows/pallas_call | solution.py:131
  90.4 6.4 %all-to-all-done.2.totals_ref = bf16[4,16,2048]{2,1,0:T(8,128)(2,1)S(1)} async-done(((bf16[4,16,2048]{2,1,0:T(8,128)(2,1)}), bf16[4,16,2048]{2,1,0:T(8,128)(2,1)S(1)}, u32[]{:S(2)}, u32[]{:S(2)}) %all-to-all-start.2) | async-done | bytes 262176 | tf_op jit(solution)/shard_map/all_to_all | solution.py:291
  96.8 1.1 %update.1 = (f32[64,2048]{1,0:T(8,128)}, f32[64,2048]{1,0:T(8,128)}) custom-call(s32[1]{0:T(128)S(6)} %copy.14.fragment_ref, bf16[4,16,2048]{2,1,0:T(8,128)(2,1)S(1)} %all-to-all-done.2.totals_ref, f32[3,64,2048]{2,1,0:T(8,128)S(1)} %copy-done, f32[64,2048]{1,0:T(8,128)S(1)} %copy-done.1), custom_call_target="tpu_custom_call" | custom-call | tf_op jit(solution)/shard_map/update/pallas_call | solution.py:222
  (15 shorter events, 0.1 us)
Async XLA Ops:
  0.6 13.7 %copy-start.2 = (bf16[1,64,2048]{2,1,0:T(8,128)(2,1)S(1)}, bf16[1,64,2048]{2,1,0:T(8,128)(2,1)}, u32[]{:S(2)}) copy-start(bf16[1,64,2048]{2,1,0:T(8,128)(2,1)} %values_ref.1) | copy-start | bytes 786436
  0.6 13.7 %copy-start.4 = (f32[1,64,16]{1,2,0:T(8,128)S(1)}, f32[1,64,16]{1,2,0:T(8,128)}, u32[]{:S(2)}) copy-start(f32[1,64,16]{1,2,0:T(8,128)} %param.18) | copy-start | bytes 12292
  3.2 40.3 %all-to-all-start = ((bf16[16,16,2048]{2,1,0:T(8,128)(2,1)}), bf16[16,16,2048]{2,1,0:T(8,128)(2,1)}, u32[]{:S(2)}, u32[]{:S(2)}) async-start(bf16[16,16,2048]{2,1,0:T(8,128)(2,1)} %bitcast.15), calls=%async_computation | async-start | bytes 2097152 | tf_op jit(solution)/shard_map/all_to_all | solution.py:258
  8.0 35.5 %collective-permute-start.3 = (bf16[1,2048,384]{2,1,0:T(8,128)(2,1)}, bf16[1,2048,384]{2,1,0:T(8,128)(2,1)}, u32[]{:S(2)}, u32[]{:S(2)}) collective-permute-start(bf16[1,2048,384]{2,1,0:T(8,128)(2,1)} %refs_0_.1), channel_id=1, source_target_pairs={{0,1},{1,0},{2,3},{3,2},{4,5},{5,4},{6,7},{7,6},{8,9},{9,8},{10,11... | collective-permute-start | bytes 4718600 | tf_op jit(solution)/shard_map/ppermute | solution.py:245
  10.0 33.6 %collective-permute-start.4 = (bf16[1,2048,384]{2,1,0:T(8,128)(2,1)}, bf16[1,2048,384]{2,1,0:T(8,128)(2,1)}, u32[]{:S(2)}, u32[]{:S(2)}) collective-permute-start(bf16[1,2048,384]{2,1,0:T(8,128)(2,1)} %refs_1_.1), channel_id=1, source_target_pairs={{0,1},{1,0},{2,3},{3,2},{4,5},{5,4},{6,7},{7,6},{8,9},{9,8},{10,11... | collective-permute-start | bytes 4718600 | tf_op jit(solution)/shard_map/ppermute | solution.py:245
  12.4 31.2 %collective-permute-start.5 = (bf16[1,384,2048]{2,1,0:T(8,128)(2,1)}, bf16[1,384,2048]{2,1,0:T(8,128)(2,1)}, u32[]{:S(2)}, u32[]{:S(2)}) collective-permute-start(bf16[1,384,2048]{2,1,0:T(8,128)(2,1)} %refs_2_.3), channel_id=1, source_target_pairs={{0,1},{1,0},{2,3},{3,2},{4,5},{5,4},{6,7},{7,6},{8,9},{9,8},{10,11... | collective-permute-start | bytes 4718600 | tf_op jit(solution)/shard_map/ppermute | solution.py:245
  14.9 10.6 %collective-permute-start = (bf16[16,2048]{1,0:T(8,128)(2,1)S(1)}, bf16[16,2048]{1,0:T(8,128)(2,1)S(1)}, u32[]{:S(2)}, u32[]{:S(2)}) collective-permute-start(bf16[16,2048]{1,0:T(8,128)(2,1)S(1)} %get-tuple-element.20), channel_id=1, source_target_pairs={{0,32},{32,64},{64,96},{96,0},{1,33},{33,65},{65,97},{97,1},{2,34}... | collective-permute-start | bytes 196616 | tf_op jit(solution)/shard_map/ppermute | solution.py:245
  19.2 10.0 %collective-permute-start.1 = (bf16[16,2048]{1,0:T(8,128)(2,1)S(1)}, bf16[16,2048]{1,0:T(8,128)(2,1)S(1)}, u32[]{:S(2)}, u32[]{:S(2)}) collective-permute-start(bf16[16,2048]{1,0:T(8,128)(2,1)S(1)} %get-tuple-element.21), channel_id=1, source_target_pairs={{0,64},{32,96},{64,0},{96,32},{1,65},{33,97},{65,1},{97,33},{2,66}... | collective-permute-start | bytes 196616 | tf_op jit(solution)/shard_map/ppermute | solution.py:245
  25.6 6.1 %collective-permute-start.2 = (bf16[16,2048]{1,0:T(8,128)(2,1)S(1)}, bf16[16,2048]{1,0:T(8,128)(2,1)S(1)}, u32[]{:S(2)}, u32[]{:S(2)}) collective-permute-start(bf16[16,2048]{1,0:T(8,128)(2,1)S(1)} %get-tuple-element.22), channel_id=1, source_target_pairs={{0,96},{32,0},{64,32},{96,64},{1,97},{33,1},{65,33},{97,65},{2,98}... | collective-permute-start | bytes 196616 | tf_op jit(solution)/shard_map/ppermute | solution.py:245
  31.8 19.7 %collective-permute-start.6 = (bf16[16,2048]{1,0:T(8,128)(2,1)S(1)}, bf16[16,2048]{1,0:T(8,128)(2,1)S(1)}, u32[]{:S(2)}, u32[]{:S(2)}) collective-permute-start(bf16[16,2048]{1,0:T(8,128)(2,1)S(1)} %add_parts.2.refs_0_), channel_id=1, source_target_pairs={{0,512},{512,0},{1,513},{513,1},{2,514},{514,2},{3,515},{515,3},{4... | collective-permute-start | bytes 196616 | tf_op jit(solution)/shard_map/ppermute | solution.py:245
  51.5 37.8 %copy-start.3 = (bf16[256,128]{1,0:T(8,128)(2,1)S(1)}, bf16[256,128]{1,0:T(8,128)(2,1)}, u32[]{:S(2)}) copy-start(bf16[256,128]{1,0:T(8,128)(2,1)} %get-tuple-element.17.combine_ref) | copy-start | bytes 196612
  51.5 33.7 %all-to-all-start.1 = ((bf16[16,16,2048]{2,1,0:T(8,128)(2,1)}), bf16[16,16,2048]{2,1,0:T(8,128)(2,1)S(1)}, u32[]{:S(2)}, u32[]{:S(2)}) async-start(bf16[16,16,2048]{2,1,0:T(8,128)(2,1)} %bitcast.14), calls=%async_computation.1 | async-start | bytes 2097152 | tf_op jit(solution)/shard_map/all_to_all | solution.py:258
  59.0 37.7 %copy-start = (f32[3,64,2048]{2,1,0:T(8,128)S(1)}, f32[3,64,2048]{2,1,0:T(8,128)}, u32[]{:S(2)}) copy-start(f32[3,64,2048]{2,1,0:T(8,128)} %base_ref.1) | copy-start | bytes 4718596
  59.1 37.7 %copy-start.1 = (f32[64,2048]{1,0:T(8,128)S(1)}, f32[64,2048]{1,0:T(8,128)}, u32[]{:S(2)}) copy-start(f32[64,2048]{1,0:T(8,128)} %momentum_ref.1) | copy-start | bytes 1572868
  85.2 11.6 %all-to-all-start.2 = ((bf16[4,16,2048]{2,1,0:T(8,128)(2,1)}), bf16[4,16,2048]{2,1,0:T(8,128)(2,1)S(1)}, u32[]{:S(2)}, u32[]{:S(2)}) async-start(bf16[4,16,2048]{2,1,0:T(8,128)(2,1)} %total_spread.1), calls=%async_computation.2 | async-start | bytes 524288 | tf_op jit(solution)/shard_map/all_to_all | solution.py:291

commit v8 on v7

--- a/solution.py
+++ b/solution.py
@@ -15,7 +15,7 @@
 outer_rate = 0.7
 
 ROUTE_PARAMS = pltpu.CompilerParams(vmem_limit_bytes=62 * 1024 * 1024)
-EXPERT_PARAMS = pltpu.CompilerParams(vmem_limit_bytes=62 * 1024 * 1024)
+EXPERT_PARAMS = pltpu.CompilerParams(vmem_limit_bytes=63 * 1024 * 1024)
 PARAMS = pltpu.CompilerParams(vmem_limit_bytes=20 * 1024 * 1024)
 VMEM = pl.BlockSpec(memory_space=pltpu.VMEM)
 HBM = pl.BlockSpec(memory_space=pltpu.HBM)
@@ -83,39 +83,57 @@
     )(*operands)
 
 
-def expert_kernel(rows_ref, *refs):
-    sources, out_ref, targets, sems = refs[:6], refs[6], refs[7:13], refs[13]
+def expert_kernel(rows_hbm, *refs):
+    sources, out_ref, targets, sems = refs[:6], refs[6], refs[7:11], refs[11]
+    rows_ref, gate_ref, up_ref, down_ref = targets
+    half = gate_ref.shape[1] // 2
+    moves = [(rows_hbm, rows_ref)]
+    for kind, target in enumerate((gate_ref, up_ref, down_ref)):
+        for side in range(2):
+            span = pl.ds(side * half, half)
+            source = sources[3 * side + kind].at[0]
+            moves.append((source, target.at[span] if kind == 2 else target.at[:, span]))
     fetches = [
         pltpu.make_async_copy(source, target, sems.at[i])
-        for i, (source, target) in enumerate(zip(sources, targets))
+        for i, (source, target) in enumerate(moves)
     ]
-    for fetch in fetches:
+    for fetch in fetches[:5]:
+        fetch.start()
+    for fetch in fetches[:3]:
+        fetch.wait()
+    for fetch in fetches[5:]:
         fetch.start()
     rows = rows_ref[...]
-    total = None
-    for first in (0, 3):
-        fetches[first].wait()
-        gate = jnp.dot(rows, targets[first][0], preferred_element_type=jnp.float32)
-        fetches[first + 1].wait()
-        up = jnp.dot(rows, targets[first + 1][0], preferred_element_type=jnp.float32)
-        hidden = (gate / (1.0 + jnp.exp(-gate)) * up).astype(jnp.bfloat16)
-        fetches[first + 2].wait()
-        part = jnp.dot(hidden, targets[first + 2][0], preferred_element_type=jnp.float32)
-        total = part if total is None else total + part
-    out_ref[...] = total.astype(jnp.bfloat16)
+    gate = jnp.dot(rows, gate_ref[...], preferred_element_type=jnp.float32)
+    for fetch in fetches[3:5]:
+        fetch.wait()
+    up = jnp.dot(rows, up_ref[...], preferred_element_type=jnp.float32)
+    hidden = (gate / (1.0 + jnp.exp(-gate)) * up).astype(jnp.bfloat16)
+    for fetch in fetches[5:]:
+        fetch.wait()
+    out_ref[...] = jnp.dot(hidden, down_ref[...], preferred_element_type=jnp.float32).astype(
+        jnp.bfloat16
+    )
 
 
 def expert_rows(rows, own, other):
-    weights = own + other
+    operands = (rows,) + own + other
+    _, width, half = own[0].shape
+    wide = pltpu.VMEM((width, 2 * half), jnp.bfloat16)
     return pl.pallas_call(
         expert_kernel,
-        in_specs=[VMEM] + [HBM] * len(weights),
+        in_specs=[HBM] * len(operands),
         out_shape=jax.ShapeDtypeStruct(rows.shape, jnp.bfloat16),
-        scratch_shapes=[pltpu.VMEM(x.shape, x.dtype) for x in weights]
-        + [pltpu.SemaphoreType.DMA((len(weights),))],
+        scratch_shapes=[
+            pltpu.VMEM(rows.shape, rows.dtype),
+            wide,
+            wide,
+            pltpu.VMEM((2 * half, width), jnp.bfloat16),
+            pltpu.SemaphoreType.DMA((len(operands),)),
+        ],
         compiler_params=EXPERT_PARAMS,
         name="expert_rows",
-    )(rows, *weights)
+    )(*operands)
 
 
 def combine_kernel(combine_ref, rows_ref, out_ref):
@@ -188,45 +206,53 @@
 
 
 def total_kernel(parts_ref, out_ref):
-    total = jnp.sum(parts_ref[...].astype(jnp.float32), axis=0).astype(jnp.bfloat16)
-    out_ref[...] = jnp.broadcast_to(total[None], out_ref.shape)
-
-
-def total_spread(parts):
+    out_ref[...] = jnp.sum(parts_ref[...].astype(jnp.float32), axis=0).astype(jnp.bfloat16)
+
+
+def total(parts):
     return pl.pallas_call(
         total_kernel,
-        out_shape=jax.ShapeDtypeStruct((RADIX,) + parts.shape[1:], jnp.bfloat16),
-        compiler_params=PARAMS,
-        name="total_spread",
+        out_shape=jax.ShapeDtypeStruct(parts.shape[1:], jnp.bfloat16),
+        compiler_params=PARAMS,
+        name="total",
     )(parts)
 
 
-def update_kernel(replicas, fragment_ref, totals_ref, base_ref, momentum_ref, params_out, momentum_out):
-    pieces, rows, _ = totals_ref.shape
-    for piece in range(pieces):
-        at = pl.ds(piece * rows, rows)
-        delta = totals_ref[piece].astype(jnp.float32) / replicas
-        new_momentum = momentum_rate * momentum_ref[at, :] + delta
-        momentum_out[at, :] = new_momentum
-        params_out[at, :] = base_ref[0, at, :] - outer_rate * (
-            delta + momentum_rate * new_momentum
-        )
-
-
-def update(replicas, totals, outer_params, momentum, fragment):
+def update_kernel(replicas, fragment_ref, place_ref, *refs):
+    part_refs = refs[:RADIX]
+    base_ref, momentum_ref, params_out, momentum_out = refs[RADIX:]
+    rows = part_refs[0].shape[0]
+    for place in range(RADIX):
+        for step, ref in enumerate(part_refs):
+
+            @pl.when((place_ref[0] + RADIX - step) % RADIX == place)
+            def _():
+                span = pl.ds(place * rows, rows)
+                delta = ref[...].astype(jnp.float32) / replicas
+                new_momentum = momentum_rate * momentum_ref[span, :] + delta
+                momentum_out[span, :] = new_momentum
+                params_out[span, :] = base_ref[0, span, :] - outer_rate * (
+                    delta + momentum_rate * new_momentum
+                )
+
+
+def update(replicas, place, parts, outer_params, momentum, fragment):
     shape = momentum.shape
+    part = parts[0].shape
 
     def whole(block):
-        return pl.BlockSpec(block, lambda i, fragment_ref: (0,) * len(block))
+        return pl.BlockSpec(block, lambda i, fragment_ref, place_ref: (0,) * len(block))
 
     return pl.pallas_call(
         functools.partial(update_kernel, replicas),
         grid_spec=pltpu.PrefetchScalarGridSpec(
-            num_scalar_prefetch=1,
+            num_scalar_prefetch=2,
             grid=(1,),
-            in_specs=[
-                whole(totals.shape),
-                pl.BlockSpec((1,) + shape, lambda i, fragment_ref: (fragment_ref[0], 0, 0)),
+            in_specs=[whole(part)] * RADIX
+            + [
+                pl.BlockSpec(
+                    (1,) + shape, lambda i, fragment_ref, place_ref: (fragment_ref[0], 0, 0)
+                ),
                 whole(shape),
             ],
             out_specs=(whole(shape), whole(shape)),
@@ -237,7 +263,7 @@
         ),
         compiler_params=PARAMS,
         name="update",
-    )(fragment, totals, outer_params, momentum)
+    )(fragment, place, *parts, outer_params, momentum)
 
 
 def shift(part, axis, step):
@@ -247,6 +273,10 @@
 
 def scatter_stage(parts, axis):
     return [parts[0]] + [shift(parts[step], axis, step) for step in range(1, RADIX)]
+
+
+def gather_stage(part, axis):
+    return [part] + [shift(part, axis, step) for step in range(1, RADIX)]
 
 
 def place_on(axis):
@@ -286,12 +316,12 @@
     rows, apart = lax.optimization_barrier((rows, apart))
     part = add_parts([part, apart])
     returned = exchange(rows, experts)
-    spread = total_spread(lax.all_gather(part, "z_far", axis=0))
-    returned, spread = lax.optimization_barrier((returned, spread))
-    totals = lax.all_to_all(spread, "z_near", split_axis=0, concat_axis=0, tiled=True)
+    sums = total(lax.all_gather(part, "z_far", axis=0))
+    parts = gather_stage(sums, "z_near")
     moe_out = combine_rows(combine, returned)
+    parts[0], moe_out = lax.optimization_barrier((parts[0], moe_out))
     new_params, new_momentum = update(
-        lax.axis_size(("y_far", "z_far", "z_near")), totals, outer_params, momentum, fragment
+        lax.axis_size(("y_far", "z_far", "z_near")), near, parts, outer_params, momentum, fragment
     )
     return (moe_out, new_params, new_momentum)
 

time: 98.5 us -> 97.7 us (level)
  the two profiles are of different devices: /device:TPU:32 before, /device:TPU:6 now
where the time goes in v8:
time: 97.7 us; the launch traced here: 97.1 us
  starting transfers between devices  47.6 us (49%)
  blocking collectives  23.4 us (24%)
  Pallas kernels  12.4 us (13%)
  waiting for transfers between devices  12.2 us (12%)
  between operations  1.51 us (2%)
    all_to_all x2, starting transfers between devices, exchange(): lax.all_to_all(rows.reshape(experts, CAP, width), 'chip', split_axis=0, c...  24.1 us
    ppermute x10, starting transfers between devices, shift(): lax.ppermute(part, axis, [(i, (i + step) % size) for i in range(size)])  23.5 us
    all_gather x1, blocking collectives, shards(): sums = total(lax.all_gather(part, 'z_far', axis=0))  23.4 us
    ppermute x10, waiting for transfers between devices, shift(): lax.ppermute(part, axis, [(i, (i + step) % size) for i in range(size)])  12.2 us
    pallas_call x1, Pallas kernels, expert_rows(): pl.pallas_call(expert_kernel, in_specs=[HBM] * len(operands), out_shape=j...  6.73 us
    pallas_call x1, Pallas kernels, route(): pl.pallas_call(functools.partial(route_kernel, experts), out_shape=(jax.S...  2.56 us
  transfers between devices with their start and end apart: 12, of which 5 were waited for; matrix products, arithmetic and copies ran while one was open for 0% of the time, Pallas kernels for 9%

profile of v8, /device:TPU:6, one launch (start us, length us, event | category | flops | bytes accessed | tf_op | source)
XLA Modules:
  0.0 97.1 jit_solution(11149425110010212907)
XLA Ops:
  0.7 2.6 %route.1 = (bf16[256,2048]{1,0:T(8,128)(2,1)}, bf16[256,128]{1,0:T(8,128)(2,1)}) custom-call(s32[8,128]{1,0:T(8,128)} %bitcast.16, f32[8,128]{1,0:T(8,128)} %bitcast.17, bf16[128,2048]{1,0:T(8,128)(2,1)} %refs_2_.2), custom_call_target="tpu_custom_call" | custom-call | tf_op jit(solution)/shard_map/route/pallas_call | solution.py:72
  3.2 17.3 %all-to-all-start = ((bf16[16,16,2048]{2,1,0:T(8,128)(2,1)}), bf16[16,16,2048]{2,1,0:T(8,128)(2,1)}, u32[]{:S(2)}, u32[]{:S(2)}) async-start(bf16[16,16,2048]{2,1,0:T(8,128)(2,1)} %bitcast.15), calls=%async_computation | async-start | bytes 2097152 | tf_op jit(solution)/shard_map/all_to_all | solution.py:288
  20.5 1.9 %collective-permute-start.3 = (bf16[1,2048,384]{2,1,0:T(8,128)(2,1)}, bf16[1,2048,384]{2,1,0:T(8,128)(2,1)}, u32[]{:S(2)}, u32[]{:S(2)}) collective-permute-start(bf16[1,2048,384]{2,1,0:T(8,128)(2,1)} %refs_0_.1), channel_id=1, source_target_pairs={{0,1},{1,0},{2,3},{3,2},{4,5},{5,4},{6,7},{7,6},{8,9},{9,8},{10,11... | collective-permute-start | bytes 4718600 | tf_op jit(solution)/shard_map/ppermute | solution.py:271
  22.4 2.4 %collective-permute-start.4 = (bf16[1,2048,384]{2,1,0:T(8,128)(2,1)}, bf16[1,2048,384]{2,1,0:T(8,128)(2,1)}, u32[]{:S(2)}, u32[]{:S(2)}) collective-permute-start(bf16[1,2048,384]{2,1,0:T(8,128)(2,1)} %refs_1_.1), channel_id=1, source_target_pairs={{0,1},{1,0},{2,3},{3,2},{4,5},{5,4},{6,7},{7,6},{8,9},{9,8},{10,11... | collective-permute-start | bytes 4718600 | tf_op jit(solution)/shard_map/ppermute | solution.py:271
  24.8 1.9 %collective-permute-start.5 = (bf16[1,384,2048]{2,1,0:T(8,128)(2,1)}, bf16[1,384,2048]{2,1,0:T(8,128)(2,1)}, u32[]{:S(2)}, u32[]{:S(2)}) collective-permute-start(bf16[1,384,2048]{2,1,0:T(8,128)(2,1)} %refs_2_.3), channel_id=1, source_target_pairs={{0,1},{1,0},{2,3},{3,2},{4,5},{5,4},{6,7},{7,6},{8,9},{9,8},{10,11... | collective-permute-start | bytes 4718600 | tf_op jit(solution)/shard_map/ppermute | solution.py:271
  26.8 0.6 dequant.1
  27.4 1.9 %collective-permute-start = (bf16[16,2048]{1,0:T(8,128)(2,1)S(1)}, bf16[16,2048]{1,0:T(8,128)(2,1)S(1)}, u32[]{:S(2)}, u32[]{:S(2)}) collective-permute-start(bf16[16,2048]{1,0:T(8,128)(2,1)S(1)} %get-tuple-element.19), channel_id=1, source_target_pairs={{0,32},{32,64},{64,96},{96,0},{1,33},{33,65},{65,97},{97,1},{2,34}... | collective-permute-start | bytes 196616 | tf_op jit(solution)/shard_map/ppermute | solution.py:271
  29.3 1.9 %collective-permute-start.1 = (bf16[16,2048]{1,0:T(8,128)(2,1)S(1)}, bf16[16,2048]{1,0:T(8,128)(2,1)S(1)}, u32[]{:S(2)}, u32[]{:S(2)}) collective-permute-start(bf16[16,2048]{1,0:T(8,128)(2,1)S(1)} %get-tuple-element.20), channel_id=1, source_target_pairs={{0,64},{32,96},{64,0},{96,32},{1,65},{33,97},{65,1},{97,33},{2,66}... | collective-permute-start | bytes 196616 | tf_op jit(solution)/shard_map/ppermute | solution.py:271
  31.2 4.4 %collective-permute-done.refs_1_ = bf16[16,2048]{1,0:T(8,128)(2,1)S(1)} collective-permute-done((bf16[16,2048]{1,0:T(8,128)(2,1)S(1)}, bf16[16,2048]{1,0:T(8,128)(2,1)S(1)}, u32[]{:S(2)}, u32[]{:S(2)}) %collective-permute-start) | collective-permute-done | bytes 65568 | tf_op jit(solution)/shard_map/ppermute | solution.py:271
  35.6 1.9 %collective-permute-start.2 = (bf16[16,2048]{1,0:T(8,128)(2,1)S(1)}, bf16[16,2048]{1,0:T(8,128)(2,1)S(1)}, u32[]{:S(2)}, u32[]{:S(2)}) collective-permute-start(bf16[16,2048]{1,0:T(8,128)(2,1)S(1)} %get-tuple-element.21), channel_id=1, source_target_pairs={{0,96},{32,0},{64,32},{96,64},{1,97},{33,1},{65,33},{97,65},{2,98}... | collective-permute-start | bytes 196616 | tf_op jit(solution)/shard_map/ppermute | solution.py:271
  37.5 0.9 collective-permute-done.1.refs_2_
  38.4 3.4 %collective-permute-done.2.refs_3_ = bf16[16,2048]{1,0:T(8,128)(2,1)S(1)} collective-permute-done((bf16[16,2048]{1,0:T(8,128)(2,1)S(1)}, bf16[16,2048]{1,0:T(8,128)(2,1)S(1)}, u32[]{:S(2)}, u32[]{:S(2)}) %collective-permute-start.2) | collective-permute-done | bytes 65568 | tf_op jit(solution)/shard_map/ppermute | solution.py:271
  41.8 1.9 %collective-permute-start.6 = (bf16[16,2048]{1,0:T(8,128)(2,1)S(1)}, bf16[16,2048]{1,0:T(8,128)(2,1)S(1)}, u32[]{:S(2)}, u32[]{:S(2)}) collective-permute-start(bf16[16,2048]{1,0:T(8,128)(2,1)S(1)} %add_parts.2.refs_0_), channel_id=1, source_target_pairs={{0,512},{512,0},{1,513},{513,1},{2,514},{514,2},{3,515},{515,3},{4... | collective-permute-start | bytes 196616 | tf_op jit(solution)/shard_map/ppermute | solution.py:271
  43.8 6.7 %expert_rows.1 = bf16[256,2048]{1,0:T(8,128)(2,1)} custom-call(bf16[256,2048]{1,0:T(8,128)(2,1)} %bitcast.3.rows_hbm, bf16[1,2048,384]{2,1,0:T(8,128)(2,1)} %refs_0_.1, bf16[1,2048,384]{2,1,0:T(8,128)(2,1)} %refs_1_.1, bf16[1,384,2048]{2,1,0:T(8,128)(2,1)} %refs_2_.3, bf16[1,2048,384]{2,1,0:T(8,128)(2,1)} %collective-permute-done.3.refs_3_, ...), custom_call_target="tpu_custom_call" | custom-call | tf_op jit(solution)/shard_map/expert_rows/pallas_call | solution.py:123
  50.5 0.0 copy-start.3
  50.5 2.1 %collective-permute-done.6.refs_1_ = bf16[16,2048]{1,0:T(8,128)(2,1)S(1)} collective-permute-done((bf16[16,2048]{1,0:T(8,128)(2,1)S(1)}, bf16[16,2048]{1,0:T(8,128)(2,1)S(1)}, u32[]{:S(2)}, u32[]{:S(2)}) %collective-permute-start.6) | collective-permute-done | bytes 65568 | tf_op jit(solution)/shard_map/ppermute | solution.py:271
  52.6 6.8 %all-to-all-start.1 = ((bf16[16,16,2048]{2,1,0:T(8,128)(2,1)}), bf16[16,16,2048]{2,1,0:T(8,128)(2,1)S(1)}, u32[]{:S(2)}, u32[]{:S(2)}) async-start(bf16[16,16,2048]{2,1,0:T(8,128)(2,1)} %bitcast.14), calls=%async_computation.1 | async-start | bytes 2097152 | tf_op jit(solution)/shard_map/all_to_all | solution.py:288
  59.4 23.4 %all-gather = bf16[64,2048]{1,0:T(8,128)(2,1)S(1)} all-gather(bf16[16,2048]{1,0:T(8,128)(2,1)S(1)} %add_parts.3), channel_id=2, replica_groups=mesh['y_far'=2,'z_far'=4,'z_near'=4,'chip'=16,'core'=2] {'z_far'}, dimensions={0}, use_global_device_ids=true | all-gather | bytes 327680 | tf_op jit(solution)/shard_map/all_gather | solution.py:319
  82.9 2.5 %collective-permute-start.7 = (bf16[16,2048]{1,0:T(8,128)(2,1)S(1)}, bf16[16,2048]{1,0:T(8,128)(2,1)S(1)}, u32[]{:S(2)}, u32[]{:S(2)}) collective-permute-start(bf16[16,2048]{1,0:T(8,128)(2,1)S(1)} %total.1.refs_0_), channel_id=1, source_target_pairs={{0,32},{32,64},{64,96},{96,0},{1,33},{33,65},{65,97},{97,1},{2,34}... | collective-permute-start | bytes 196616 | tf_op jit(solution)/shard_map/ppermute | solution.py:271
  85.4 4.3 %collective-permute-start.8 = (bf16[16,2048]{1,0:T(8,128)(2,1)S(1)}, bf16[16,2048]{1,0:T(8,128)(2,1)S(1)}, u32[]{:S(2)}, u32[]{:S(2)}) collective-permute-start(bf16[16,2048]{1,0:T(8,128)(2,1)S(1)} %total.1.refs_0_), channel_id=1, source_target_pairs={{0,64},{32,96},{64,0},{96,32},{1,65},{33,97},{65,1},{97,33},{2,66}... | collective-permute-start | bytes 196616 | tf_op jit(solution)/shard_map/ppermute | solution.py:271
  89.6 2.8 %collective-permute-start.9 = (bf16[16,2048]{1,0:T(8,128)(2,1)S(1)}, bf16[16,2048]{1,0:T(8,128)(2,1)S(1)}, u32[]{:S(2)}, u32[]{:S(2)}) collective-permute-start(bf16[16,2048]{1,0:T(8,128)(2,1)S(1)} %total.1.refs_0_), channel_id=1, source_target_pairs={{0,96},{32,0},{64,32},{96,64},{1,97},{33,1},{65,33},{97,65},{2,98}... | collective-permute-start | bytes 196616 | tf_op jit(solution)/shard_map/ppermute | solution.py:271
  93.1 1.1 %combine_rows.1 = bf16[128,2048]{1,0:T(8,128)(2,1)} custom-call(bf16[256,128]{1,0:T(8,128)(2,1)S(1)} %copy-done.3, bf16[256,2048]{1,0:T(8,128)(2,1)S(1)} %bitcast.11), custom_call_target="tpu_custom_call" | custom-call | tf_op jit(solution)/shard_map/combine_rows/pallas_call | solution.py:149
  94.3 1.6 %collective-permute-done.9.refs_3_ = bf16[16,2048]{1,0:T(8,128)(2,1)S(1)} collective-permute-done((bf16[16,2048]{1,0:T(8,128)(2,1)S(1)}, bf16[16,2048]{1,0:T(8,128)(2,1)S(1)}, u32[]{:S(2)}, u32[]{:S(2)}) %collective-permute-start.9) | collective-permute-done | bytes 65568 | tf_op jit(solution)/shard_map/ppermute | solution.py:271
  95.8 1.3 %update.1 = (f32[64,2048]{1,0:T(8,128)}, f32[64,2048]{1,0:T(8,128)}) custom-call(s32[1]{0:T(128)S(6)} %copy.14.fragment_ref, s32[1]{0:T(128)} %bitcast.4.place_ref, bf16[16,2048]{1,0:T(8,128)(2,1)S(1)} %total.1.refs_0_, bf16[16,2048]{1,0:T(8,128)(2,1)S(1)} %collective-permute-done.7.refs_1_, bf16[16,2048]{1,0:T(8,128)(2,1)S(1)} %collective-permute-done.8.refs_2_, ...), custom_call_target="tpu_custom_call" | custom-call | tf_op jit(solution)/shard_map/update/pallas_call | solution.py:246
  (19 shorter events, 0.1 us)
Async XLA Ops:
  0.6 26.1 %copy-start.2 = (bf16[1,64,2048]{2,1,0:T(8,128)(2,1)S(1)}, bf16[1,64,2048]{2,1,0:T(8,128)(2,1)}, u32[]{:S(2)}) copy-start(bf16[1,64,2048]{2,1,0:T(8,128)(2,1)} %values_ref.1) | copy-start | bytes 786436
  0.6 26.1 %copy-start.4 = (f32[1,64,16]{1,2,0:T(8,128)S(1)}, f32[1,64,16]{1,2,0:T(8,128)}, u32[]{:S(2)}) copy-start(f32[1,64,16]{1,2,0:T(8,128)} %param.18) | copy-start | bytes 12292
  3.2 40.5 %all-to-all-start = ((bf16[16,16,2048]{2,1,0:T(8,128)(2,1)}), bf16[16,16,2048]{2,1,0:T(8,128)(2,1)}, u32[]{:S(2)}, u32[]{:S(2)}) async-start(bf16[16,16,2048]{2,1,0:T(8,128)(2,1)} %bitcast.15), calls=%async_computation | async-start | bytes 2097152 | tf_op jit(solution)/shard_map/all_to_all | solution.py:288
  20.5 23.2 %collective-permute-start.3 = (bf16[1,2048,384]{2,1,0:T(8,128)(2,1)}, bf16[1,2048,384]{2,1,0:T(8,128)(2,1)}, u32[]{:S(2)}, u32[]{:S(2)}) collective-permute-start(bf16[1,2048,384]{2,1,0:T(8,128)(2,1)} %refs_0_.1), channel_id=1, source_target_pairs={{0,1},{1,0},{2,3},{3,2},{4,5},{5,4},{6,7},{7,6},{8,9},{9,8},{10,11... | collective-permute-start | bytes 4718600 | tf_op jit(solution)/shard_map/ppermute | solution.py:271
  22.4 21.3 %collective-permute-start.4 = (bf16[1,2048,384]{2,1,0:T(8,128)(2,1)}, bf16[1,2048,384]{2,1,0:T(8,128)(2,1)}, u32[]{:S(2)}, u32[]{:S(2)}) collective-permute-start(bf16[1,2048,384]{2,1,0:T(8,128)(2,1)} %refs_1_.1), channel_id=1, source_target_pairs={{0,1},{1,0},{2,3},{3,2},{4,5},{5,4},{6,7},{7,6},{8,9},{9,8},{10,11... | collective-permute-start | bytes 4718600 | tf_op jit(solution)/shard_map/ppermute | solution.py:271
  24.8 18.9 %collective-permute-start.5 = (bf16[1,384,2048]{2,1,0:T(8,128)(2,1)}, bf16[1,384,2048]{2,1,0:T(8,128)(2,1)}, u32[]{:S(2)}, u32[]{:S(2)}) collective-permute-start(bf16[1,384,2048]{2,1,0:T(8,128)(2,1)} %refs_2_.3), channel_id=1, source_target_pairs={{0,1},{1,0},{2,3},{3,2},{4,5},{5,4},{6,7},{7,6},{8,9},{9,8},{10,11... | collective-permute-start | bytes 4718600 | tf_op jit(solution)/shard_map/ppermute | solution.py:271
  27.4 8.2 %collective-permute-start = (bf16[16,2048]{1,0:T(8,128)(2,1)S(1)}, bf16[16,2048]{1,0:T(8,128)(2,1)S(1)}, u32[]{:S(2)}, u32[]{:S(2)}) collective-permute-start(bf16[16,2048]{1,0:T(8,128)(2,1)S(1)} %get-tuple-element.19), channel_id=1, source_target_pairs={{0,32},{32,64},{64,96},{96,0},{1,33},{33,65},{65,97},{97,1},{2,34}... | collective-permute-start | bytes 196616 | tf_op jit(solution)/shard_map/ppermute | solution.py:271
  29.3 9.1 %collective-permute-start.1 = (bf16[16,2048]{1,0:T(8,128)(2,1)S(1)}, bf16[16,2048]{1,0:T(8,128)(2,1)S(1)}, u32[]{:S(2)}, u32[]{:S(2)}) collective-permute-start(bf16[16,2048]{1,0:T(8,128)(2,1)S(1)} %get-tuple-element.20), channel_id=1, source_target_pairs={{0,64},{32,96},{64,0},{96,32},{1,65},{33,97},{65,1},{97,33},{2,66}... | collective-permute-start | bytes 196616 | tf_op jit(solution)/shard_map/ppermute | solution.py:271
  35.6 6.1 %collective-permute-start.2 = (bf16[16,2048]{1,0:T(8,128)(2,1)S(1)}, bf16[16,2048]{1,0:T(8,128)(2,1)S(1)}, u32[]{:S(2)}, u32[]{:S(2)}) collective-permute-start(bf16[16,2048]{1,0:T(8,128)(2,1)S(1)} %get-tuple-element.21), channel_id=1, source_target_pairs={{0,96},{32,0},{64,32},{96,64},{1,97},{33,1},{65,33},{97,65},{2,98}... | collective-permute-start | bytes 196616 | tf_op jit(solution)/shard_map/ppermute | solution.py:271
  41.8 10.8 %collective-permute-start.6 = (bf16[16,2048]{1,0:T(8,128)(2,1)S(1)}, bf16[16,2048]{1,0:T(8,128)(2,1)S(1)}, u32[]{:S(2)}, u32[]{:S(2)}) collective-permute-start(bf16[16,2048]{1,0:T(8,128)(2,1)S(1)} %add_parts.2.refs_0_), channel_id=1, source_target_pairs={{0,512},{512,0},{1,513},{513,1},{2,514},{514,2},{3,515},{515,3},{4... | collective-permute-start | bytes 196616 | tf_op jit(solution)/shard_map/ppermute | solution.py:271
  50.5 42.6 %copy-start.3 = (bf16[256,128]{1,0:T(8,128)(2,1)S(1)}, bf16[256,128]{1,0:T(8,128)(2,1)}, u32[]{:S(2)}) copy-start(bf16[256,128]{1,0:T(8,128)(2,1)} %get-tuple-element.25.combine_ref) | copy-start | bytes 196612
  52.6 40.5 %all-to-all-start.1 = ((bf16[16,16,2048]{2,1,0:T(8,128)(2,1)}), bf16[16,16,2048]{2,1,0:T(8,128)(2,1)S(1)}, u32[]{:S(2)}, u32[]{:S(2)}) async-start(bf16[16,16,2048]{2,1,0:T(8,128)(2,1)} %bitcast.14), calls=%async_computation.1 | async-start | bytes 2097152 | tf_op jit(solution)/shard_map/all_to_all | solution.py:288
  59.4 36.4 %copy-start = (f32[3,64,2048]{2,1,0:T(8,128)S(1)}, f32[3,64,2048]{2,1,0:T(8,128)}, u32[]{:S(2)}) copy-start(f32[3,64,2048]{2,1,0:T(8,128)} %refs_4_.1) | copy-start | bytes 4718596
  59.4 36.4 %copy-start.1 = (f32[64,2048]{1,0:T(8,128)S(1)}, f32[64,2048]{1,0:T(8,128)}, u32[]{:S(2)}) copy-start(f32[64,2048]{1,0:T(8,128)} %refs_5_.1) | copy-start | bytes 1572868
  82.9 11.4 %collective-permute-start.7 = (bf16[16,2048]{1,0:T(8,128)(2,1)S(1)}, bf16[16,2048]{1,0:T(8,128)(2,1)S(1)}, u32[]{:S(2)}, u32[]{:S(2)}) collective-permute-start(bf16[16,2048]{1,0:T(8,128)(2,1)S(1)} %total.1.refs_0_), channel_id=1, source_target_pairs={{0,32},{32,64},{64,96},{96,0},{1,33},{33,65},{65,97},{97,1},{2,34}... | collective-permute-start | bytes 196616 | tf_op jit(solution)/shard_map/ppermute | solution.py:271
  85.4 8.9 %collective-permute-start.8 = (bf16[16,2048]{1,0:T(8,128)(2,1)S(1)}, bf16[16,2048]{1,0:T(8,128)(2,1)S(1)}, u32[]{:S(2)}, u32[]{:S(2)}) collective-permute-start(bf16[16,2048]{1,0:T(8,128)(2,1)S(1)} %total.1.refs_0_), channel_id=1, source_target_pairs={{0,64},{32,96},{64,0},{96,32},{1,65},{33,97},{65,1},{97,33},{2,66}... | collective-permute-start | bytes 196616 | tf_op jit(solution)/shard_map/ppermute | solution.py:271
  89.6 6.2 %collective-permute-start.9 = (bf16[16,2048]{1,0:T(8,128)(2,1)S(1)}, bf16[16,2048]{1,0:T(8,128)(2,1)S(1)}, u32[]{:S(2)}, u32[]{:S(2)}) collective-permute-start(bf16[16,2048]{1,0:T(8,128)(2,1)S(1)} %total.1.refs_0_), channel_id=1, source_target_pairs={{0,96},{32,0},{64,32},{96,64},{1,97},{33,1},{65,33},{97,65},{2,98}... | collective-permute-start | bytes 196616 | tf_op jit(solution)/shard_map/ppermute | solution.py:271

commit v9 on v8

--- a/solution.py
+++ b/solution.py
@@ -154,9 +154,9 @@
     )(combine, rows)
 
 
-def dequant_kernel(place_ref, values_ref, scales_ref, *out_refs):
-    rows, width = out_refs[0].shape
-    blocks = scales_ref.shape[0]
+def dequant_kernel(near_ref, values_ref, scales_ref, kept_ref, sent_ref):
+    rows = values_ref.shape[1] // RADIX
+    blocks, width = scales_ref.shape[0], values_ref.shape[2]
     column = lax.broadcasted_iota(jnp.int32, (blocks, width), 1) // (width // blocks)
     spread = (column == lax.broadcasted_iota(jnp.int32, (blocks, width), 0)).astype(jnp.bfloat16)
     scales = scales_ref[...]
@@ -171,25 +171,50 @@
         for part in (high, middle, low)
     )
     whole = (values_ref[0].astype(jnp.float32) * wide).astype(jnp.bfloat16)
-    for place in range(RADIX):
-        block = whole[place * rows : (place + 1) * rows]
-        for step, out_ref in enumerate(out_refs):
-
-            @pl.when((place_ref[0] + step) % RADIX == place)
-            def _():
-                out_ref[...] = block
-
-
-def dequant(place, values, scales):
+    for bit in range(2):
+
+        @pl.when(near_ref[0] % 2 == bit)
+        def _():
+            for i in range(RADIX):
+                out_ref = kept_ref if i % 2 == bit else sent_ref
+                out_ref[i // 2 * rows : (i // 2 + 1) * rows] = whole[i * rows : (i + 1) * rows]
+
+
+def dequant(near, values, scales):
     _, rows, width = values.shape
-    part = jax.ShapeDtypeStruct((rows // RADIX, width), jnp.bfloat16)
+    part = jax.ShapeDtypeStruct((rows // 2, width), jnp.bfloat16)
     return pl.pallas_call(
         dequant_kernel,
         in_specs=[SMEM, VMEM, VMEM],
-        out_shape=(part,) * RADIX,
+        out_shape=(part, part),
         compiler_params=PARAMS,
         name="dequant",
-    )(place, values, scales[0].T)
+    )(near, values, scales[0].T)
+
+
+def add_split_kernel(near_ref, kept_ref, got_ref, own_ref, sent_ref):
+    rows = own_ref.shape[0]
+    total = (kept_ref[...].astype(jnp.float32) + got_ref[...].astype(jnp.float32)).astype(
+        jnp.bfloat16
+    )
+    for bit in range(2):
+
+        @pl.when(near_ref[0] // 2 == bit)
+        def _():
+            own_ref[...] = total[bit * rows : (bit + 1) * rows]
+            sent_ref[...] = total[(1 - bit) * rows : (2 - bit) * rows]
+
+
+def add_split(near, kept, got):
+    rows, width = kept.shape
+    part = jax.ShapeDtypeStruct((rows // 2, width), jnp.bfloat16)
+    return pl.pallas_call(
+        add_split_kernel,
+        in_specs=[SMEM, VMEM, VMEM],
+        out_shape=(part, part),
+        compiler_params=PARAMS,
+        name="add_split",
+    )(near, kept, got)
 
 
 def add_kernel(*refs):
@@ -271,8 +296,8 @@
     return lax.ppermute(part, axis, [(i, (i + step) % size) for i in range(size)])
 
 
-def scatter_stage(parts, axis):
-    return [parts[0]] + [shift(parts[step], axis, step) for step in range(1, RADIX)]
+def pair(part, axis, distance):
+    return lax.ppermute(part, axis, [(i, i ^ distance) for i in range(lax.axis_size(axis))])
 
 
 def gather_stage(part, axis):
@@ -308,9 +333,12 @@
     mine = exchange(buffer, experts)
     own = (w_gate, w_up, w_down)
     near = place_on("z_near")
-    part = add_parts(scatter_stage(dequant(near, pseudo_values, block_scales), "z_near"))
+    kept, sent = dequant(near, pseudo_values, block_scales)
+    got = pair(sent, "z_near", 1)
+    other = tuple(shift(w, "core", 1) for w in own)
+    mine_part, sent = add_split(near, kept, got)
+    part = add_parts([mine_part, pair(sent, "z_near", 2)])
     apart = shift(part, "y_far", 1)
-    other = tuple(shift(w, "core", 1) for w in own)
     mine, part = lax.optimization_barrier((mine, part))
     rows = expert_rows(mine, own, other)
     rows, apart = lax.optimization_barrier((rows, apart))

time: 97.7 us -> 99.4 us (1.017)
  waiting for transfers between devices: 12.2 us -> 15.5 us
  starting transfers between devices: 47.6 us -> 45.3 us
    ppermute x0 -> x2, waiting for transfers between devices: none -> 11.8 us  [pair(): lax.ppermute(part, axis, [(i, i ^ distance) for i in range(lax.axis_size(...]
    ppermute x10 -> x7, waiting for transfers between devices: 12.2 us -> 3.69 us  [shift(): lax.ppermute(part, axis, [(i, (i + step) % size) for i in range(size)])]
    ppermute x10 -> x7, starting transfers between devices: 23.5 us -> 17.8 us  [shift(): lax.ppermute(part, axis, [(i, (i + step) % size) for i in range(size)])]
    ppermute x0 -> x2, starting transfers between devices: none -> 3.84 us  [pair(): lax.ppermute(part, axis, [(i, i ^ distance) for i in range(lax.axis_size(...]
  transfers between devices with their start and end apart: 12 -> 11, of which waited for: 5 -> 4; matrix products, arithmetic and copies ran while one was open for 0% -> 0% of each run, Pallas kernels for 9% -> 9%
where the time goes in v9:
time: 99.4 us; the launch traced here: 98.4 us
  starting transfers between devices  45.3 us (46%)
  blocking collectives  23.9 us (24%)
  waiting for transfers between devices  15.5 us (16%)
  Pallas kernels  12.3 us (12%)
  between operations  1.51 us (2%)
    all_gather x1, blocking collectives, shards(): sums = total(lax.all_gather(part, 'z_far', axis=0))  23.9 us
    all_to_all x2, starting transfers between devices, exchange(): lax.all_to_all(rows.reshape(experts, CAP, width), 'chip', split_axis=0, c...  23.6 us
    ppermute x7, starting transfers between devices, shift(): lax.ppermute(part, axis, [(i, (i + step) % size) for i in range(size)])  17.8 us
    ppermute x2, waiting for transfers between devices, pair(): lax.ppermute(part, axis, [(i, i ^ distance) for i in range(lax.axis_size(...  11.8 us
    pallas_call x1, Pallas kernels, expert_rows(): pl.pallas_call(expert_kernel, in_specs=[HBM] * len(operands), out_shape=j...  6.73 us
    ppermute x2, starting transfers between devices, pair(): lax.ppermute(part, axis, [(i, i ^ distance) for i in range(lax.axis_size(...  3.84 us
    ppermute x7, waiting for transfers between devices, shift(): lax.ppermute(part, axis, [(i, (i + step) % size) for i in range(size)])  3.69 us
    pallas_call x1, Pallas kernels, route(): pl.pallas_call(functools.partial(route_kernel, experts), out_shape=(jax.S...  2.56 us
  transfers between devices with their start and end apart: 11, of which 4 were waited for; matrix products, arithmetic and copies ran while one was open for 0% of the time, Pallas kernels for 9%

profile of v9, /device:TPU:6, one launch (start us, length us, event | category | flops | bytes accessed | tf_op | source)
XLA Modules:
  0.0 98.4 jit_solution(15898497906152386777)
XLA Ops:
  0.7 2.6 %route.1 = (bf16[256,2048]{1,0:T(8,128)(2,1)}, bf16[256,128]{1,0:T(8,128)(2,1)}) custom-call(s32[8,128]{1,0:T(8,128)} %bitcast.16, f32[8,128]{1,0:T(8,128)} %bitcast.17, bf16[128,2048]{1,0:T(8,128)(2,1)} %refs_2_.2), custom_call_target="tpu_custom_call" | custom-call | tf_op jit(solution)/shard_map/route/pallas_call | solution.py:72
  3.2 17.3 %all-to-all-start = ((bf16[16,16,2048]{2,1,0:T(8,128)(2,1)}), bf16[16,16,2048]{2,1,0:T(8,128)(2,1)}, u32[]{:S(2)}, u32[]{:S(2)}) async-start(bf16[16,16,2048]{2,1,0:T(8,128)(2,1)} %bitcast.15), calls=%async_computation | async-start | bytes 2097152 | tf_op jit(solution)/shard_map/all_to_all | solution.py:313
  20.5 1.9 %collective-permute-start.2 = (bf16[1,2048,384]{2,1,0:T(8,128)(2,1)}, bf16[1,2048,384]{2,1,0:T(8,128)(2,1)}, u32[]{:S(2)}, u32[]{:S(2)}) collective-permute-start(bf16[1,2048,384]{2,1,0:T(8,128)(2,1)} %refs_0_.1), channel_id=1, source_target_pairs={{0,1},{1,0},{2,3},{3,2},{4,5},{5,4},{6,7},{7,6},{8,9},{9,8},{10,11... | collective-permute-start | bytes 4718600 | tf_op jit(solution)/shard_map/ppermute | solution.py:296
  22.4 2.4 %collective-permute-start.3 = (bf16[1,2048,384]{2,1,0:T(8,128)(2,1)}, bf16[1,2048,384]{2,1,0:T(8,128)(2,1)}, u32[]{:S(2)}, u32[]{:S(2)}) collective-permute-start(bf16[1,2048,384]{2,1,0:T(8,128)(2,1)} %refs_1_.1), channel_id=1, source_target_pairs={{0,1},{1,0},{2,3},{3,2},{4,5},{5,4},{6,7},{7,6},{8,9},{9,8},{10,11... | collective-permute-start | bytes 4718600 | tf_op jit(solution)/shard_map/ppermute | solution.py:296
  24.8 1.9 %collective-permute-start.4 = (bf16[1,384,2048]{2,1,0:T(8,128)(2,1)}, bf16[1,384,2048]{2,1,0:T(8,128)(2,1)}, u32[]{:S(2)}, u32[]{:S(2)}) collective-permute-start(bf16[1,384,2048]{2,1,0:T(8,128)(2,1)} %refs_2_.3), channel_id=1, source_target_pairs={{0,1},{1,0},{2,3},{3,2},{4,5},{5,4},{6,7},{7,6},{8,9},{9,8},{10,11... | collective-permute-start | bytes 4718600 | tf_op jit(solution)/shard_map/ppermute | solution.py:296
  26.8 0.4 dequant.1
  27.2 1.9 %collective-permute-start = (bf16[32,2048]{1,0:T(8,128)(2,1)S(1)}, bf16[32,2048]{1,0:T(8,128)(2,1)S(1)}, u32[]{:S(2)}, u32[]{:S(2)}) collective-permute-start(bf16[32,2048]{1,0:T(8,128)(2,1)S(1)} %get-tuple-element.19), channel_id=1, source_target_pairs={{0,32},{32,0},{64,96},{96,64},{1,33},{33,1},{65,97},{97,65},{2,34}... | collective-permute-start | bytes 393224 | tf_op jit(solution)/shard_map/ppermute | solution.py:300
  29.1 5.9 %collective-permute-done.got_ref = bf16[32,2048]{1,0:T(8,128)(2,1)S(1)} collective-permute-done((bf16[32,2048]{1,0:T(8,128)(2,1)S(1)}, bf16[32,2048]{1,0:T(8,128)(2,1)S(1)}, u32[]{:S(2)}, u32[]{:S(2)}) %collective-permute-start) | collective-permute-done | bytes 131104 | tf_op jit(solution)/shard_map/ppermute | solution.py:300
  35.0 0.1 add_split.1
  35.1 1.9 %collective-permute-start.1 = (bf16[16,2048]{1,0:T(8,128)(2,1)S(1)}, bf16[16,2048]{1,0:T(8,128)(2,1)S(1)}, u32[]{:S(2)}, u32[]{:S(2)}) collective-permute-start(bf16[16,2048]{1,0:T(8,128)(2,1)S(1)} %get-tuple-element.21), channel_id=1, source_target_pairs={{0,64},{32,96},{64,0},{96,32},{1,65},{33,97},{65,1},{97,33},{2,66}... | collective-permute-start | bytes 196616 | tf_op jit(solution)/shard_map/ppermute | solution.py:300
  37.0 5.9 %collective-permute-done.1.refs_1_ = bf16[16,2048]{1,0:T(8,128)(2,1)S(1)} collective-permute-done((bf16[16,2048]{1,0:T(8,128)(2,1)S(1)}, bf16[16,2048]{1,0:T(8,128)(2,1)S(1)}, u32[]{:S(2)}, u32[]{:S(2)}) %collective-permute-start.1) | collective-permute-done | bytes 65568 | tf_op jit(solution)/shard_map/ppermute | solution.py:300
  42.9 1.9 %collective-permute-start.5 = (bf16[16,2048]{1,0:T(8,128)(2,1)S(1)}, bf16[16,2048]{1,0:T(8,128)(2,1)S(1)}, u32[]{:S(2)}, u32[]{:S(2)}) collective-permute-start(bf16[16,2048]{1,0:T(8,128)(2,1)S(1)} %add_parts.2.refs_0_), channel_id=1, source_target_pairs={{0,512},{512,0},{1,513},{513,1},{2,514},{514,2},{3,515},{515,3},{4... | collective-permute-start | bytes 196616 | tf_op jit(solution)/shard_map/ppermute | solution.py:296
  44.9 6.7 %expert_rows.1 = bf16[256,2048]{1,0:T(8,128)(2,1)} custom-call(bf16[256,2048]{1,0:T(8,128)(2,1)} %bitcast.3.rows_hbm, bf16[1,2048,384]{2,1,0:T(8,128)(2,1)} %refs_0_.1, bf16[1,2048,384]{2,1,0:T(8,128)(2,1)} %refs_1_.1, bf16[1,384,2048]{2,1,0:T(8,128)(2,1)} %refs_2_.3, bf16[1,2048,384]{2,1,0:T(8,128)(2,1)} %collective-permute-done.2.refs_3_, ...), custom_call_target="tpu_custom_call" | custom-call | tf_op jit(solution)/shard_map/expert_rows/pallas_call | solution.py:123
  51.6 0.0 copy-start.3
  51.7 2.5 %collective-permute-done.5.refs_1_ = bf16[16,2048]{1,0:T(8,128)(2,1)S(1)} collective-permute-done((bf16[16,2048]{1,0:T(8,128)(2,1)S(1)}, bf16[16,2048]{1,0:T(8,128)(2,1)S(1)}, u32[]{:S(2)}, u32[]{:S(2)}) %collective-permute-start.5) | collective-permute-done | bytes 65568 | tf_op jit(solution)/shard_map/ppermute | solution.py:296
  54.2 6.3 %all-to-all-start.1 = ((bf16[16,16,2048]{2,1,0:T(8,128)(2,1)}), bf16[16,16,2048]{2,1,0:T(8,128)(2,1)S(1)}, u32[]{:S(2)}, u32[]{:S(2)}) async-start(bf16[16,16,2048]{2,1,0:T(8,128)(2,1)} %bitcast.14), calls=%async_computation.1 | async-start | bytes 2097152 | tf_op jit(solution)/shard_map/all_to_all | solution.py:313
  60.5 0.0 copy-start.1
  60.6 23.9 %all-gather = bf16[64,2048]{1,0:T(8,128)(2,1)S(1)} all-gather(bf16[16,2048]{1,0:T(8,128)(2,1)S(1)} %add_parts.3), channel_id=2, replica_groups=mesh['y_far'=2,'z_far'=4,'z_near'=4,'chip'=16,'core'=2] {'z_far'}, dimensions={0}, use_global_device_ids=true | all-gather | bytes 327680 | tf_op jit(solution)/shard_map/all_gather | solution.py:347
  84.5 1.9 %collective-permute-start.6 = (bf16[16,2048]{1,0:T(8,128)(2,1)S(1)}, bf16[16,2048]{1,0:T(8,128)(2,1)S(1)}, u32[]{:S(2)}, u32[]{:S(2)}) collective-permute-start(bf16[16,2048]{1,0:T(8,128)(2,1)S(1)} %total.1.refs_0_), channel_id=1, source_target_pairs={{0,32},{32,64},{64,96},{96,0},{1,33},{33,65},{65,97},{97,1},{2,34}... | collective-permute-start | bytes 196616 | tf_op jit(solution)/shard_map/ppermute | solution.py:296
  86.4 4.5 %collective-permute-start.7 = (bf16[16,2048]{1,0:T(8,128)(2,1)S(1)}, bf16[16,2048]{1,0:T(8,128)(2,1)S(1)}, u32[]{:S(2)}, u32[]{:S(2)}) collective-permute-start(bf16[16,2048]{1,0:T(8,128)(2,1)S(1)} %total.1.refs_0_), channel_id=1, source_target_pairs={{0,64},{32,96},{64,0},{96,32},{1,65},{33,97},{65,1},{97,33},{2,66}... | collective-permute-start | bytes 196616 | tf_op jit(solution)/shard_map/ppermute | solution.py:296
  90.9 3.2 %collective-permute-start.8 = (bf16[16,2048]{1,0:T(8,128)(2,1)S(1)}, bf16[16,2048]{1,0:T(8,128)(2,1)S(1)}, u32[]{:S(2)}, u32[]{:S(2)}) collective-permute-start(bf16[16,2048]{1,0:T(8,128)(2,1)S(1)} %total.1.refs_0_), channel_id=1, source_target_pairs={{0,96},{32,0},{64,32},{96,64},{1,97},{33,1},{65,33},{97,65},{2,98}... | collective-permute-start | bytes 196616 | tf_op jit(solution)/shard_map/ppermute | solution.py:296
  94.8 1.1 %combine_rows.1 = bf16[128,2048]{1,0:T(8,128)(2,1)} custom-call(bf16[256,128]{1,0:T(8,128)(2,1)S(1)} %copy-done.3, bf16[256,2048]{1,0:T(8,128)(2,1)S(1)} %bitcast.11), custom_call_target="tpu_custom_call" | custom-call | tf_op jit(solution)/shard_map/combine_rows/pallas_call | solution.py:149
  95.9 1.1 %collective-permute-done.8.refs_3_ = bf16[16,2048]{1,0:T(8,128)(2,1)S(1)} collective-permute-done((bf16[16,2048]{1,0:T(8,128)(2,1)S(1)}, bf16[16,2048]{1,0:T(8,128)(2,1)S(1)}, u32[]{:S(2)}, u32[]{:S(2)}) %collective-permute-start.8) | collective-permute-done | bytes 65568 | tf_op jit(solution)/shard_map/ppermute | solution.py:296
  97.1 1.3 %update.1 = (f32[64,2048]{1,0:T(8,128)}, f32[64,2048]{1,0:T(8,128)}) custom-call(s32[1]{0:T(128)S(6)} %copy.14.fragment_ref, s32[1]{0:T(128)} %bitcast.4.near_ref.place_ref, bf16[16,2048]{1,0:T(8,128)(2,1)S(1)} %total.1.refs_0_, bf16[16,2048]{1,0:T(8,128)(2,1)S(1)} %collective-permute-done.6.refs_1_, bf16[16,2048]{1,0:T(8,128)(2,1)S(1)} %collective-permute-done.7.refs_2_, ...), custom_call_target="tpu_custom_call" | custom-call | tf_op jit(solution)/shard_map/update/pallas_call | solution.py:271
  (18 shorter events, 0.1 us)
Async XLA Ops:
  0.6 26.1 %copy-start.2 = (bf16[1,64,2048]{2,1,0:T(8,128)(2,1)S(1)}, bf16[1,64,2048]{2,1,0:T(8,128)(2,1)}, u32[]{:S(2)}) copy-start(bf16[1,64,2048]{2,1,0:T(8,128)(2,1)} %values_ref.1) | copy-start | bytes 786436
  0.6 26.1 %copy-start.4 = (f32[1,64,16]{1,2,0:T(8,128)S(1)}, f32[1,64,16]{1,2,0:T(8,128)}, u32[]{:S(2)}) copy-start(f32[1,64,16]{1,2,0:T(8,128)} %param.18) | copy-start | bytes 12292
  3.2 41.7 %all-to-all-start = ((bf16[16,16,2048]{2,1,0:T(8,128)(2,1)}), bf16[16,16,2048]{2,1,0:T(8,128)(2,1)}, u32[]{:S(2)}, u32[]{:S(2)}) async-start(bf16[16,16,2048]{2,1,0:T(8,128)(2,1)} %bitcast.15), calls=%async_computation | async-start | bytes 2097152 | tf_op jit(solution)/shard_map/all_to_all | solution.py:313
  20.5 24.4 %collective-permute-start.2 = (bf16[1,2048,384]{2,1,0:T(8,128)(2,1)}, bf16[1,2048,384]{2,1,0:T(8,128)(2,1)}, u32[]{:S(2)}, u32[]{:S(2)}) collective-permute-start(bf16[1,2048,384]{2,1,0:T(8,128)(2,1)} %refs_0_.1), channel_id=1, source_target_pairs={{0,1},{1,0},{2,3},{3,2},{4,5},{5,4},{6,7},{7,6},{8,9},{9,8},{10,11... | collective-permute-start | bytes 4718600 | tf_op jit(solution)/shard_map/ppermute | solution.py:296
  22.4 22.5 %collective-permute-start.3 = (bf16[1,2048,384]{2,1,0:T(8,128)(2,1)}, bf16[1,2048,384]{2,1,0:T(8,128)(2,1)}, u32[]{:S(2)}, u32[]{:S(2)}) collective-permute-start(bf16[1,2048,384]{2,1,0:T(8,128)(2,1)} %refs_1_.1), channel_id=1, source_target_pairs={{0,1},{1,0},{2,3},{3,2},{4,5},{5,4},{6,7},{7,6},{8,9},{9,8},{10,11... | collective-permute-start | bytes 4718600 | tf_op jit(solution)/shard_map/ppermute | solution.py:296
  24.8 20.1 %collective-permute-start.4 = (bf16[1,384,2048]{2,1,0:T(8,128)(2,1)}, bf16[1,384,2048]{2,1,0:T(8,128)(2,1)}, u32[]{:S(2)}, u32[]{:S(2)}) collective-permute-start(bf16[1,384,2048]{2,1,0:T(8,128)(2,1)} %refs_2_.3), channel_id=1, source_target_pairs={{0,1},{1,0},{2,3},{3,2},{4,5},{5,4},{6,7},{7,6},{8,9},{9,8},{10,11... | collective-permute-start | bytes 4718600 | tf_op jit(solution)/shard_map/ppermute | solution.py:296
  27.2 7.8 %collective-permute-start = (bf16[32,2048]{1,0:T(8,128)(2,1)S(1)}, bf16[32,2048]{1,0:T(8,128)(2,1)S(1)}, u32[]{:S(2)}, u32[]{:S(2)}) collective-permute-start(bf16[32,2048]{1,0:T(8,128)(2,1)S(1)} %get-tuple-element.19), channel_id=1, source_target_pairs={{0,32},{32,0},{64,96},{96,64},{1,33},{33,1},{65,97},{97,65},{2,34}... | collective-permute-start | bytes 393224 | tf_op jit(solution)/shard_map/ppermute | solution.py:300
  35.1 7.8 %collective-permute-start.1 = (bf16[16,2048]{1,0:T(8,128)(2,1)S(1)}, bf16[16,2048]{1,0:T(8,128)(2,1)S(1)}, u32[]{:S(2)}, u32[]{:S(2)}) collective-permute-start(bf16[16,2048]{1,0:T(8,128)(2,1)S(1)} %get-tuple-element.21), channel_id=1, source_target_pairs={{0,64},{32,96},{64,0},{96,32},{1,65},{33,97},{65,1},{97,33},{2,66}... | collective-permute-start | bytes 196616 | tf_op jit(solution)/shard_map/ppermute | solution.py:300
  42.9 11.3 %collective-permute-start.5 = (bf16[16,2048]{1,0:T(8,128)(2,1)S(1)}, bf16[16,2048]{1,0:T(8,128)(2,1)S(1)}, u32[]{:S(2)}, u32[]{:S(2)}) collective-permute-start(bf16[16,2048]{1,0:T(8,128)(2,1)S(1)} %add_parts.2.refs_0_), channel_id=1, source_target_pairs={{0,512},{512,0},{1,513},{513,1},{2,514},{514,2},{3,515},{515,3},{4... | collective-permute-start | bytes 196616 | tf_op jit(solution)/shard_map/ppermute | solution.py:296
  51.6 43.2 %copy-start.3 = (bf16[256,128]{1,0:T(8,128)(2,1)S(1)}, bf16[256,128]{1,0:T(8,128)(2,1)}, u32[]{:S(2)}) copy-start(bf16[256,128]{1,0:T(8,128)(2,1)} %get-tuple-element.25.combine_ref) | copy-start | bytes 196612
  54.2 40.6 %all-to-all-start.1 = ((bf16[16,16,2048]{2,1,0:T(8,128)(2,1)}), bf16[16,16,2048]{2,1,0:T(8,128)(2,1)S(1)}, u32[]{:S(2)}, u32[]{:S(2)}) async-start(bf16[16,16,2048]{2,1,0:T(8,128)(2,1)} %bitcast.14), calls=%async_computation.1 | async-start | bytes 2097152 | tf_op jit(solution)/shard_map/all_to_all | solution.py:313
  60.5 36.6 %copy-start = (f32[3,64,2048]{2,1,0:T(8,128)S(1)}, f32[3,64,2048]{2,1,0:T(8,128)}, u32[]{:S(2)}) copy-start(f32[3,64,2048]{2,1,0:T(8,128)} %refs_4_.1) | copy-start | bytes 4718596
  60.5 36.6 %copy-start.1 = (f32[64,2048]{1,0:T(8,128)S(1)}, f32[64,2048]{1,0:T(8,128)}, u32[]{:S(2)}) copy-start(f32[64,2048]{1,0:T(8,128)} %refs_5_.1) | copy-start | bytes 1572868
  84.5 11.5 %collective-permute-start.6 = (bf16[16,2048]{1,0:T(8,128)(2,1)S(1)}, bf16[16,2048]{1,0:T(8,128)(2,1)S(1)}, u32[]{:S(2)}, u32[]{:S(2)}) collective-permute-start(bf16[16,2048]{1,0:T(8,128)(2,1)S(1)} %total.1.refs_0_), channel_id=1, source_target_pairs={{0,32},{32,64},{64,96},{96,0},{1,33},{33,65},{65,97},{97,1},{2,34}... | collective-permute-start | bytes 196616 | tf_op jit(solution)/shard_map/ppermute | solution.py:296
  86.4 9.6 %collective-permute-start.7 = (bf16[16,2048]{1,0:T(8,128)(2,1)S(1)}, bf16[16,2048]{1,0:T(8,128)(2,1)S(1)}, u32[]{:S(2)}, u32[]{:S(2)}) collective-permute-start(bf16[16,2048]{1,0:T(8,128)(2,1)S(1)} %total.1.refs_0_), channel_id=1, source_target_pairs={{0,64},{32,96},{64,0},{96,32},{1,65},{33,97},{65,1},{97,33},{2,66}... | collective-permute-start | bytes 196616 | tf_op jit(solution)/shard_map/ppermute | solution.py:296
  90.9 6.2 %collective-permute-start.8 = (bf16[16,2048]{1,0:T(8,128)(2,1)S(1)}, bf16[16,2048]{1,0:T(8,128)(2,1)S(1)}, u32[]{:S(2)}, u32[]{:S(2)}) collective-permute-start(bf16[16,2048]{1,0:T(8,128)(2,1)S(1)} %total.1.refs_0_), channel_id=1, source_target_pairs={{0,96},{32,0},{64,32},{96,64},{1,97},{33,1},{65,33},{97,65},{2,98}... | collective-permute-start | bytes 196616 | tf_op jit(solution)/shard_map/ppermute | solution.py:296

commit v10 on v8

--- a/solution.py
+++ b/solution.py
@@ -309,8 +309,9 @@
     own = (w_gate, w_up, w_down)
     near = place_on("z_near")
     part = add_parts(scatter_stage(dequant(near, pseudo_values, block_scales), "z_near"))
+    part, down = lax.optimization_barrier((part, w_down))
+    other = (shift(w_gate, "core", 1), shift(w_up, "core", 1), shift(down, "core", 1))
     apart = shift(part, "y_far", 1)
-    other = tuple(shift(w, "core", 1) for w in own)
     mine, part = lax.optimization_barrier((mine, part))
     rows = expert_rows(mine, own, other)
     rows, apart = lax.optimization_barrier((rows, apart))

time: 97.7 us -> 98.1 us (level)
  waiting for transfers between devices: 12.2 us -> 5.45 us
  starting transfers between devices: 47.6 us -> 53.3 us
  blocking collectives: 23.4 us -> 24.8 us
    ppermute x10, waiting for transfers between devices: 12.2 us -> 5.44 us  [shift(): lax.ppermute(part, axis, [(i, (i + step) % size) for i in range(size)])]
    ppermute x10, starting transfers between devices: 23.5 us -> 29.5 us  [shift(): lax.ppermute(part, axis, [(i, (i + step) % size) for i in range(size)])]
    all_gather x1, blocking collectives: 23.4 us -> 24.8 us  [shards(): sums = total(lax.all_gather(part, 'z_far', axis=0))]
  transfers between devices with their start and end apart: 12 -> 12, of which waited for: 5 -> 3; matrix products, arithmetic and copies ran while one was open for 0% -> 0% of each run, Pallas kernels for 9% -> 9%
where the time goes in v10:
time: 98.1 us; the launch traced here: 97.5 us
  starting transfers between devices  53.3 us (54%)
  blocking collectives  24.8 us (25%)
  Pallas kernels  12.4 us (13%)
  waiting for transfers between devices  5.45 us (6%)
  between operations  1.51 us (2%)
    ppermute x10, starting transfers between devices, shift(): lax.ppermute(part, axis, [(i, (i + step) % size) for i in range(size)])  29.5 us
    all_gather x1, blocking collectives, shards(): sums = total(lax.all_gather(part, 'z_far', axis=0))  24.8 us
    all_to_all x2, starting transfers between devices, exchange(): lax.all_to_all(rows.reshape(experts, CAP, width), 'chip', split_axis=0, c...  23.7 us
    pallas_call x1, Pallas kernels, expert_rows(): pl.pallas_call(expert_kernel, in_specs=[HBM] * len(operands), out_shape=j...  6.72 us
    ppermute x10, waiting for transfers between devices, shift(): lax.ppermute(part, axis, [(i, (i + step) % size) for i in range(size)])  5.44 us
    pallas_call x1, Pallas kernels, route(): pl.pallas_call(functools.partial(route_kernel, experts), out_shape=(jax.S...  2.56 us
  transfers between devices with their start and end apart: 12, of which 3 were waited for; matrix products, arithmetic and copies ran while one was open for 0% of the time, Pallas kernels for 9%

profile of v10, /device:TPU:6, one launch (start us, length us, event | category | flops | bytes accessed | tf_op | source)
XLA Modules:
  0.0 97.5 jit_solution(18379782429034298686)
XLA Ops:
  0.7 2.6 %route.1 = (bf16[256,2048]{1,0:T(8,128)(2,1)}, bf16[256,128]{1,0:T(8,128)(2,1)}) custom-call(s32[8,128]{1,0:T(8,128)} %bitcast.16, f32[8,128]{1,0:T(8,128)} %bitcast.17, bf16[128,2048]{1,0:T(8,128)(2,1)} %refs_2_.2), custom_call_target="tpu_custom_call" | custom-call | tf_op jit(solution)/shard_map/route/pallas_call | solution.py:72
  3.2 17.3 %all-to-all-start = ((bf16[16,16,2048]{2,1,0:T(8,128)(2,1)}), bf16[16,16,2048]{2,1,0:T(8,128)(2,1)}, u32[]{:S(2)}, u32[]{:S(2)}) async-start(bf16[16,16,2048]{2,1,0:T(8,128)(2,1)} %bitcast.15), calls=%async_computation | async-start | bytes 2097152 | tf_op jit(solution)/shard_map/all_to_all | solution.py:288
  20.5 0.6 dequant.1
  21.1 1.9 %collective-permute-start = (bf16[16,2048]{1,0:T(8,128)(2,1)S(1)}, bf16[16,2048]{1,0:T(8,128)(2,1)S(1)}, u32[]{:S(2)}, u32[]{:S(2)}) collective-permute-start(bf16[16,2048]{1,0:T(8,128)(2,1)S(1)} %get-tuple-element.21), channel_id=1, source_target_pairs={{0,32},{32,64},{64,96},{96,0},{1,33},{33,65},{65,97},{97,1},{2,34}... | collective-permute-start | bytes 196616 | tf_op jit(solution)/shard_map/ppermute | solution.py:271
  23.0 1.9 %collective-permute-start.1 = (bf16[16,2048]{1,0:T(8,128)(2,1)S(1)}, bf16[16,2048]{1,0:T(8,128)(2,1)S(1)}, u32[]{:S(2)}, u32[]{:S(2)}) collective-permute-start(bf16[16,2048]{1,0:T(8,128)(2,1)S(1)} %get-tuple-element.22), channel_id=1, source_target_pairs={{0,64},{32,96},{64,0},{96,32},{1,65},{33,97},{65,1},{97,33},{2,66}... | collective-permute-start | bytes 196616 | tf_op jit(solution)/shard_map/ppermute | solution.py:271
  25.0 5.7 %collective-permute-start.2 = (bf16[16,2048]{1,0:T(8,128)(2,1)S(1)}, bf16[16,2048]{1,0:T(8,128)(2,1)S(1)}, u32[]{:S(2)}, u32[]{:S(2)}) collective-permute-start(bf16[16,2048]{1,0:T(8,128)(2,1)S(1)} %get-tuple-element.23), channel_id=1, source_target_pairs={{0,96},{32,0},{64,32},{96,64},{1,97},{33,1},{65,33},{97,65},{2,98}... | collective-permute-start | bytes 196616 | tf_op jit(solution)/shard_map/ppermute | solution.py:271
  30.7 1.9 %collective-permute-start.3 = (bf16[1,2048,384]{2,1,0:T(8,128)(2,1)}, bf16[1,2048,384]{2,1,0:T(8,128)(2,1)}, u32[]{:S(2)}, u32[]{:S(2)}) collective-permute-start(bf16[1,2048,384]{2,1,0:T(8,128)(2,1)} %refs_0_.1), channel_id=1, source_target_pairs={{0,1},{1,0},{2,3},{3,2},{4,5},{5,4},{6,7},{7,6},{8,9},{9,8},{10,11... | collective-permute-start | bytes 4718600 | tf_op jit(solution)/shard_map/ppermute | solution.py:271
  32.6 2.4 %collective-permute-start.4 = (bf16[1,2048,384]{2,1,0:T(8,128)(2,1)}, bf16[1,2048,384]{2,1,0:T(8,128)(2,1)}, u32[]{:S(2)}, u32[]{:S(2)}) collective-permute-start(bf16[1,2048,384]{2,1,0:T(8,128)(2,1)} %refs_1_.1), channel_id=1, source_target_pairs={{0,1},{1,0},{2,3},{3,2},{4,5},{5,4},{6,7},{7,6},{8,9},{9,8},{10,11... | collective-permute-start | bytes 4718600 | tf_op jit(solution)/shard_map/ppermute | solution.py:271
  35.0 0.0 collective-permute-done.refs_1_
  35.1 1.9 %collective-permute-start.5 = (bf16[1,384,2048]{2,1,0:T(8,128)(2,1)}, bf16[1,384,2048]{2,1,0:T(8,128)(2,1)}, u32[]{:S(2)}, u32[]{:S(2)}) collective-permute-start(bf16[1,384,2048]{2,1,0:T(8,128)(2,1)} %refs_2_.3), channel_id=1, source_target_pairs={{0,1},{1,0},{2,3},{3,2},{4,5},{5,4},{6,7},{7,6},{8,9},{9,8},{10,11... | collective-permute-start | bytes 4718600 | tf_op jit(solution)/shard_map/ppermute | solution.py:271
  37.0 1.9 %collective-permute-start.6 = (bf16[16,2048]{1,0:T(8,128)(2,1)S(1)}, bf16[16,2048]{1,0:T(8,128)(2,1)S(1)}, u32[]{:S(2)}, u32[]{:S(2)}) collective-permute-start(bf16[16,2048]{1,0:T(8,128)(2,1)S(1)} %add_parts.2.refs_0_), channel_id=1, source_target_pairs={{0,512},{512,0},{1,513},{513,1},{2,514},{514,2},{3,515},{515,3},{4... | collective-permute-start | bytes 196616 | tf_op jit(solution)/shard_map/ppermute | solution.py:271
  39.0 1.8 %collective-permute-done.5.refs_5_ = bf16[1,384,2048]{2,1,0:T(8,128)(2,1)} collective-permute-done((bf16[1,384,2048]{2,1,0:T(8,128)(2,1)}, bf16[1,384,2048]{2,1,0:T(8,128)(2,1)}, u32[]{:S(2)}, u32[]{:S(2)}) %collective-permute-start.5) | collective-permute-done | bytes 1572896 | tf_op jit(solution)/shard_map/ppermute | solution.py:271
  40.8 6.7 %expert_rows.1 = bf16[256,2048]{1,0:T(8,128)(2,1)} custom-call(bf16[256,2048]{1,0:T(8,128)(2,1)} %bitcast.3.rows_hbm, bf16[1,2048,384]{2,1,0:T(8,128)(2,1)} %refs_0_.1, bf16[1,2048,384]{2,1,0:T(8,128)(2,1)} %refs_1_.1, bf16[1,384,2048]{2,1,0:T(8,128)(2,1)} %refs_2_.3, bf16[1,2048,384]{2,1,0:T(8,128)(2,1)} %collective-permute-done.3.refs_3_, ...), custom_call_target="tpu_custom_call" | custom-call | tf_op jit(solution)/shard_map/expert_rows/pallas_call | solution.py:123
  47.6 0.0 copy-start.3
  47.6 1.2 %collective-permute-done.6.refs_1_ = bf16[16,2048]{1,0:T(8,128)(2,1)S(1)} collective-permute-done((bf16[16,2048]{1,0:T(8,128)(2,1)S(1)}, bf16[16,2048]{1,0:T(8,128)(2,1)S(1)}, u32[]{:S(2)}, u32[]{:S(2)}) %collective-permute-start.6) | collective-permute-done | bytes 65568 | tf_op jit(solution)/shard_map/ppermute | solution.py:271
  48.7 6.5 %all-to-all-start.1 = ((bf16[16,16,2048]{2,1,0:T(8,128)(2,1)}), bf16[16,16,2048]{2,1,0:T(8,128)(2,1)S(1)}, u32[]{:S(2)}, u32[]{:S(2)}) async-start(bf16[16,16,2048]{2,1,0:T(8,128)(2,1)} %bitcast.14), calls=%async_computation.1 | async-start | bytes 2097152 | tf_op jit(solution)/shard_map/all_to_all | solution.py:288
  55.2 0.0 copy-start.1
  55.3 24.8 %all-gather = bf16[64,2048]{1,0:T(8,128)(2,1)S(1)} all-gather(bf16[16,2048]{1,0:T(8,128)(2,1)S(1)} %add_parts.3), channel_id=2, replica_groups=mesh['y_far'=2,'z_far'=4,'z_near'=4,'chip'=16,'core'=2] {'z_far'}, dimensions={0}, use_global_device_ids=true | all-gather | bytes 327680 | tf_op jit(solution)/shard_map/all_gather | solution.py:320
  80.1 3.9 %collective-permute-start.7 = (bf16[16,2048]{1,0:T(8,128)(2,1)S(1)}, bf16[16,2048]{1,0:T(8,128)(2,1)S(1)}, u32[]{:S(2)}, u32[]{:S(2)}) collective-permute-start(bf16[16,2048]{1,0:T(8,128)(2,1)S(1)} %total.1.refs_0_), channel_id=1, source_target_pairs={{0,32},{32,64},{64,96},{96,0},{1,33},{33,65},{65,97},{97,1},{2,34}... | collective-permute-start | bytes 196616 | tf_op jit(solution)/shard_map/ppermute | solution.py:271
  84.1 5.9 %collective-permute-start.8 = (bf16[16,2048]{1,0:T(8,128)(2,1)S(1)}, bf16[16,2048]{1,0:T(8,128)(2,1)S(1)}, u32[]{:S(2)}, u32[]{:S(2)}) collective-permute-start(bf16[16,2048]{1,0:T(8,128)(2,1)S(1)} %total.1.refs_0_), channel_id=1, source_target_pairs={{0,64},{32,96},{64,0},{96,32},{1,65},{33,97},{65,1},{97,33},{2,66}... | collective-permute-start | bytes 196616 | tf_op jit(solution)/shard_map/ppermute | solution.py:271
  90.0 1.9 %collective-permute-start.9 = (bf16[16,2048]{1,0:T(8,128)(2,1)S(1)}, bf16[16,2048]{1,0:T(8,128)(2,1)S(1)}, u32[]{:S(2)}, u32[]{:S(2)}) collective-permute-start(bf16[16,2048]{1,0:T(8,128)(2,1)S(1)} %total.1.refs_0_), channel_id=1, source_target_pairs={{0,96},{32,0},{64,32},{96,64},{1,97},{33,1},{65,33},{97,65},{2,98}... | collective-permute-start | bytes 196616 | tf_op jit(solution)/shard_map/ppermute | solution.py:271
  92.6 1.1 %combine_rows.1 = bf16[128,2048]{1,0:T(8,128)(2,1)} custom-call(bf16[256,128]{1,0:T(8,128)(2,1)S(1)} %copy-done.3, bf16[256,2048]{1,0:T(8,128)(2,1)S(1)} %bitcast.11), custom_call_target="tpu_custom_call" | custom-call | tf_op jit(solution)/shard_map/combine_rows/pallas_call | solution.py:149
  93.8 2.4 %collective-permute-done.9.refs_3_ = bf16[16,2048]{1,0:T(8,128)(2,1)S(1)} collective-permute-done((bf16[16,2048]{1,0:T(8,128)(2,1)S(1)}, bf16[16,2048]{1,0:T(8,128)(2,1)S(1)}, u32[]{:S(2)}, u32[]{:S(2)}) %collective-permute-start.9) | collective-permute-done | bytes 65568 | tf_op jit(solution)/shard_map/ppermute | solution.py:271
  96.2 1.3 %update.1 = (f32[64,2048]{1,0:T(8,128)}, f32[64,2048]{1,0:T(8,128)}) custom-call(s32[1]{0:T(128)S(6)} %copy.14.fragment_ref, s32[1]{0:T(128)} %bitcast.4.place_ref, bf16[16,2048]{1,0:T(8,128)(2,1)S(1)} %total.1.refs_0_, bf16[16,2048]{1,0:T(8,128)(2,1)S(1)} %collective-permute-done.7.refs_1_, bf16[16,2048]{1,0:T(8,128)(2,1)S(1)} %collective-permute-done.8.refs_2_, ...), custom_call_target="tpu_custom_call" | custom-call | tf_op jit(solution)/shard_map/update/pallas_call | solution.py:246
  (19 shorter events, 0.1 us)
Async XLA Ops:
  0.6 19.9 %copy-start.2 = (bf16[1,64,2048]{2,1,0:T(8,128)(2,1)S(1)}, bf16[1,64,2048]{2,1,0:T(8,128)(2,1)}, u32[]{:S(2)}) copy-start(bf16[1,64,2048]{2,1,0:T(8,128)(2,1)} %values_ref.1) | copy-start | bytes 786436
  0.6 19.9 %copy-start.4 = (f32[1,64,16]{1,2,0:T(8,128)S(1)}, f32[1,64,16]{1,2,0:T(8,128)}, u32[]{:S(2)}) copy-start(f32[1,64,16]{1,2,0:T(8,128)} %param.18) | copy-start | bytes 12292
  3.2 35.8 %all-to-all-start = ((bf16[16,16,2048]{2,1,0:T(8,128)(2,1)}), bf16[16,16,2048]{2,1,0:T(8,128)(2,1)}, u32[]{:S(2)}, u32[]{:S(2)}) async-start(bf16[16,16,2048]{2,1,0:T(8,128)(2,1)} %bitcast.15), calls=%async_computation | async-start | bytes 2097152 | tf_op jit(solution)/shard_map/all_to_all | solution.py:288
  21.1 13.9 %collective-permute-start = (bf16[16,2048]{1,0:T(8,128)(2,1)S(1)}, bf16[16,2048]{1,0:T(8,128)(2,1)S(1)}, u32[]{:S(2)}, u32[]{:S(2)}) collective-permute-start(bf16[16,2048]{1,0:T(8,128)(2,1)S(1)} %get-tuple-element.21), channel_id=1, source_target_pairs={{0,32},{32,64},{64,96},{96,0},{1,33},{33,65},{65,97},{97,1},{2,34}... | collective-permute-start | bytes 196616 | tf_op jit(solution)/shard_map/ppermute | solution.py:271
  23.0 12.0 %collective-permute-start.1 = (bf16[16,2048]{1,0:T(8,128)(2,1)S(1)}, bf16[16,2048]{1,0:T(8,128)(2,1)S(1)}, u32[]{:S(2)}, u32[]{:S(2)}) collective-permute-start(bf16[16,2048]{1,0:T(8,128)(2,1)S(1)} %get-tuple-element.22), channel_id=1, source_target_pairs={{0,64},{32,96},{64,0},{96,32},{1,65},{33,97},{65,1},{97,33},{2,66}... | collective-permute-start | bytes 196616 | tf_op jit(solution)/shard_map/ppermute | solution.py:271
  25.0 10.1 %collective-permute-start.2 = (bf16[16,2048]{1,0:T(8,128)(2,1)S(1)}, bf16[16,2048]{1,0:T(8,128)(2,1)S(1)}, u32[]{:S(2)}, u32[]{:S(2)}) collective-permute-start(bf16[16,2048]{1,0:T(8,128)(2,1)S(1)} %get-tuple-element.23), channel_id=1, source_target_pairs={{0,96},{32,0},{64,32},{96,64},{1,97},{33,1},{65,33},{97,65},{2,98}... | collective-permute-start | bytes 196616 | tf_op jit(solution)/shard_map/ppermute | solution.py:271
  30.7 8.3 %collective-permute-start.3 = (bf16[1,2048,384]{2,1,0:T(8,128)(2,1)}, bf16[1,2048,384]{2,1,0:T(8,128)(2,1)}, u32[]{:S(2)}, u32[]{:S(2)}) collective-permute-start(bf16[1,2048,384]{2,1,0:T(8,128)(2,1)} %refs_0_.1), channel_id=1, source_target_pairs={{0,1},{1,0},{2,3},{3,2},{4,5},{5,4},{6,7},{7,6},{8,9},{9,8},{10,11... | collective-permute-start | bytes 4718600 | tf_op jit(solution)/shard_map/ppermute | solution.py:271
  32.6 6.4 %collective-permute-start.4 = (bf16[1,2048,384]{2,1,0:T(8,128)(2,1)}, bf16[1,2048,384]{2,1,0:T(8,128)(2,1)}, u32[]{:S(2)}, u32[]{:S(2)}) collective-permute-start(bf16[1,2048,384]{2,1,0:T(8,128)(2,1)} %refs_1_.1), channel_id=1, source_target_pairs={{0,1},{1,0},{2,3},{3,2},{4,5},{5,4},{6,7},{7,6},{8,9},{9,8},{10,11... | collective-permute-start | bytes 4718600 | tf_op jit(solution)/shard_map/ppermute | solution.py:271
  35.1 5.7 %collective-permute-start.5 = (bf16[1,384,2048]{2,1,0:T(8,128)(2,1)}, bf16[1,384,2048]{2,1,0:T(8,128)(2,1)}, u32[]{:S(2)}, u32[]{:S(2)}) collective-permute-start(bf16[1,384,2048]{2,1,0:T(8,128)(2,1)} %refs_2_.3), channel_id=1, source_target_pairs={{0,1},{1,0},{2,3},{3,2},{4,5},{5,4},{6,7},{7,6},{8,9},{9,8},{10,11... | collective-permute-start | bytes 4718600 | tf_op jit(solution)/shard_map/ppermute | solution.py:271
  37.0 11.7 %collective-permute-start.6 = (bf16[16,2048]{1,0:T(8,128)(2,1)S(1)}, bf16[16,2048]{1,0:T(8,128)(2,1)S(1)}, u32[]{:S(2)}, u32[]{:S(2)}) collective-permute-start(bf16[16,2048]{1,0:T(8,128)(2,1)S(1)} %add_parts.2.refs_0_), channel_id=1, source_target_pairs={{0,512},{512,0},{1,513},{513,1},{2,514},{514,2},{3,515},{515,3},{4... | collective-permute-start | bytes 196616 | tf_op jit(solution)/shard_map/ppermute | solution.py:271
  47.6 45.0 %copy-start.3 = (bf16[256,128]{1,0:T(8,128)(2,1)S(1)}, bf16[256,128]{1,0:T(8,128)(2,1)}, u32[]{:S(2)}) copy-start(bf16[256,128]{1,0:T(8,128)(2,1)} %get-tuple-element.29.combine_ref) | copy-start | bytes 196612
  48.7 43.8 %all-to-all-start.1 = ((bf16[16,16,2048]{2,1,0:T(8,128)(2,1)}), bf16[16,16,2048]{2,1,0:T(8,128)(2,1)S(1)}, u32[]{:S(2)}, u32[]{:S(2)}) async-start(bf16[16,16,2048]{2,1,0:T(8,128)(2,1)} %bitcast.14), calls=%async_computation.1 | async-start | bytes 2097152 | tf_op jit(solution)/shard_map/all_to_all | solution.py:288
  55.2 41.0 %copy-start = (f32[3,64,2048]{2,1,0:T(8,128)S(1)}, f32[3,64,2048]{2,1,0:T(8,128)}, u32[]{:S(2)}) copy-start(f32[3,64,2048]{2,1,0:T(8,128)} %refs_4_.1) | copy-start | bytes 4718596
  55.2 41.0 %copy-start.1 = (f32[64,2048]{1,0:T(8,128)S(1)}, f32[64,2048]{1,0:T(8,128)}, u32[]{:S(2)}) copy-start(f32[64,2048]{1,0:T(8,128)} %refs_5_.1) | copy-start | bytes 1572868
  80.1 13.6 %collective-permute-start.7 = (bf16[16,2048]{1,0:T(8,128)(2,1)S(1)}, bf16[16,2048]{1,0:T(8,128)(2,1)S(1)}, u32[]{:S(2)}, u32[]{:S(2)}) collective-permute-start(bf16[16,2048]{1,0:T(8,128)(2,1)S(1)} %total.1.refs_0_), channel_id=1, source_target_pairs={{0,32},{32,64},{64,96},{96,0},{1,33},{33,65},{65,97},{97,1},{2,34}... | collective-permute-start | bytes 196616 | tf_op jit(solution)/shard_map/ppermute | solution.py:271
  84.1 9.7 %collective-permute-start.8 = (bf16[16,2048]{1,0:T(8,128)(2,1)S(1)}, bf16[16,2048]{1,0:T(8,128)(2,1)S(1)}, u32[]{:S(2)}, u32[]{:S(2)}) collective-permute-start(bf16[16,2048]{1,0:T(8,128)(2,1)S(1)} %total.1.refs_0_), channel_id=1, source_target_pairs={{0,64},{32,96},{64,0},{96,32},{1,65},{33,97},{65,1},{97,33},{2,66}... | collective-permute-start | bytes 196616 | tf_op jit(solution)/shard_map/ppermute | solution.py:271
  90.0 6.2 %collective-permute-start.9 = (bf16[16,2048]{1,0:T(8,128)(2,1)S(1)}, bf16[16,2048]{1,0:T(8,128)(2,1)S(1)}, u32[]{:S(2)}, u32[]{:S(2)}) collective-permute-start(bf16[16,2048]{1,0:T(8,128)(2,1)S(1)} %total.1.refs_0_), channel_id=1, source_target_pairs={{0,96},{32,0},{64,32},{96,64},{1,97},{33,1},{65,33},{97,65},{2,98}... | collective-permute-start | bytes 196616 | tf_op jit(solution)/shard_map/ppermute | solution.py:271

commit v11 on v10

--- a/solution.py
+++ b/solution.py
@@ -10,6 +10,7 @@
 
 CAP = 16
 RADIX = 4
+CHUNKS = 4
 
 momentum_rate = 0.9
 outer_rate = 0.7
@@ -87,29 +88,44 @@
     sources, out_ref, targets, sems = refs[:6], refs[6], refs[7:11], refs[11]
     rows_ref, gate_ref, up_ref, down_ref = targets
     half = gate_ref.shape[1] // 2
-    moves = [(rows_hbm, rows_ref)]
-    for kind, target in enumerate((gate_ref, up_ref, down_ref)):
-        for side in range(2):
-            span = pl.ds(side * half, half)
-            source = sources[3 * side + kind].at[0]
-            moves.append((source, target.at[span] if kind == 2 else target.at[:, span]))
-    fetches = [
-        pltpu.make_async_copy(source, target, sems.at[i])
-        for i, (source, target) in enumerate(moves)
-    ]
-    for fetch in fetches[:5]:
-        fetch.start()
-    for fetch in fetches[:3]:
-        fetch.wait()
-    for fetch in fetches[5:]:
-        fetch.start()
-    rows = rows_ref[...]
-    gate = jnp.dot(rows, gate_ref[...], preferred_element_type=jnp.float32)
-    for fetch in fetches[3:5]:
-        fetch.wait()
-    up = jnp.dot(rows, up_ref[...], preferred_element_type=jnp.float32)
+    depth = rows_ref.shape[1] // CHUNKS
+    sides = [pl.ds(side * half, half) for side in range(2)]
+    stages = []
+    for chunk in range(CHUNKS):
+        deep = pl.ds(chunk * depth, depth)
+        stage = [(rows_hbm.at[:, deep], rows_ref.at[:, deep])]
+        for kind, target in enumerate((gate_ref, up_ref)):
+            for side, span in enumerate(sides):
+                stage.append((sources[3 * side + kind].at[0, deep], target.at[deep, span]))
+        stages.append(stage)
+    stages.append([(sources[3 * side + 2].at[0], down_ref.at[sides[side]]) for side in range(2)])
+    fetches = []
+    for stage in stages:
+        first = sum(len(done) for done in fetches)
+        fetches.append(
+            [
+                pltpu.make_async_copy(source, target, sems.at[first + i])
+                for i, (source, target) in enumerate(stage)
+            ]
+        )
+    for stage in fetches[:2]:
+        for fetch in stage:
+            fetch.start()
+    gate = up = None
+    for chunk in range(CHUNKS):
+        for fetch in fetches[chunk]:
+            fetch.wait()
+        if chunk + 2 < len(fetches):
+            for fetch in fetches[chunk + 2]:
+                fetch.start()
+        deep = slice(chunk * depth, (chunk + 1) * depth)
+        rows = rows_ref[:, deep]
+        gate_part = jnp.dot(rows, gate_ref[deep], preferred_element_type=jnp.float32)
+        up_part = jnp.dot(rows, up_ref[deep], preferred_element_type=jnp.float32)
+        gate = gate_part if gate is None else gate + gate_part
+        up = up_part if up is None else up + up_part
     hidden = (gate / (1.0 + jnp.exp(-gate)) * up).astype(jnp.bfloat16)
-    for fetch in fetches[5:]:
+    for fetch in fetches[CHUNKS]:
         fetch.wait()
     out_ref[...] = jnp.dot(hidden, down_ref[...], preferred_element_type=jnp.float32).astype(
         jnp.bfloat16
@@ -129,7 +145,7 @@
             wide,
             wide,
             pltpu.VMEM((2 * half, width), jnp.bfloat16),
-            pltpu.SemaphoreType.DMA((len(operands),)),
+            pltpu.SemaphoreType.DMA((5 * CHUNKS + 2,)),
         ],
         compiler_params=EXPERT_PARAMS,
         name="expert_rows",

time: 98.1 us -> 98.7 us (level)
  no operation moved by 1% of the time
where the time goes in v11:
time: 98.7 us; the launch traced here: 98 us
  starting transfers between devices  53.7 us (54%)
  blocking collectives  24.9 us (25%)
  Pallas kernels  12.8 us (13%)
  waiting for transfers between devices  5 us (5%)
  between operations  1.51 us (2%)
    ppermute x10, starting transfers between devices, shift(): lax.ppermute(part, axis, [(i, (i + step) % size) for i in range(size)])  29.6 us
    all_gather x1, blocking collectives, shards(): sums = total(lax.all_gather(part, 'z_far', axis=0))  24.9 us
    all_to_all x2, starting transfers between devices, exchange(): lax.all_to_all(rows.reshape(experts, CAP, width), 'chip', split_axis=0, c...  24.1 us
    pallas_call x1, Pallas kernels, expert_rows(): pl.pallas_call(expert_kernel, in_specs=[HBM] * len(operands), out_shape=j...  7.17 us
    ppermute x10, waiting for transfers between devices, shift(): lax.ppermute(part, axis, [(i, (i + step) % size) for i in range(size)])  4.99 us
    pallas_call x1, Pallas kernels, route(): pl.pallas_call(functools.partial(route_kernel, experts), out_shape=(jax.S...  2.56 us
  transfers between devices with their start and end apart: 12, of which 3 were waited for; matrix products, arithmetic and copies ran while one was open for 0% of the time, Pallas kernels for 9%

profile of v11, /device:TPU:6, one launch (start us, length us, event | category | flops | bytes accessed | tf_op | source)
XLA Modules:
  0.0 98.0 jit_solution(11467918116776212214)
XLA Ops:
  0.7 2.6 %route.1 = (bf16[256,2048]{1,0:T(8,128)(2,1)}, bf16[256,128]{1,0:T(8,128)(2,1)}) custom-call(s32[8,128]{1,0:T(8,128)} %bitcast.16, f32[8,128]{1,0:T(8,128)} %bitcast.17, bf16[128,2048]{1,0:T(8,128)(2,1)} %refs_2_.2), custom_call_target="tpu_custom_call" | custom-call | tf_op jit(solution)/shard_map/route/pallas_call | solution.py:73
  3.2 17.3 %all-to-all-start = ((bf16[16,16,2048]{2,1,0:T(8,128)(2,1)}), bf16[16,16,2048]{2,1,0:T(8,128)(2,1)}, u32[]{:S(2)}, u32[]{:S(2)}) async-start(bf16[16,16,2048]{2,1,0:T(8,128)(2,1)} %bitcast.15), calls=%async_computation | async-start | bytes 2097152 | tf_op jit(solution)/shard_map/all_to_all | solution.py:304
  20.5 0.6 dequant.1
  21.1 1.9 %collective-permute-start = (bf16[16,2048]{1,0:T(8,128)(2,1)S(1)}, bf16[16,2048]{1,0:T(8,128)(2,1)S(1)}, u32[]{:S(2)}, u32[]{:S(2)}) collective-permute-start(bf16[16,2048]{1,0:T(8,128)(2,1)S(1)} %get-tuple-element.21), channel_id=1, source_target_pairs={{0,32},{32,64},{64,96},{96,0},{1,33},{33,65},{65,97},{97,1},{2,34}... | collective-permute-start | bytes 196616 | tf_op jit(solution)/shard_map/ppermute | solution.py:287
  23.0 1.9 %collective-permute-start.1 = (bf16[16,2048]{1,0:T(8,128)(2,1)S(1)}, bf16[16,2048]{1,0:T(8,128)(2,1)S(1)}, u32[]{:S(2)}, u32[]{:S(2)}) collective-permute-start(bf16[16,2048]{1,0:T(8,128)(2,1)S(1)} %get-tuple-element.22), channel_id=1, source_target_pairs={{0,64},{32,96},{64,0},{96,32},{1,65},{33,97},{65,1},{97,33},{2,66}... | collective-permute-start | bytes 196616 | tf_op jit(solution)/shard_map/ppermute | solution.py:287
  25.0 5.7 %collective-permute-start.2 = (bf16[16,2048]{1,0:T(8,128)(2,1)S(1)}, bf16[16,2048]{1,0:T(8,128)(2,1)S(1)}, u32[]{:S(2)}, u32[]{:S(2)}) collective-permute-start(bf16[16,2048]{1,0:T(8,128)(2,1)S(1)} %get-tuple-element.23), channel_id=1, source_target_pairs={{0,96},{32,0},{64,32},{96,64},{1,97},{33,1},{65,33},{97,65},{2,98}... | collective-permute-start | bytes 196616 | tf_op jit(solution)/shard_map/ppermute | solution.py:287
  30.7 1.9 %collective-permute-start.3 = (bf16[1,2048,384]{2,1,0:T(8,128)(2,1)}, bf16[1,2048,384]{2,1,0:T(8,128)(2,1)}, u32[]{:S(2)}, u32[]{:S(2)}) collective-permute-start(bf16[1,2048,384]{2,1,0:T(8,128)(2,1)} %refs_0_.1), channel_id=1, source_target_pairs={{0,1},{1,0},{2,3},{3,2},{4,5},{5,4},{6,7},{7,6},{8,9},{9,8},{10,11... | collective-permute-start | bytes 4718600 | tf_op jit(solution)/shard_map/ppermute | solution.py:287
  32.6 2.4 %collective-permute-start.4 = (bf16[1,2048,384]{2,1,0:T(8,128)(2,1)}, bf16[1,2048,384]{2,1,0:T(8,128)(2,1)}, u32[]{:S(2)}, u32[]{:S(2)}) collective-permute-start(bf16[1,2048,384]{2,1,0:T(8,128)(2,1)} %refs_1_.1), channel_id=1, source_target_pairs={{0,1},{1,0},{2,3},{3,2},{4,5},{5,4},{6,7},{7,6},{8,9},{9,8},{10,11... | collective-permute-start | bytes 4718600 | tf_op jit(solution)/shard_map/ppermute | solution.py:287
  35.0 0.0 collective-permute-done.refs_1_
  35.1 1.9 %collective-permute-start.5 = (bf16[1,384,2048]{2,1,0:T(8,128)(2,1)}, bf16[1,384,2048]{2,1,0:T(8,128)(2,1)}, u32[]{:S(2)}, u32[]{:S(2)}) collective-permute-start(bf16[1,384,2048]{2,1,0:T(8,128)(2,1)} %refs_2_.3), channel_id=1, source_target_pairs={{0,1},{1,0},{2,3},{3,2},{4,5},{5,4},{6,7},{7,6},{8,9},{9,8},{10,11... | collective-permute-start | bytes 4718600 | tf_op jit(solution)/shard_map/ppermute | solution.py:287
  37.0 1.9 %collective-permute-start.6 = (bf16[16,2048]{1,0:T(8,128)(2,1)S(1)}, bf16[16,2048]{1,0:T(8,128)(2,1)S(1)}, u32[]{:S(2)}, u32[]{:S(2)}) collective-permute-start(bf16[16,2048]{1,0:T(8,128)(2,1)S(1)} %add_parts.2.refs_0_), channel_id=1, source_target_pairs={{0,512},{512,0},{1,513},{513,1},{2,514},{514,2},{3,515},{515,3},{4... | collective-permute-start | bytes 196616 | tf_op jit(solution)/shard_map/ppermute | solution.py:287
  39.0 1.8 %collective-permute-done.5.refs_5_ = bf16[1,384,2048]{2,1,0:T(8,128)(2,1)} collective-permute-done((bf16[1,384,2048]{2,1,0:T(8,128)(2,1)}, bf16[1,384,2048]{2,1,0:T(8,128)(2,1)}, u32[]{:S(2)}, u32[]{:S(2)}) %collective-permute-start.5) | collective-permute-done | bytes 1572896 | tf_op jit(solution)/shard_map/ppermute | solution.py:287
  40.8 7.2 %expert_rows.1 = bf16[256,2048]{1,0:T(8,128)(2,1)} custom-call(bf16[256,2048]{1,0:T(8,128)(2,1)} %bitcast.3.rows_hbm, bf16[1,2048,384]{2,1,0:T(8,128)(2,1)} %refs_0_.1, bf16[1,2048,384]{2,1,0:T(8,128)(2,1)} %refs_1_.1, bf16[1,384,2048]{2,1,0:T(8,128)(2,1)} %refs_2_.3, bf16[1,2048,384]{2,1,0:T(8,128)(2,1)} %collective-permute-done.3.refs_3_, ...), custom_call_target="tpu_custom_call" | custom-call | tf_op jit(solution)/shard_map/expert_rows/pallas_call | solution.py:139
  48.0 0.0 copy-start.3
  48.0 0.7 collective-permute-done.6.refs_1_
  48.7 6.8 %all-to-all-start.1 = ((bf16[16,16,2048]{2,1,0:T(8,128)(2,1)}), bf16[16,16,2048]{2,1,0:T(8,128)(2,1)S(1)}, u32[]{:S(2)}, u32[]{:S(2)}) async-start(bf16[16,16,2048]{2,1,0:T(8,128)(2,1)} %bitcast.14), calls=%async_computation.1 | async-start | bytes 2097152 | tf_op jit(solution)/shard_map/all_to_all | solution.py:304
  55.6 0.0 copy-start.1
  55.6 24.9 %all-gather = bf16[64,2048]{1,0:T(8,128)(2,1)S(1)} all-gather(bf16[16,2048]{1,0:T(8,128)(2,1)S(1)} %add_parts.3), channel_id=2, replica_groups=mesh['y_far'=2,'z_far'=4,'z_near'=4,'chip'=16,'core'=2] {'z_far'}, dimensions={0}, use_global_device_ids=true | all-gather | bytes 327680 | tf_op jit(solution)/shard_map/all_gather | solution.py:336
  80.6 3.9 %collective-permute-start.7 = (bf16[16,2048]{1,0:T(8,128)(2,1)S(1)}, bf16[16,2048]{1,0:T(8,128)(2,1)S(1)}, u32[]{:S(2)}, u32[]{:S(2)}) collective-permute-start(bf16[16,2048]{1,0:T(8,128)(2,1)S(1)} %total.1.refs_0_), channel_id=1, source_target_pairs={{0,32},{32,64},{64,96},{96,0},{1,33},{33,65},{65,97},{97,1},{2,34}... | collective-permute-start | bytes 196616 | tf_op jit(solution)/shard_map/ppermute | solution.py:287
  84.5 6.0 %collective-permute-start.8 = (bf16[16,2048]{1,0:T(8,128)(2,1)S(1)}, bf16[16,2048]{1,0:T(8,128)(2,1)S(1)}, u32[]{:S(2)}, u32[]{:S(2)}) collective-permute-start(bf16[16,2048]{1,0:T(8,128)(2,1)S(1)} %total.1.refs_0_), channel_id=1, source_target_pairs={{0,64},{32,96},{64,0},{96,32},{1,65},{33,97},{65,1},{97,33},{2,66}... | collective-permute-start | bytes 196616 | tf_op jit(solution)/shard_map/ppermute | solution.py:287
  90.6 1.9 %collective-permute-start.9 = (bf16[16,2048]{1,0:T(8,128)(2,1)S(1)}, bf16[16,2048]{1,0:T(8,128)(2,1)S(1)}, u32[]{:S(2)}, u32[]{:S(2)}) collective-permute-start(bf16[16,2048]{1,0:T(8,128)(2,1)S(1)} %total.1.refs_0_), channel_id=1, source_target_pairs={{0,96},{32,0},{64,32},{96,64},{1,97},{33,1},{65,33},{97,65},{2,98}... | collective-permute-start | bytes 196616 | tf_op jit(solution)/shard_map/ppermute | solution.py:287
  93.2 1.1 %combine_rows.1 = bf16[128,2048]{1,0:T(8,128)(2,1)} custom-call(bf16[256,128]{1,0:T(8,128)(2,1)S(1)} %copy-done.3, bf16[256,2048]{1,0:T(8,128)(2,1)S(1)} %bitcast.11), custom_call_target="tpu_custom_call" | custom-call | tf_op jit(solution)/shard_map/combine_rows/pallas_call | solution.py:165
  94.3 2.4 %collective-permute-done.9.refs_3_ = bf16[16,2048]{1,0:T(8,128)(2,1)S(1)} collective-permute-done((bf16[16,2048]{1,0:T(8,128)(2,1)S(1)}, bf16[16,2048]{1,0:T(8,128)(2,1)S(1)}, u32[]{:S(2)}, u32[]{:S(2)}) %collective-permute-start.9) | collective-permute-done | bytes 65568 | tf_op jit(solution)/shard_map/ppermute | solution.py:287
  96.7 1.3 %update.1 = (f32[64,2048]{1,0:T(8,128)}, f32[64,2048]{1,0:T(8,128)}) custom-call(s32[1]{0:T(128)S(6)} %copy.14.fragment_ref, s32[1]{0:T(128)} %bitcast.4.place_ref, bf16[16,2048]{1,0:T(8,128)(2,1)S(1)} %total.1.refs_0_, bf16[16,2048]{1,0:T(8,128)(2,1)S(1)} %collective-permute-done.7.refs_1_, bf16[16,2048]{1,0:T(8,128)(2,1)S(1)} %collective-permute-done.8.refs_2_, ...), custom_call_target="tpu_custom_call" | custom-call | tf_op jit(solution)/shard_map/update/pallas_call | solution.py:262
  (19 shorter events, 0.1 us)
Async XLA Ops:
  0.6 19.9 %copy-start.2 = (bf16[1,64,2048]{2,1,0:T(8,128)(2,1)S(1)}, bf16[1,64,2048]{2,1,0:T(8,128)(2,1)}, u32[]{:S(2)}) copy-start(bf16[1,64,2048]{2,1,0:T(8,128)(2,1)} %values_ref.1) | copy-start | bytes 786436
  0.6 19.9 %copy-start.4 = (f32[1,64,16]{1,2,0:T(8,128)S(1)}, f32[1,64,16]{1,2,0:T(8,128)}, u32[]{:S(2)}) copy-start(f32[1,64,16]{1,2,0:T(8,128)} %param.18) | copy-start | bytes 12292
  3.2 35.8 %all-to-all-start = ((bf16[16,16,2048]{2,1,0:T(8,128)(2,1)}), bf16[16,16,2048]{2,1,0:T(8,128)(2,1)}, u32[]{:S(2)}, u32[]{:S(2)}) async-start(bf16[16,16,2048]{2,1,0:T(8,128)(2,1)} %bitcast.15), calls=%async_computation | async-start | bytes 2097152 | tf_op jit(solution)/shard_map/all_to_all | solution.py:304
  21.1 13.9 %collective-permute-start = (bf16[16,2048]{1,0:T(8,128)(2,1)S(1)}, bf16[16,2048]{1,0:T(8,128)(2,1)S(1)}, u32[]{:S(2)}, u32[]{:S(2)}) collective-permute-start(bf16[16,2048]{1,0:T(8,128)(2,1)S(1)} %get-tuple-element.21), channel_id=1, source_target_pairs={{0,32},{32,64},{64,96},{96,0},{1,33},{33,65},{65,97},{97,1},{2,34}... | collective-permute-start | bytes 196616 | tf_op jit(solution)/shard_map/ppermute | solution.py:287
  23.0 12.0 %collective-permute-start.1 = (bf16[16,2048]{1,0:T(8,128)(2,1)S(1)}, bf16[16,2048]{1,0:T(8,128)(2,1)S(1)}, u32[]{:S(2)}, u32[]{:S(2)}) collective-permute-start(bf16[16,2048]{1,0:T(8,128)(2,1)S(1)} %get-tuple-element.22), channel_id=1, source_target_pairs={{0,64},{32,96},{64,0},{96,32},{1,65},{33,97},{65,1},{97,33},{2,66}... | collective-permute-start | bytes 196616 | tf_op jit(solution)/shard_map/ppermute | solution.py:287
  25.0 10.1 %collective-permute-start.2 = (bf16[16,2048]{1,0:T(8,128)(2,1)S(1)}, bf16[16,2048]{1,0:T(8,128)(2,1)S(1)}, u32[]{:S(2)}, u32[]{:S(2)}) collective-permute-start(bf16[16,2048]{1,0:T(8,128)(2,1)S(1)} %get-tuple-element.23), channel_id=1, source_target_pairs={{0,96},{32,0},{64,32},{96,64},{1,97},{33,1},{65,33},{97,65},{2,98}... | collective-permute-start | bytes 196616 | tf_op jit(solution)/shard_map/ppermute | solution.py:287
  30.7 8.3 %collective-permute-start.3 = (bf16[1,2048,384]{2,1,0:T(8,128)(2,1)}, bf16[1,2048,384]{2,1,0:T(8,128)(2,1)}, u32[]{:S(2)}, u32[]{:S(2)}) collective-permute-start(bf16[1,2048,384]{2,1,0:T(8,128)(2,1)} %refs_0_.1), channel_id=1, source_target_pairs={{0,1},{1,0},{2,3},{3,2},{4,5},{5,4},{6,7},{7,6},{8,9},{9,8},{10,11... | collective-permute-start | bytes 4718600 | tf_op jit(solution)/shard_map/ppermute | solution.py:287
  32.6 6.4 %collective-permute-start.4 = (bf16[1,2048,384]{2,1,0:T(8,128)(2,1)}, bf16[1,2048,384]{2,1,0:T(8,128)(2,1)}, u32[]{:S(2)}, u32[]{:S(2)}) collective-permute-start(bf16[1,2048,384]{2,1,0:T(8,128)(2,1)} %refs_1_.1), channel_id=1, source_target_pairs={{0,1},{1,0},{2,3},{3,2},{4,5},{5,4},{6,7},{7,6},{8,9},{9,8},{10,11... | collective-permute-start | bytes 4718600 | tf_op jit(solution)/shard_map/ppermute | solution.py:287
  35.1 5.7 %collective-permute-start.5 = (bf16[1,384,2048]{2,1,0:T(8,128)(2,1)}, bf16[1,384,2048]{2,1,0:T(8,128)(2,1)}, u32[]{:S(2)}, u32[]{:S(2)}) collective-permute-start(bf16[1,384,2048]{2,1,0:T(8,128)(2,1)} %refs_2_.3), channel_id=1, source_target_pairs={{0,1},{1,0},{2,3},{3,2},{4,5},{5,4},{6,7},{7,6},{8,9},{9,8},{10,11... | collective-permute-start | bytes 4718600 | tf_op jit(solution)/shard_map/ppermute | solution.py:287
  37.0 11.7 %collective-permute-start.6 = (bf16[16,2048]{1,0:T(8,128)(2,1)S(1)}, bf16[16,2048]{1,0:T(8,128)(2,1)S(1)}, u32[]{:S(2)}, u32[]{:S(2)}) collective-permute-start(bf16[16,2048]{1,0:T(8,128)(2,1)S(1)} %add_parts.2.refs_0_), channel_id=1, source_target_pairs={{0,512},{512,0},{1,513},{513,1},{2,514},{514,2},{3,515},{515,3},{4... | collective-permute-start | bytes 196616 | tf_op jit(solution)/shard_map/ppermute | solution.py:287
  48.0 45.1 %copy-start.3 = (bf16[256,128]{1,0:T(8,128)(2,1)S(1)}, bf16[256,128]{1,0:T(8,128)(2,1)}, u32[]{:S(2)}) copy-start(bf16[256,128]{1,0:T(8,128)(2,1)} %get-tuple-element.29.combine_ref) | copy-start | bytes 196612
  48.7 44.4 %all-to-all-start.1 = ((bf16[16,16,2048]{2,1,0:T(8,128)(2,1)}), bf16[16,16,2048]{2,1,0:T(8,128)(2,1)S(1)}, u32[]{:S(2)}, u32[]{:S(2)}) async-start(bf16[16,16,2048]{2,1,0:T(8,128)(2,1)} %bitcast.14), calls=%async_computation.1 | async-start | bytes 2097152 | tf_op jit(solution)/shard_map/all_to_all | solution.py:304
  55.6 41.2 %copy-start = (f32[3,64,2048]{2,1,0:T(8,128)S(1)}, f32[3,64,2048]{2,1,0:T(8,128)}, u32[]{:S(2)}) copy-start(f32[3,64,2048]{2,1,0:T(8,128)} %refs_4_.1) | copy-start | bytes 4718596
  55.6 41.2 %copy-start.1 = (f32[64,2048]{1,0:T(8,128)S(1)}, f32[64,2048]{1,0:T(8,128)}, u32[]{:S(2)}) copy-start(f32[64,2048]{1,0:T(8,128)} %refs_5_.1) | copy-start | bytes 1572868
  80.6 13.7 %collective-permute-start.7 = (bf16[16,2048]{1,0:T(8,128)(2,1)S(1)}, bf16[16,2048]{1,0:T(8,128)(2,1)S(1)}, u32[]{:S(2)}, u32[]{:S(2)}) collective-permute-start(bf16[16,2048]{1,0:T(8,128)(2,1)S(1)} %total.1.refs_0_), channel_id=1, source_target_pairs={{0,32},{32,64},{64,96},{96,0},{1,33},{33,65},{65,97},{97,1},{2,34}... | collective-permute-start | bytes 196616 | tf_op jit(solution)/shard_map/ppermute | solution.py:287
  84.5 9.8 %collective-permute-start.8 = (bf16[16,2048]{1,0:T(8,128)(2,1)S(1)}, bf16[16,2048]{1,0:T(8,128)(2,1)S(1)}, u32[]{:S(2)}, u32[]{:S(2)}) collective-permute-start(bf16[16,2048]{1,0:T(8,128)(2,1)S(1)} %total.1.refs_0_), channel_id=1, source_target_pairs={{0,64},{32,96},{64,0},{96,32},{1,65},{33,97},{65,1},{97,33},{2,66}... | collective-permute-start | bytes 196616 | tf_op jit(solution)/shard_map/ppermute | solution.py:287
  90.6 6.2 %collective-permute-start.9 = (bf16[16,2048]{1,0:T(8,128)(2,1)S(1)}, bf16[16,2048]{1,0:T(8,128)(2,1)S(1)}, u32[]{:S(2)}, u32[]{:S(2)}) collective-permute-start(bf16[16,2048]{1,0:T(8,128)(2,1)S(1)} %total.1.refs_0_), channel_id=1, source_target_pairs={{0,96},{32,0},{64,32},{96,64},{1,97},{33,1},{65,33},{97,65},{2,98}... | collective-permute-start | bytes 196616 | tf_op jit(solution)/shard_map/ppermute | solution.py:287

commit v12 on v8

--- a/solution.py
+++ b/solution.py
@@ -309,8 +309,9 @@
     own = (w_gate, w_up, w_down)
     near = place_on("z_near")
     part = add_parts(scatter_stage(dequant(near, pseudo_values, block_scales), "z_near"))
+    part, sent = lax.optimization_barrier((part, own))
+    other = tuple(shift(w, "core", 1) for w in sent)
     apart = shift(part, "y_far", 1)
-    other = tuple(shift(w, "core", 1) for w in own)
     mine, part = lax.optimization_barrier((mine, part))
     rows = expert_rows(mine, own, other)
     rows, apart = lax.optimization_barrier((rows, apart))

time: 97.7 us -> 99.6 us (1.019)
  waiting for transfers between devices: 12.2 us -> 8.21 us
  starting transfers between devices: 47.6 us -> 51.5 us
  blocking collectives: 23.4 us -> 24.8 us
    ppermute x10, starting transfers between devices: 23.5 us -> 27.8 us  [shift(): lax.ppermute(part, axis, [(i, (i + step) % size) for i in range(size)])]
    ppermute x10, waiting for transfers between devices: 12.2 us -> 8.21 us  [shift(): lax.ppermute(part, axis, [(i, (i + step) % size) for i in range(size)])]
    all_gather x1, blocking collectives: 23.4 us -> 24.8 us  [shards(): sums = total(lax.all_gather(part, 'z_far', axis=0))]
  transfers between devices with their start and end apart: 12 -> 12, of which waited for: 5 -> 4; matrix products, arithmetic and copies ran while one was open for 0% -> 0% of each run, Pallas kernels for 9% -> 9%
where the time goes in v12:
time: 99.6 us; the launch traced here: 98.4 us
  starting transfers between devices  51.5 us (52%)
  blocking collectives  24.8 us (25%)
  Pallas kernels  12.4 us (12%)
  waiting for transfers between devices  8.21 us (8%)
  between operations  1.5 us (2%)
    ppermute x10, starting transfers between devices, shift(): lax.ppermute(part, axis, [(i, (i + step) % size) for i in range(size)])  27.8 us
    all_gather x1, blocking collectives, shards(): sums = total(lax.all_gather(part, 'z_far', axis=0))  24.8 us
    all_to_all x2, starting transfers between devices, exchange(): lax.all_to_all(rows.reshape(experts, CAP, width), 'chip', split_axis=0, c...  23.7 us
    ppermute x10, waiting for transfers between devices, shift(): lax.ppermute(part, axis, [(i, (i + step) % size) for i in range(size)])  8.21 us
    pallas_call x1, Pallas kernels, expert_rows(): pl.pallas_call(expert_kernel, in_specs=[HBM] * len(operands), out_shape=j...  6.72 us
    pallas_call x1, Pallas kernels, route(): pl.pallas_call(functools.partial(route_kernel, experts), out_shape=(jax.S...  2.56 us
  transfers between devices with their start and end apart: 12, of which 4 were waited for; matrix products, arithmetic and copies ran while one was open for 0% of the time, Pallas kernels for 9%

profile of v12, /device:TPU:6, one launch (start us, length us, event | category | flops | bytes accessed | tf_op | source)
XLA Modules:
  0.0 98.4 jit_solution(13248249965050922777)
XLA Ops:
  0.7 2.6 %route.1 = (bf16[256,2048]{1,0:T(8,128)(2,1)}, bf16[256,128]{1,0:T(8,128)(2,1)}) custom-call(s32[8,128]{1,0:T(8,128)} %bitcast.16, f32[8,128]{1,0:T(8,128)} %bitcast.17, bf16[128,2048]{1,0:T(8,128)(2,1)} %refs_2_.2), custom_call_target="tpu_custom_call" | custom-call | tf_op jit(solution)/shard_map/route/pallas_call | solution.py:72
  3.2 17.3 %all-to-all-start = ((bf16[16,16,2048]{2,1,0:T(8,128)(2,1)}), bf16[16,16,2048]{2,1,0:T(8,128)(2,1)}, u32[]{:S(2)}, u32[]{:S(2)}) async-start(bf16[16,16,2048]{2,1,0:T(8,128)(2,1)} %bitcast.15), calls=%async_computation | async-start | bytes 2097152 | tf_op jit(solution)/shard_map/all_to_all | solution.py:288
  20.5 0.6 dequant.1
  21.1 1.9 %collective-permute-start = (bf16[16,2048]{1,0:T(8,128)(2,1)S(1)}, bf16[16,2048]{1,0:T(8,128)(2,1)S(1)}, u32[]{:S(2)}, u32[]{:S(2)}) collective-permute-start(bf16[16,2048]{1,0:T(8,128)(2,1)S(1)} %get-tuple-element.23), channel_id=1, source_target_pairs={{0,32},{32,64},{64,96},{96,0},{1,33},{33,65},{65,97},{97,1},{2,34}... | collective-permute-start | bytes 196616 | tf_op jit(solution)/shard_map/ppermute | solution.py:271
  23.0 1.9 %collective-permute-start.1 = (bf16[16,2048]{1,0:T(8,128)(2,1)S(1)}, bf16[16,2048]{1,0:T(8,128)(2,1)S(1)}, u32[]{:S(2)}, u32[]{:S(2)}) collective-permute-start(bf16[16,2048]{1,0:T(8,128)(2,1)S(1)} %get-tuple-element.24), channel_id=1, source_target_pairs={{0,64},{32,96},{64,0},{96,32},{1,65},{33,97},{65,1},{97,33},{2,66}... | collective-permute-start | bytes 196616 | tf_op jit(solution)/shard_map/ppermute | solution.py:271
  25.0 5.7 %collective-permute-start.2 = (bf16[16,2048]{1,0:T(8,128)(2,1)S(1)}, bf16[16,2048]{1,0:T(8,128)(2,1)S(1)}, u32[]{:S(2)}, u32[]{:S(2)}) collective-permute-start(bf16[16,2048]{1,0:T(8,128)(2,1)S(1)} %get-tuple-element.25), channel_id=1, source_target_pairs={{0,96},{32,0},{64,32},{96,64},{1,97},{33,1},{65,33},{97,65},{2,98}... | collective-permute-start | bytes 196616 | tf_op jit(solution)/shard_map/ppermute | solution.py:271
  30.7 2.8 %collective-permute-done.2.refs_3_ = bf16[16,2048]{1,0:T(8,128)(2,1)S(1)} collective-permute-done((bf16[16,2048]{1,0:T(8,128)(2,1)S(1)}, bf16[16,2048]{1,0:T(8,128)(2,1)S(1)}, u32[]{:S(2)}, u32[]{:S(2)}) %collective-permute-start.2) | collective-permute-done | bytes 65568 | tf_op jit(solution)/shard_map/ppermute | solution.py:271
  33.5 1.9 %collective-permute-start.3 = (bf16[1,2048,384]{2,1,0:T(8,128)(2,1)}, bf16[1,2048,384]{2,1,0:T(8,128)(2,1)}, u32[]{:S(2)}, u32[]{:S(2)}) collective-permute-start(bf16[1,2048,384]{2,1,0:T(8,128)(2,1)} %refs_0_.1), channel_id=1, source_target_pairs={{0,1},{1,0},{2,3},{3,2},{4,5},{5,4},{6,7},{7,6},{8,9},{9,8},{10,11... | collective-permute-start | bytes 4718600 | tf_op jit(solution)/shard_map/ppermute | solution.py:271
  35.4 2.4 %collective-permute-start.4 = (bf16[1,2048,384]{2,1,0:T(8,128)(2,1)}, bf16[1,2048,384]{2,1,0:T(8,128)(2,1)}, u32[]{:S(2)}, u32[]{:S(2)}) collective-permute-start(bf16[1,2048,384]{2,1,0:T(8,128)(2,1)} %refs_1_.1), channel_id=1, source_target_pairs={{0,1},{1,0},{2,3},{3,2},{4,5},{5,4},{6,7},{7,6},{8,9},{9,8},{10,11... | collective-permute-start | bytes 4718600 | tf_op jit(solution)/shard_map/ppermute | solution.py:271
  37.9 1.9 %collective-permute-start.5 = (bf16[1,384,2048]{2,1,0:T(8,128)(2,1)}, bf16[1,384,2048]{2,1,0:T(8,128)(2,1)}, u32[]{:S(2)}, u32[]{:S(2)}) collective-permute-start(bf16[1,384,2048]{2,1,0:T(8,128)(2,1)} %refs_2_.3), channel_id=1, source_target_pairs={{0,1},{1,0},{2,3},{3,2},{4,5},{5,4},{6,7},{7,6},{8,9},{9,8},{10,11... | collective-permute-start | bytes 4718600 | tf_op jit(solution)/shard_map/ppermute | solution.py:271
  39.8 1.9 %collective-permute-start.6 = (bf16[16,2048]{1,0:T(8,128)(2,1)S(1)}, bf16[16,2048]{1,0:T(8,128)(2,1)S(1)}, u32[]{:S(2)}, u32[]{:S(2)}) collective-permute-start(bf16[16,2048]{1,0:T(8,128)(2,1)S(1)} %add_parts.2.refs_0_), channel_id=1, source_target_pairs={{0,512},{512,0},{1,513},{513,1},{2,514},{514,2},{3,515},{515,3},{4... | collective-permute-start | bytes 196616 | tf_op jit(solution)/shard_map/ppermute | solution.py:271
  41.8 1.9 %collective-permute-done.5.refs_5_ = bf16[1,384,2048]{2,1,0:T(8,128)(2,1)} collective-permute-done((bf16[1,384,2048]{2,1,0:T(8,128)(2,1)}, bf16[1,384,2048]{2,1,0:T(8,128)(2,1)}, u32[]{:S(2)}, u32[]{:S(2)}) %collective-permute-start.5) | collective-permute-done | bytes 1572896 | tf_op jit(solution)/shard_map/ppermute | solution.py:271
  43.7 6.7 %expert_rows.1 = bf16[256,2048]{1,0:T(8,128)(2,1)} custom-call(bf16[256,2048]{1,0:T(8,128)(2,1)} %bitcast.3.rows_hbm, bf16[1,2048,384]{2,1,0:T(8,128)(2,1)} %refs_0_.1, bf16[1,2048,384]{2,1,0:T(8,128)(2,1)} %refs_1_.1, bf16[1,384,2048]{2,1,0:T(8,128)(2,1)} %refs_2_.3, bf16[1,2048,384]{2,1,0:T(8,128)(2,1)} %collective-permute-done.3.refs_3_, ...), custom_call_target="tpu_custom_call" | custom-call | tf_op jit(solution)/shard_map/expert_rows/pallas_call | solution.py:123
  50.4 0.0 copy-start.3
  50.4 1.1 %collective-permute-done.6.refs_1_ = bf16[16,2048]{1,0:T(8,128)(2,1)S(1)} collective-permute-done((bf16[16,2048]{1,0:T(8,128)(2,1)S(1)}, bf16[16,2048]{1,0:T(8,128)(2,1)S(1)}, u32[]{:S(2)}, u32[]{:S(2)}) %collective-permute-start.6) | collective-permute-done | bytes 65568 | tf_op jit(solution)/shard_map/ppermute | solution.py:271
  51.5 6.5 %all-to-all-start.1 = ((bf16[16,16,2048]{2,1,0:T(8,128)(2,1)}), bf16[16,16,2048]{2,1,0:T(8,128)(2,1)S(1)}, u32[]{:S(2)}, u32[]{:S(2)}) async-start(bf16[16,16,2048]{2,1,0:T(8,128)(2,1)} %bitcast.14), calls=%async_computation.1 | async-start | bytes 2097152 | tf_op jit(solution)/shard_map/all_to_all | solution.py:288
  58.0 0.0 copy-start.1
  58.0 24.8 %all-gather = bf16[64,2048]{1,0:T(8,128)(2,1)S(1)} all-gather(bf16[16,2048]{1,0:T(8,128)(2,1)S(1)} %add_parts.3), channel_id=2, replica_groups=mesh['y_far'=2,'z_far'=4,'z_near'=4,'chip'=16,'core'=2] {'z_far'}, dimensions={0}, use_global_device_ids=true | all-gather | bytes 327680 | tf_op jit(solution)/shard_map/all_gather | solution.py:320
  82.8 1.9 %collective-permute-start.7 = (bf16[16,2048]{1,0:T(8,128)(2,1)S(1)}, bf16[16,2048]{1,0:T(8,128)(2,1)S(1)}, u32[]{:S(2)}, u32[]{:S(2)}) collective-permute-start(bf16[16,2048]{1,0:T(8,128)(2,1)S(1)} %total.1.refs_0_), channel_id=1, source_target_pairs={{0,32},{32,64},{64,96},{96,0},{1,33},{33,65},{65,97},{97,1},{2,34}... | collective-permute-start | bytes 196616 | tf_op jit(solution)/shard_map/ppermute | solution.py:271
  84.7 6.2 %collective-permute-start.8 = (bf16[16,2048]{1,0:T(8,128)(2,1)S(1)}, bf16[16,2048]{1,0:T(8,128)(2,1)S(1)}, u32[]{:S(2)}, u32[]{:S(2)}) collective-permute-start(bf16[16,2048]{1,0:T(8,128)(2,1)S(1)} %total.1.refs_0_), channel_id=1, source_target_pairs={{0,64},{32,96},{64,0},{96,32},{1,65},{33,97},{65,1},{97,33},{2,66}... | collective-permute-start | bytes 196616 | tf_op jit(solution)/shard_map/ppermute | solution.py:271
  90.9 1.9 %collective-permute-start.9 = (bf16[16,2048]{1,0:T(8,128)(2,1)S(1)}, bf16[16,2048]{1,0:T(8,128)(2,1)S(1)}, u32[]{:S(2)}, u32[]{:S(2)}) collective-permute-start(bf16[16,2048]{1,0:T(8,128)(2,1)S(1)} %total.1.refs_0_), channel_id=1, source_target_pairs={{0,96},{32,0},{64,32},{96,64},{1,97},{33,1},{65,33},{97,65},{2,98}... | collective-permute-start | bytes 196616 | tf_op jit(solution)/shard_map/ppermute | solution.py:271
  93.5 1.1 %combine_rows.1 = bf16[128,2048]{1,0:T(8,128)(2,1)} custom-call(bf16[256,128]{1,0:T(8,128)(2,1)S(1)} %copy-done.3, bf16[256,2048]{1,0:T(8,128)(2,1)S(1)} %bitcast.11), custom_call_target="tpu_custom_call" | custom-call | tf_op jit(solution)/shard_map/combine_rows/pallas_call | solution.py:149
  94.6 2.4 %collective-permute-done.9.refs_3_ = bf16[16,2048]{1,0:T(8,128)(2,1)S(1)} collective-permute-done((bf16[16,2048]{1,0:T(8,128)(2,1)S(1)}, bf16[16,2048]{1,0:T(8,128)(2,1)S(1)}, u32[]{:S(2)}, u32[]{:S(2)}) %collective-permute-start.9) | collective-permute-done | bytes 65568 | tf_op jit(solution)/shard_map/ppermute | solution.py:271
  97.1 1.3 %update.1 = (f32[64,2048]{1,0:T(8,128)}, f32[64,2048]{1,0:T(8,128)}) custom-call(s32[1]{0:T(128)S(6)} %copy.14.fragment_ref, s32[1]{0:T(128)} %bitcast.4.place_ref, bf16[16,2048]{1,0:T(8,128)(2,1)S(1)} %total.1.refs_0_, bf16[16,2048]{1,0:T(8,128)(2,1)S(1)} %collective-permute-done.7.refs_1_, bf16[16,2048]{1,0:T(8,128)(2,1)S(1)} %collective-permute-done.8.refs_2_, ...), custom_call_target="tpu_custom_call" | custom-call | tf_op jit(solution)/shard_map/update/pallas_call | solution.py:246
  (19 shorter events, 0.1 us)
Async XLA Ops:
  0.6 19.9 %copy-start.2 = (bf16[1,64,2048]{2,1,0:T(8,128)(2,1)S(1)}, bf16[1,64,2048]{2,1,0:T(8,128)(2,1)}, u32[]{:S(2)}) copy-start(bf16[1,64,2048]{2,1,0:T(8,128)(2,1)} %values_ref.1) | copy-start | bytes 786436
  0.6 19.9 %copy-start.4 = (f32[1,64,16]{1,2,0:T(8,128)S(1)}, f32[1,64,16]{1,2,0:T(8,128)}, u32[]{:S(2)}) copy-start(f32[1,64,16]{1,2,0:T(8,128)} %param.18) | copy-start | bytes 12292
  3.2 38.5 %all-to-all-start = ((bf16[16,16,2048]{2,1,0:T(8,128)(2,1)}), bf16[16,16,2048]{2,1,0:T(8,128)(2,1)}, u32[]{:S(2)}, u32[]{:S(2)}) async-start(bf16[16,16,2048]{2,1,0:T(8,128)(2,1)} %bitcast.15), calls=%async_computation | async-start | bytes 2097152 | tf_op jit(solution)/shard_map/all_to_all | solution.py:288
  21.1 9.6 %collective-permute-start = (bf16[16,2048]{1,0:T(8,128)(2,1)S(1)}, bf16[16,2048]{1,0:T(8,128)(2,1)S(1)}, u32[]{:S(2)}, u32[]{:S(2)}) collective-permute-start(bf16[16,2048]{1,0:T(8,128)(2,1)S(1)} %get-tuple-element.23), channel_id=1, source_target_pairs={{0,32},{32,64},{64,96},{96,0},{1,33},{33,65},{65,97},{97,1},{2,34}... | collective-permute-start | bytes 196616 | tf_op jit(solution)/shard_map/ppermute | solution.py:271
  23.0 7.7 %collective-permute-start.1 = (bf16[16,2048]{1,0:T(8,128)(2,1)S(1)}, bf16[16,2048]{1,0:T(8,128)(2,1)S(1)}, u32[]{:S(2)}, u32[]{:S(2)}) collective-permute-start(bf16[16,2048]{1,0:T(8,128)(2,1)S(1)} %get-tuple-element.24), channel_id=1, source_target_pairs={{0,64},{32,96},{64,0},{96,32},{1,65},{33,97},{65,1},{97,33},{2,66}... | collective-permute-start | bytes 196616 | tf_op jit(solution)/shard_map/ppermute | solution.py:271
  25.0 8.5 %collective-permute-start.2 = (bf16[16,2048]{1,0:T(8,128)(2,1)S(1)}, bf16[16,2048]{1,0:T(8,128)(2,1)S(1)}, u32[]{:S(2)}, u32[]{:S(2)}) collective-permute-start(bf16[16,2048]{1,0:T(8,128)(2,1)S(1)} %get-tuple-element.25), channel_id=1, source_target_pairs={{0,96},{32,0},{64,32},{96,64},{1,97},{33,1},{65,33},{97,65},{2,98}... | collective-permute-start | bytes 196616 | tf_op jit(solution)/shard_map/ppermute | solution.py:271
  33.5 8.2 %collective-permute-start.3 = (bf16[1,2048,384]{2,1,0:T(8,128)(2,1)}, bf16[1,2048,384]{2,1,0:T(8,128)(2,1)}, u32[]{:S(2)}, u32[]{:S(2)}) collective-permute-start(bf16[1,2048,384]{2,1,0:T(8,128)(2,1)} %refs_0_.1), channel_id=1, source_target_pairs={{0,1},{1,0},{2,3},{3,2},{4,5},{5,4},{6,7},{7,6},{8,9},{9,8},{10,11... | collective-permute-start | bytes 4718600 | tf_op jit(solution)/shard_map/ppermute | solution.py:271
  35.4 6.3 %collective-permute-start.4 = (bf16[1,2048,384]{2,1,0:T(8,128)(2,1)}, bf16[1,2048,384]{2,1,0:T(8,128)(2,1)}, u32[]{:S(2)}, u32[]{:S(2)}) collective-permute-start(bf16[1,2048,384]{2,1,0:T(8,128)(2,1)} %refs_1_.1), channel_id=1, source_target_pairs={{0,1},{1,0},{2,3},{3,2},{4,5},{5,4},{6,7},{7,6},{8,9},{9,8},{10,11... | collective-permute-start | bytes 4718600 | tf_op jit(solution)/shard_map/ppermute | solution.py:271
  37.9 5.8 %collective-permute-start.5 = (bf16[1,384,2048]{2,1,0:T(8,128)(2,1)}, bf16[1,384,2048]{2,1,0:T(8,128)(2,1)}, u32[]{:S(2)}, u32[]{:S(2)}) collective-permute-start(bf16[1,384,2048]{2,1,0:T(8,128)(2,1)} %refs_2_.3), channel_id=1, source_target_pairs={{0,1},{1,0},{2,3},{3,2},{4,5},{5,4},{6,7},{7,6},{8,9},{9,8},{10,11... | collective-permute-start | bytes 4718600 | tf_op jit(solution)/shard_map/ppermute | solution.py:271
  39.8 11.7 %collective-permute-start.6 = (bf16[16,2048]{1,0:T(8,128)(2,1)S(1)}, bf16[16,2048]{1,0:T(8,128)(2,1)S(1)}, u32[]{:S(2)}, u32[]{:S(2)}) collective-permute-start(bf16[16,2048]{1,0:T(8,128)(2,1)S(1)} %add_parts.2.refs_0_), channel_id=1, source_target_pairs={{0,512},{512,0},{1,513},{513,1},{2,514},{514,2},{3,515},{515,3},{4... | collective-permute-start | bytes 196616 | tf_op jit(solution)/shard_map/ppermute | solution.py:271
  50.4 43.1 %copy-start.3 = (bf16[256,128]{1,0:T(8,128)(2,1)S(1)}, bf16[256,128]{1,0:T(8,128)(2,1)}, u32[]{:S(2)}) copy-start(bf16[256,128]{1,0:T(8,128)(2,1)} %get-tuple-element.33.combine_ref) | copy-start | bytes 196612
  51.5 42.0 %all-to-all-start.1 = ((bf16[16,16,2048]{2,1,0:T(8,128)(2,1)}), bf16[16,16,2048]{2,1,0:T(8,128)(2,1)S(1)}, u32[]{:S(2)}, u32[]{:S(2)}) async-start(bf16[16,16,2048]{2,1,0:T(8,128)(2,1)} %bitcast.14), calls=%async_computation.1 | async-start | bytes 2097152 | tf_op jit(solution)/shard_map/all_to_all | solution.py:288
  58.0 39.1 %copy-start = (f32[3,64,2048]{2,1,0:T(8,128)S(1)}, f32[3,64,2048]{2,1,0:T(8,128)}, u32[]{:S(2)}) copy-start(f32[3,64,2048]{2,1,0:T(8,128)} %refs_4_.1) | copy-start | bytes 4718596
  58.0 39.1 %copy-start.1 = (f32[64,2048]{1,0:T(8,128)S(1)}, f32[64,2048]{1,0:T(8,128)}, u32[]{:S(2)}) copy-start(f32[64,2048]{1,0:T(8,128)} %refs_5_.1) | copy-start | bytes 1572868
  82.8 11.8 %collective-permute-start.7 = (bf16[16,2048]{1,0:T(8,128)(2,1)S(1)}, bf16[16,2048]{1,0:T(8,128)(2,1)S(1)}, u32[]{:S(2)}, u32[]{:S(2)}) collective-permute-start(bf16[16,2048]{1,0:T(8,128)(2,1)S(1)} %total.1.refs_0_), channel_id=1, source_target_pairs={{0,32},{32,64},{64,96},{96,0},{1,33},{33,65},{65,97},{97,1},{2,34}... | collective-permute-start | bytes 196616 | tf_op jit(solution)/shard_map/ppermute | solution.py:271
  84.7 9.9 %collective-permute-start.8 = (bf16[16,2048]{1,0:T(8,128)(2,1)S(1)}, bf16[16,2048]{1,0:T(8,128)(2,1)S(1)}, u32[]{:S(2)}, u32[]{:S(2)}) collective-permute-start(bf16[16,2048]{1,0:T(8,128)(2,1)S(1)} %total.1.refs_0_), channel_id=1, source_target_pairs={{0,64},{32,96},{64,0},{96,32},{1,65},{33,97},{65,1},{97,33},{2,66}... | collective-permute-start | bytes 196616 | tf_op jit(solution)/shard_map/ppermute | solution.py:271
  90.9 6.2 %collective-permute-start.9 = (bf16[16,2048]{1,0:T(8,128)(2,1)S(1)}, bf16[16,2048]{1,0:T(8,128)(2,1)S(1)}, u32[]{:S(2)}, u32[]{:S(2)}) collective-permute-start(bf16[16,2048]{1,0:T(8,128)(2,1)S(1)} %total.1.refs_0_), channel_id=1, source_target_pairs={{0,96},{32,0},{64,32},{96,64},{1,97},{33,1},{65,33},{97,65},{2,98}... | collective-permute-start | bytes 196616 | tf_op jit(solution)/shard_map/ppermute | solution.py:271

commit v13 on v10

--- a/solution.py
+++ b/solution.py
@@ -206,53 +206,45 @@
 
 
 def total_kernel(parts_ref, out_ref):
-    out_ref[...] = jnp.sum(parts_ref[...].astype(jnp.float32), axis=0).astype(jnp.bfloat16)
-
-
-def total(parts):
+    total = jnp.sum(parts_ref[...].astype(jnp.float32), axis=0).astype(jnp.bfloat16)
+    out_ref[...] = jnp.broadcast_to(total[None], out_ref.shape)
+
+
+def total_spread(parts):
     return pl.pallas_call(
         total_kernel,
-        out_shape=jax.ShapeDtypeStruct(parts.shape[1:], jnp.bfloat16),
-        compiler_params=PARAMS,
-        name="total",
+        out_shape=jax.ShapeDtypeStruct((RADIX,) + parts.shape[1:], jnp.bfloat16),
+        compiler_params=PARAMS,
+        name="total_spread",
     )(parts)
 
 
-def update_kernel(replicas, fragment_ref, place_ref, *refs):
-    part_refs = refs[:RADIX]
-    base_ref, momentum_ref, params_out, momentum_out = refs[RADIX:]
-    rows = part_refs[0].shape[0]
-    for place in range(RADIX):
-        for step, ref in enumerate(part_refs):
-
-            @pl.when((place_ref[0] + RADIX - step) % RADIX == place)
-            def _():
-                span = pl.ds(place * rows, rows)
-                delta = ref[...].astype(jnp.float32) / replicas
-                new_momentum = momentum_rate * momentum_ref[span, :] + delta
-                momentum_out[span, :] = new_momentum
-                params_out[span, :] = base_ref[0, span, :] - outer_rate * (
-                    delta + momentum_rate * new_momentum
-                )
-
-
-def update(replicas, place, parts, outer_params, momentum, fragment):
+def update_kernel(replicas, fragment_ref, totals_ref, base_ref, momentum_ref, params_out, momentum_out):
+    pieces, rows, _ = totals_ref.shape
+    for piece in range(pieces):
+        at = pl.ds(piece * rows, rows)
+        delta = totals_ref[piece].astype(jnp.float32) / replicas
+        new_momentum = momentum_rate * momentum_ref[at, :] + delta
+        momentum_out[at, :] = new_momentum
+        params_out[at, :] = base_ref[0, at, :] - outer_rate * (
+            delta + momentum_rate * new_momentum
+        )
+
+
+def update(replicas, totals, outer_params, momentum, fragment):
     shape = momentum.shape
-    part = parts[0].shape
 
     def whole(block):
-        return pl.BlockSpec(block, lambda i, fragment_ref, place_ref: (0,) * len(block))
+        return pl.BlockSpec(block, lambda i, fragment_ref: (0,) * len(block))
 
     return pl.pallas_call(
         functools.partial(update_kernel, replicas),
         grid_spec=pltpu.PrefetchScalarGridSpec(
-            num_scalar_prefetch=2,
+            num_scalar_prefetch=1,
             grid=(1,),
-            in_specs=[whole(part)] * RADIX
-            + [
-                pl.BlockSpec(
-                    (1,) + shape, lambda i, fragment_ref, place_ref: (fragment_ref[0], 0, 0)
-                ),
+            in_specs=[
+                whole(totals.shape),
+                pl.BlockSpec((1,) + shape, lambda i, fragment_ref: (fragment_ref[0], 0, 0)),
                 whole(shape),
             ],
             out_specs=(whole(shape), whole(shape)),
@@ -263,7 +255,7 @@
         ),
         compiler_params=PARAMS,
         name="update",
-    )(fragment, place, *parts, outer_params, momentum)
+    )(fragment, totals, outer_params, momentum)
 
 
 def shift(part, axis, step):
@@ -273,10 +265,6 @@
 
 def scatter_stage(parts, axis):
     return [parts[0]] + [shift(parts[step], axis, step) for step in range(1, RADIX)]
-
-
-def gather_stage(part, axis):
-    return [part] + [shift(part, axis, step) for step in range(1, RADIX)]
 
 
 def place_on(axis):
@@ -317,12 +305,12 @@
     rows, apart = lax.optimization_barrier((rows, apart))
     part = add_parts([part, apart])
     returned = exchange(rows, experts)
-    sums = total(lax.all_gather(part, "z_far", axis=0))
-    parts = gather_stage(sums, "z_near")
+    spread = total_spread(lax.all_gather(part, "z_far", axis=0))
+    returned, spread = lax.optimization_barrier((returned, spread))
+    totals = lax.all_to_all(spread, "z_near", split_axis=0, concat_axis=0, tiled=True)
     moe_out = combine_rows(combine, returned)
-    parts[0], moe_out = lax.optimization_barrier((parts[0], moe_out))
     new_params, new_momentum = update(
-        lax.axis_size(("y_far", "z_far", "z_near")), near, parts, outer_params, momentum, fragment
+        lax.axis_size(("y_far", "z_far", "z_near")), totals, outer_params, momentum, fragment
     )
     return (moe_out, new_params, new_momentum)
 

time: 98.1 us -> 96.3 us (0.982)
  starting transfers between devices: 53.3 us -> 48.2 us
  waiting for transfers between devices: 5.45 us -> 8.14 us
    ppermute x10 -> x7, starting transfers between devices: 29.5 us -> 17.7 us  [shift(): lax.ppermute(part, axis, [(i, (i + step) % size) for i in range(size)])]
    all_to_all x0 -> x1, starting transfers between devices: none -> 6.64 us  [shards(): lax.all_to_all(spread, 'z_near', split_axis=0, concat_axis=0, tiled=True)]
    all_to_all x0 -> x1, waiting for transfers between devices: none -> 4.99 us  [shards(): lax.all_to_all(spread, 'z_near', split_axis=0, concat_axis=0, tiled=True)]
    ppermute x10 -> x7, waiting for transfers between devices: 5.44 us -> 3.02 us  [shift(): lax.ppermute(part, axis, [(i, (i + step) % size) for i in range(size)])]
  transfers between devices with their start and end apart: 12 -> 10, of which waited for: 3 -> 4; matrix products, arithmetic and copies ran while one was open for 0% -> 0% of each run, Pallas kernels for 9% -> 10%
where the time goes in v13:
time: 96.3 us; the launch traced here: 95.6 us
  starting transfers between devices  48.2 us (50%)
  blocking collectives  24.8 us (26%)
  Pallas kernels  12.9 us (13%)
  waiting for transfers between devices  8.14 us (8%)
  between operations  1.48 us (2%)
    all_gather x1, blocking collectives, shards(): spread = total_spread(lax.all_gather(part, 'z_far', axis=0))  24.8 us
    all_to_all x2, starting transfers between devices, exchange(): lax.all_to_all(rows.reshape(experts, CAP, width), 'chip', split_axis=0, c...  23.9 us
    ppermute x7, starting transfers between devices, shift(): lax.ppermute(part, axis, [(i, (i + step) % size) for i in range(size)])  17.7 us
    pallas_call x1, Pallas kernels, expert_rows(): pl.pallas_call(expert_kernel, in_specs=[HBM] * len(operands), out_shape=j...  6.72 us
    all_to_all x1, starting transfers between devices, shards(): lax.all_to_all(spread, 'z_near', split_axis=0, concat_axis=0, tiled=True)  6.64 us
    all_to_all x1, waiting for transfers between devices, shards(): lax.all_to_all(spread, 'z_near', split_axis=0, concat_axis=0, tiled=True)  4.99 us
    ppermute x7, waiting for transfers between devices, shift(): lax.ppermute(part, axis, [(i, (i + step) % size) for i in range(size)])  3.02 us
    pallas_call x1, Pallas kernels, route(): pl.pallas_call(functools.partial(route_kernel, experts), out_shape=(jax.S...  2.56 us
  transfers between devices with their start and end apart: 10, of which 4 were waited for; matrix products, arithmetic and copies ran while one was open for 0% of the time, Pallas kernels for 10%

profile of v13, /device:TPU:6, one launch (start us, length us, event | category | flops | bytes accessed | tf_op | source)
XLA Modules:
  0.0 95.6 jit_solution(18288377724842398472)
XLA Ops:
  0.7 2.6 %route.1 = (bf16[256,2048]{1,0:T(8,128)(2,1)}, bf16[256,128]{1,0:T(8,128)(2,1)}) custom-call(s32[8,128]{1,0:T(8,128)} %bitcast.16, f32[8,128]{1,0:T(8,128)} %bitcast.17, bf16[128,2048]{1,0:T(8,128)(2,1)} %refs_2_.2), custom_call_target="tpu_custom_call" | custom-call | tf_op jit(solution)/shard_map/route/pallas_call | solution.py:72
  3.2 17.3 %all-to-all-start = ((bf16[16,16,2048]{2,1,0:T(8,128)(2,1)}), bf16[16,16,2048]{2,1,0:T(8,128)(2,1)}, u32[]{:S(2)}, u32[]{:S(2)}) async-start(bf16[16,16,2048]{2,1,0:T(8,128)(2,1)} %bitcast.15), calls=%async_computation | async-start | bytes 2097152 | tf_op jit(solution)/shard_map/all_to_all | solution.py:276
  20.5 0.6 dequant.1
  21.1 1.9 %collective-permute-start = (bf16[16,2048]{1,0:T(8,128)(2,1)S(1)}, bf16[16,2048]{1,0:T(8,128)(2,1)S(1)}, u32[]{:S(2)}, u32[]{:S(2)}) collective-permute-start(bf16[16,2048]{1,0:T(8,128)(2,1)S(1)} %get-tuple-element.22), channel_id=1, source_target_pairs={{0,32},{32,64},{64,96},{96,0},{1,33},{33,65},{65,97},{97,1},{2,34}... | collective-permute-start | bytes 196616 | tf_op jit(solution)/shard_map/ppermute | solution.py:263
  23.0 1.9 %collective-permute-start.1 = (bf16[16,2048]{1,0:T(8,128)(2,1)S(1)}, bf16[16,2048]{1,0:T(8,128)(2,1)S(1)}, u32[]{:S(2)}, u32[]{:S(2)}) collective-permute-start(bf16[16,2048]{1,0:T(8,128)(2,1)S(1)} %get-tuple-element.23), channel_id=1, source_target_pairs={{0,64},{32,96},{64,0},{96,32},{1,65},{33,97},{65,1},{97,33},{2,66}... | collective-permute-start | bytes 196616 | tf_op jit(solution)/shard_map/ppermute | solution.py:263
  25.0 5.7 %collective-permute-start.2 = (bf16[16,2048]{1,0:T(8,128)(2,1)S(1)}, bf16[16,2048]{1,0:T(8,128)(2,1)S(1)}, u32[]{:S(2)}, u32[]{:S(2)}) collective-permute-start(bf16[16,2048]{1,0:T(8,128)(2,1)S(1)} %get-tuple-element.24), channel_id=1, source_target_pairs={{0,96},{32,0},{64,32},{96,64},{1,97},{33,1},{65,33},{97,65},{2,98}... | collective-permute-start | bytes 196616 | tf_op jit(solution)/shard_map/ppermute | solution.py:263
  30.7 1.9 %collective-permute-start.3 = (bf16[1,2048,384]{2,1,0:T(8,128)(2,1)}, bf16[1,2048,384]{2,1,0:T(8,128)(2,1)}, u32[]{:S(2)}, u32[]{:S(2)}) collective-permute-start(bf16[1,2048,384]{2,1,0:T(8,128)(2,1)} %refs_0_.1), channel_id=1, source_target_pairs={{0,1},{1,0},{2,3},{3,2},{4,5},{5,4},{6,7},{7,6},{8,9},{9,8},{10,11... | collective-permute-start | bytes 4718600 | tf_op jit(solution)/shard_map/ppermute | solution.py:263
  32.6 2.4 %collective-permute-start.4 = (bf16[1,2048,384]{2,1,0:T(8,128)(2,1)}, bf16[1,2048,384]{2,1,0:T(8,128)(2,1)}, u32[]{:S(2)}, u32[]{:S(2)}) collective-permute-start(bf16[1,2048,384]{2,1,0:T(8,128)(2,1)} %refs_1_.1), channel_id=1, source_target_pairs={{0,1},{1,0},{2,3},{3,2},{4,5},{5,4},{6,7},{7,6},{8,9},{9,8},{10,11... | collective-permute-start | bytes 4718600 | tf_op jit(solution)/shard_map/ppermute | solution.py:263
  35.0 0.0 collective-permute-done.refs_1_
  35.1 0.0 collective-permute-done.1.refs_2_
  35.1 1.9 %collective-permute-start.5 = (bf16[1,384,2048]{2,1,0:T(8,128)(2,1)}, bf16[1,384,2048]{2,1,0:T(8,128)(2,1)}, u32[]{:S(2)}, u32[]{:S(2)}) collective-permute-start(bf16[1,384,2048]{2,1,0:T(8,128)(2,1)} %refs_2_.3), channel_id=1, source_target_pairs={{0,1},{1,0},{2,3},{3,2},{4,5},{5,4},{6,7},{7,6},{8,9},{9,8},{10,11... | collective-permute-start | bytes 4718600 | tf_op jit(solution)/shard_map/ppermute | solution.py:263
  37.0 1.9 %collective-permute-start.6 = (bf16[16,2048]{1,0:T(8,128)(2,1)S(1)}, bf16[16,2048]{1,0:T(8,128)(2,1)S(1)}, u32[]{:S(2)}, u32[]{:S(2)}) collective-permute-start(bf16[16,2048]{1,0:T(8,128)(2,1)S(1)} %add_parts.2.refs_0_), channel_id=1, source_target_pairs={{0,512},{512,0},{1,513},{513,1},{2,514},{514,2},{3,515},{515,3},{4... | collective-permute-start | bytes 196616 | tf_op jit(solution)/shard_map/ppermute | solution.py:263
  39.0 1.8 %collective-permute-done.5.refs_5_ = bf16[1,384,2048]{2,1,0:T(8,128)(2,1)} collective-permute-done((bf16[1,384,2048]{2,1,0:T(8,128)(2,1)}, bf16[1,384,2048]{2,1,0:T(8,128)(2,1)}, u32[]{:S(2)}, u32[]{:S(2)}) %collective-permute-start.5) | collective-permute-done | bytes 1572896 | tf_op jit(solution)/shard_map/ppermute | solution.py:263
  40.8 6.7 %expert_rows.1 = bf16[256,2048]{1,0:T(8,128)(2,1)} custom-call(bf16[256,2048]{1,0:T(8,128)(2,1)} %bitcast.3.rows_hbm, bf16[1,2048,384]{2,1,0:T(8,128)(2,1)} %refs_0_.1, bf16[1,2048,384]{2,1,0:T(8,128)(2,1)} %refs_1_.1, bf16[1,384,2048]{2,1,0:T(8,128)(2,1)} %refs_2_.3, bf16[1,2048,384]{2,1,0:T(8,128)(2,1)} %collective-permute-done.3.refs_3_, ...), custom_call_target="tpu_custom_call" | custom-call | tf_op jit(solution)/shard_map/expert_rows/pallas_call | solution.py:123
  47.6 1.2 %collective-permute-done.6.refs_1_ = bf16[16,2048]{1,0:T(8,128)(2,1)S(1)} collective-permute-done((bf16[16,2048]{1,0:T(8,128)(2,1)S(1)}, bf16[16,2048]{1,0:T(8,128)(2,1)S(1)}, u32[]{:S(2)}, u32[]{:S(2)}) %collective-permute-start.6) | collective-permute-done | bytes 65568 | tf_op jit(solution)/shard_map/ppermute | solution.py:263
  48.8 6.6 %all-to-all-start.1 = ((bf16[16,16,2048]{2,1,0:T(8,128)(2,1)}), bf16[16,16,2048]{2,1,0:T(8,128)(2,1)S(1)}, u32[]{:S(2)}, u32[]{:S(2)}) async-start(bf16[16,16,2048]{2,1,0:T(8,128)(2,1)} %bitcast.14), calls=%async_computation.1 | async-start | bytes 2097152 | tf_op jit(solution)/shard_map/all_to_all | solution.py:276
  55.3 0.0 copy-start.1
  55.4 24.8 %all-gather = bf16[64,2048]{1,0:T(8,128)(2,1)S(1)} all-gather(bf16[16,2048]{1,0:T(8,128)(2,1)S(1)} %add_parts.3), channel_id=2, replica_groups=mesh['y_far'=2,'z_far'=4,'z_near'=4,'chip'=16,'core'=2] {'z_far'}, dimensions={0}, use_global_device_ids=true | all-gather | bytes 327680 | tf_op jit(solution)/shard_map/all_gather | solution.py:308
  80.2 0.7 total_spread.1
  81.0 0.1 all-to-all-done.1
  81.1 6.6 %all-to-all-start.2 = ((bf16[4,16,2048]{2,1,0:T(8,128)(2,1)}), bf16[4,16,2048]{2,1,0:T(8,128)(2,1)S(1)}, u32[]{:S(2)}, u32[]{:S(2)}) async-start(bf16[4,16,2048]{2,1,0:T(8,128)(2,1)} %total_spread.1), calls=%async_computation.2 | async-start | bytes 524288 | tf_op jit(solution)/shard_map/all_to_all | solution.py:310
  88.4 1.1 %combine_rows.1 = bf16[128,2048]{1,0:T(8,128)(2,1)} custom-call(bf16[256,128]{1,0:T(8,128)(2,1)S(1)} %copy-done.3, bf16[256,2048]{1,0:T(8,128)(2,1)S(1)} %bitcast.11), custom_call_target="tpu_custom_call" | custom-call | tf_op jit(solution)/shard_map/combine_rows/pallas_call | solution.py:149
  89.5 5.0 %all-to-all-done.2.totals_ref = bf16[4,16,2048]{2,1,0:T(8,128)(2,1)S(1)} async-done(((bf16[4,16,2048]{2,1,0:T(8,128)(2,1)}), bf16[4,16,2048]{2,1,0:T(8,128)(2,1)S(1)}, u32[]{:S(2)}, u32[]{:S(2)}) %all-to-all-start.2) | async-done | bytes 262176 | tf_op jit(solution)/shard_map/all_to_all | solution.py:310
  94.5 1.1 %update.1 = (f32[64,2048]{1,0:T(8,128)}, f32[64,2048]{1,0:T(8,128)}) custom-call(s32[1]{0:T(128)S(6)} %copy.14.fragment_ref, bf16[4,16,2048]{2,1,0:T(8,128)(2,1)S(1)} %all-to-all-done.2.totals_ref, f32[3,64,2048]{2,1,0:T(8,128)S(1)} %copy-done, f32[64,2048]{1,0:T(8,128)S(1)} %copy-done.1), custom_call_target="tpu_custom_call" | custom-call | tf_op jit(solution)/shard_map/update/pallas_call | solution.py:240
  (15 shorter events, 0.1 us)
Async XLA Ops:
  0.6 19.9 %copy-start.2 = (bf16[1,64,2048]{2,1,0:T(8,128)(2,1)S(1)}, bf16[1,64,2048]{2,1,0:T(8,128)(2,1)}, u32[]{:S(2)}) copy-start(bf16[1,64,2048]{2,1,0:T(8,128)(2,1)} %values_ref.1) | copy-start | bytes 786436
  0.6 19.9 %copy-start.4 = (f32[1,64,16]{1,2,0:T(8,128)S(1)}, f32[1,64,16]{1,2,0:T(8,128)}, u32[]{:S(2)}) copy-start(f32[1,64,16]{1,2,0:T(8,128)} %param.18) | copy-start | bytes 12292
  3.2 35.8 %all-to-all-start = ((bf16[16,16,2048]{2,1,0:T(8,128)(2,1)}), bf16[16,16,2048]{2,1,0:T(8,128)(2,1)}, u32[]{:S(2)}, u32[]{:S(2)}) async-start(bf16[16,16,2048]{2,1,0:T(8,128)(2,1)} %bitcast.15), calls=%async_computation | async-start | bytes 2097152 | tf_op jit(solution)/shard_map/all_to_all | solution.py:276
  21.1 13.9 %collective-permute-start = (bf16[16,2048]{1,0:T(8,128)(2,1)S(1)}, bf16[16,2048]{1,0:T(8,128)(2,1)S(1)}, u32[]{:S(2)}, u32[]{:S(2)}) collective-permute-start(bf16[16,2048]{1,0:T(8,128)(2,1)S(1)} %get-tuple-element.22), channel_id=1, source_target_pairs={{0,32},{32,64},{64,96},{96,0},{1,33},{33,65},{65,97},{97,1},{2,34}... | collective-permute-start | bytes 196616 | tf_op jit(solution)/shard_map/ppermute | solution.py:263
  23.0 12.0 %collective-permute-start.1 = (bf16[16,2048]{1,0:T(8,128)(2,1)S(1)}, bf16[16,2048]{1,0:T(8,128)(2,1)S(1)}, u32[]{:S(2)}, u32[]{:S(2)}) collective-permute-start(bf16[16,2048]{1,0:T(8,128)(2,1)S(1)} %get-tuple-element.23), channel_id=1, source_target_pairs={{0,64},{32,96},{64,0},{96,32},{1,65},{33,97},{65,1},{97,33},{2,66}... | collective-permute-start | bytes 196616 | tf_op jit(solution)/shard_map/ppermute | solution.py:263
  25.0 10.1 %collective-permute-start.2 = (bf16[16,2048]{1,0:T(8,128)(2,1)S(1)}, bf16[16,2048]{1,0:T(8,128)(2,1)S(1)}, u32[]{:S(2)}, u32[]{:S(2)}) collective-permute-start(bf16[16,2048]{1,0:T(8,128)(2,1)S(1)} %get-tuple-element.24), channel_id=1, source_target_pairs={{0,96},{32,0},{64,32},{96,64},{1,97},{33,1},{65,33},{97,65},{2,98}... | collective-permute-start | bytes 196616 | tf_op jit(solution)/shard_map/ppermute | solution.py:263
  30.7 8.3 %collective-permute-start.3 = (bf16[1,2048,384]{2,1,0:T(8,128)(2,1)}, bf16[1,2048,384]{2,1,0:T(8,128)(2,1)}, u32[]{:S(2)}, u32[]{:S(2)}) collective-permute-start(bf16[1,2048,384]{2,1,0:T(8,128)(2,1)} %refs_0_.1), channel_id=1, source_target_pairs={{0,1},{1,0},{2,3},{3,2},{4,5},{5,4},{6,7},{7,6},{8,9},{9,8},{10,11... | collective-permute-start | bytes 4718600 | tf_op jit(solution)/shard_map/ppermute | solution.py:263
  32.6 6.4 %collective-permute-start.4 = (bf16[1,2048,384]{2,1,0:T(8,128)(2,1)}, bf16[1,2048,384]{2,1,0:T(8,128)(2,1)}, u32[]{:S(2)}, u32[]{:S(2)}) collective-permute-start(bf16[1,2048,384]{2,1,0:T(8,128)(2,1)} %refs_1_.1), channel_id=1, source_target_pairs={{0,1},{1,0},{2,3},{3,2},{4,5},{5,4},{6,7},{7,6},{8,9},{9,8},{10,11... | collective-permute-start | bytes 4718600 | tf_op jit(solution)/shard_map/ppermute | solution.py:263
  35.1 5.7 %collective-permute-start.5 = (bf16[1,384,2048]{2,1,0:T(8,128)(2,1)}, bf16[1,384,2048]{2,1,0:T(8,128)(2,1)}, u32[]{:S(2)}, u32[]{:S(2)}) collective-permute-start(bf16[1,384,2048]{2,1,0:T(8,128)(2,1)} %refs_2_.3), channel_id=1, source_target_pairs={{0,1},{1,0},{2,3},{3,2},{4,5},{5,4},{6,7},{7,6},{8,9},{9,8},{10,11... | collective-permute-start | bytes 4718600 | tf_op jit(solution)/shard_map/ppermute | solution.py:263
  37.0 11.7 %collective-permute-start.6 = (bf16[16,2048]{1,0:T(8,128)(2,1)S(1)}, bf16[16,2048]{1,0:T(8,128)(2,1)S(1)}, u32[]{:S(2)}, u32[]{:S(2)}) collective-permute-start(bf16[16,2048]{1,0:T(8,128)(2,1)S(1)} %add_parts.2.refs_0_), channel_id=1, source_target_pairs={{0,512},{512,0},{1,513},{513,1},{2,514},{514,2},{3,515},{515,3},{4... | collective-permute-start | bytes 196616 | tf_op jit(solution)/shard_map/ppermute | solution.py:263
  48.8 39.6 %copy-start.3 = (bf16[256,128]{1,0:T(8,128)(2,1)S(1)}, bf16[256,128]{1,0:T(8,128)(2,1)}, u32[]{:S(2)}) copy-start(bf16[256,128]{1,0:T(8,128)(2,1)} %get-tuple-element.19.combine_ref) | copy-start | bytes 196612
  48.8 32.3 %all-to-all-start.1 = ((bf16[16,16,2048]{2,1,0:T(8,128)(2,1)}), bf16[16,16,2048]{2,1,0:T(8,128)(2,1)S(1)}, u32[]{:S(2)}, u32[]{:S(2)}) async-start(bf16[16,16,2048]{2,1,0:T(8,128)(2,1)} %bitcast.14), calls=%async_computation.1 | async-start | bytes 2097152 | tf_op jit(solution)/shard_map/all_to_all | solution.py:276
  55.3 39.2 %copy-start = (f32[3,64,2048]{2,1,0:T(8,128)S(1)}, f32[3,64,2048]{2,1,0:T(8,128)}, u32[]{:S(2)}) copy-start(f32[3,64,2048]{2,1,0:T(8,128)} %base_ref.1) | copy-start | bytes 4718596
  55.3 39.2 %copy-start.1 = (f32[64,2048]{1,0:T(8,128)S(1)}, f32[64,2048]{1,0:T(8,128)}, u32[]{:S(2)}) copy-start(f32[64,2048]{1,0:T(8,128)} %momentum_ref.1) | copy-start | bytes 1572868
  81.1 13.4 %all-to-all-start.2 = ((bf16[4,16,2048]{2,1,0:T(8,128)(2,1)}), bf16[4,16,2048]{2,1,0:T(8,128)(2,1)S(1)}, u32[]{:S(2)}, u32[]{:S(2)}) async-start(bf16[4,16,2048]{2,1,0:T(8,128)(2,1)} %total_spread.1), calls=%async_computation.2 | async-start | bytes 524288 | tf_op jit(solution)/shard_map/all_to_all | solution.py:310
